TPU v7x, 32 devices: a whole 2x2x4 slice. The times are simulated.
32 devices in a mesh: ctx: 16 (over z, y, x), wa: 2 (over core).
Axes of the slice: x: 2, y: 2, z: 4, core: 2. Of those that a mesh axis runs over, the one named last changes fastest.
Arguments:
- hidden_in: bfloat16 [256, 16, 1024], P(None, 'ctx'), may hold values from -6 to 6
- attn_gain: float32 [1024], replicated, may hold values from 0.25 to 1.75
- query_weight: bfloat16 [1024, 1024], P(None, 'wa'), may hold values from -0.1875 to 0.1875
- key_weight: bfloat16 [1024, 512], P(None, 'wa'), may hold values from -0.1875 to 0.1875
- value_weight: bfloat16 [1024, 512], P(None, 'wa'), may hold values from -0.1875 to 0.1875
- query_gain: float32 [64], replicated, may hold values from 0.6 to 1.8
- key_gain: float32 [64], replicated, may hold values from 0.6 to 1.8
- out_weight: bfloat16 [1024, 1024], P('wa'), may hold values from -1.5 to 1.5
- ffn_gain: float32 [1024], replicated, may hold values from 0.25 to 1.75
- gate_weight: bfloat16 [1024, 4608], P(None, 'wa'), may hold values from -0.1875 to 0.1875
- up_weight: bfloat16 [1024, 4608], P(None, 'wa'), may hold values from -0.1875 to 0.1875
- down_weight: bfloat16 [4608, 1024], P('wa'), may hold values from -0.09375 to 0.09375
- query_adapt_in: bfloat16 [1024, 128], replicated, may hold values from -0.1875 to 0.1875
- query_adapt_out: bfloat16 [128, 1024], P(None, 'wa'), may hold values from -0.75 to 0.75
- key_adapt_in: bfloat16 [1024, 128], replicated, may hold values from -0.1875 to 0.1875
- key_adapt_out: bfloat16 [128, 512], P(None, 'wa'), may hold values from -0.75 to 0.75
- value_adapt_in: bfloat16 [1024, 128], replicated, may hold values from -0.1875 to 0.1875
- value_adapt_out: bfloat16 [128, 512], P(None, 'wa'), may hold values from -0.75 to 0.75
- out_adapt_in: bfloat16 [1024, 128], P('wa'), may hold values from -1.5 to 1.5
- out_adapt_out: bfloat16 [128, 1024], replicated, may hold values from -0.75 to 0.75
- gate_adapt_in: bfloat16 [1024, 128], replicated, may hold values from -0.1875 to 0.1875
- gate_adapt_out: bfloat16 [128, 4608], P(None, 'wa'), may hold values from -0.75 to 0.75
- up_adapt_in: bfloat16 [1024, 128], replicated, may hold values from -0.1875 to 0.1875
- up_adapt_out: bfloat16 [128, 4608], P(None, 'wa'), may hold values from -0.75 to 0.75
- down_adapt_in: bfloat16 [4608, 128], P('wa'), may hold values from -0.09375 to 0.09375
- down_adapt_out: bfloat16 [128, 1024], replicated, may hold values from -0.75 to 0.75
- document_extra: int32 [4], replicated, may hold values from 1 to 1801, 3300 in all
- document_adapter: int32 [4], replicated, may hold values from 0 to 7
- cotangent: bfloat16 [256, 16, 1024], P(None, 'ctx'), may hold values from -6 to 6
Outputs:
- output: bfloat16 [256, 16, 1024], P(None, 'ctx')
- input_grad: bfloat16 [256, 16, 1024], P(None, 'ctx')
- query_in_grad: float32 [1024, 128], replicated
- query_out_grad: float32 [128, 1024], P(None, 'wa')
- key_in_grad: float32 [1024, 128], replicated
- key_out_grad: float32 [128, 512], P(None, 'wa')
- value_in_grad: float32 [1024, 128], replicated
- value_out_grad: float32 [128, 512], P(None, 'wa')
- out_in_grad: float32 [1024, 128], P('wa')
- out_out_grad: float32 [128, 1024], replicated
- gate_in_grad: float32 [1024, 128], replicated
- gate_out_grad: float32 [128, 4608], P(None, 'wa')
- up_in_grad: float32 [1024, 128], replicated
- up_out_grad: float32 [128, 4608], P(None, 'wa')
- down_in_grad: float32 [4608, 128], P('wa')
- down_out_grad: float32 [128, 1024], replicated
Inputs may be any that keep to these rules, and one draw needn't show every extreme that they name: Document j has document_extra[j] + 199 tokens; the documents fill the 4096 tokens in order, and one has exactly 2000 tokens.
All inputs are finite; a program needn't handle non-finite values.
Results may differ from a plain program's by a relative error of at most 0.02.
Values may be sent and summed in bfloat16 or wider, within the bound.
No kernel may reach another device: no remote copies, remote signals or barrier semaphores. Data moves between devices by JAX's collectives and lax.ppermute only.
A program may use at most 256 MiB of HBM per device.

v0:
```python
import math

import jax
import jax.numpy as jnp
from jax import lax
from jax.sharding import PartitionSpec as P

RANK = 16
DOC_MIN = 200


norm_eps = 1e-05
masked_score = -1e30
theta_base = 1000000.0


def rms_gain(values, gain):
    return values * lax.rsqrt(jnp.mean(values * values, axis=-1, keepdims=True) + norm_eps) * gain


def rotate(values, cosine, sine):
    half_width = values.shape[-1] // 2
    first_half = values[..., :half_width]
    second = values[..., half_width:]
    return jnp.concatenate(
        [first_half * cosine - second * sine, second * cosine + first_half * sine], axis=-1
    )


def head_prep(raw, gain, cosine, sine):
    heads = raw.reshape(raw.shape[0], -1, gain.shape[0])
    return rotate(rms_gain(heads, gain), cosine[:, None, :], sine[:, None, :])


def swiglu(gate, upper):
    return jax.nn.silu(gate) * upper


def segment_of(token_index, doc_ends):
    return jnp.sum((doc_ends[None, :] <= token_index[:, None]).astype(jnp.int32), axis=1)


def column(inputs, weight, adapt_in, adapt_out, adapt_mask):
    side = (adapt_mask * jnp.dot(inputs, adapt_in, preferred_element_type=jnp.float32)).astype(
        jnp.bfloat16
    )
    return (
        jnp.dot(inputs, weight, preferred_element_type=jnp.float32)
        + jnp.dot(side, adapt_out, preferred_element_type=jnp.float32),
        side,
    )


def column_back(inputs, weight, adapt_in, adapt_out, side, grad_result, adapt_mask):
    grad_side = (
        adapt_mask
        * jnp.einsum("to,ro->tr", grad_result, adapt_out, preferred_element_type=jnp.float32)
    ).astype(jnp.bfloat16)
    grad_factor_out = jnp.einsum("tr,to->ro", side, grad_result, preferred_element_type=jnp.float32)
    grad_factor_in = jnp.einsum("td,tr->dr", inputs, grad_side, preferred_element_type=jnp.float32)
    grad_inputs = jnp.einsum(
        "to,do->td", grad_result, weight, preferred_element_type=jnp.float32
    ) + jnp.einsum("tr,dr->td", grad_side, adapt_in, preferred_element_type=jnp.float32)
    return (grad_inputs, grad_factor_in, grad_factor_out)


def grouped(step_fn, carry_in, pieces, block_limit):
    shard_total = pieces[0].shape[0]
    group_size = block_limit
    while shard_total % group_size:
        group_size = group_size // 2
    stacked = tuple(
        (
            piece_arr.reshape((shard_total // group_size, group_size) + piece_arr.shape[1:])
            for piece_arr in pieces
        )
    )
    offsets = jnp.arange(shard_total // group_size, dtype=jnp.int32) * group_size

    def advance(carry_now, item):
        return (step_fn(carry_now, item[0], item[1]), None)

    result, unused = lax.scan(advance, carry_in, (stacked, offsets))
    return result


def per_device(
    hidden_in,
    attn_gain,
    query_weight,
    key_weight,
    value_weight,
    query_gain,
    key_gain,
    out_weight,
    ffn_gain,
    gate_weight,
    up_weight,
    down_weight,
    query_adapt_in,
    query_adapt_out,
    key_adapt_in,
    key_adapt_out,
    value_adapt_in,
    value_adapt_out,
    out_adapt_in,
    out_adapt_out,
    gate_adapt_in,
    gate_adapt_out,
    up_adapt_in,
    up_adapt_out,
    down_adapt_in,
    down_adapt_out,
    document_extra,
    document_adapter,
    cotangent,
):
    ctx_count = lax.axis_size("ctx")
    ctx_index = lax.axis_index("ctx")
    tok_rows = hidden_in.shape[0]
    head_dim = query_gain.shape[0]
    score_scale = head_dim ** (-0.5)
    kv_width = key_weight.shape[1]
    kv_heads = kv_width // head_dim
    groups = query_weight.shape[1] // kv_width
    block_limit = max(1, 2048 // tok_rows)
    local_rows = jnp.arange(tok_rows, dtype=jnp.int32)
    x_rows = hidden_in[:, 0, :].astype(jnp.float32)
    grad_branch = cotangent[:, 0, :]
    global_index = local_rows * ctx_count + ctx_index
    lengths = document_extra + (DOC_MIN - 1)
    doc_ends = jnp.cumsum(lengths)
    doc_starts = doc_ends - lengths
    doc_of = segment_of(global_index, doc_ends)
    doc_onehot = (
        doc_of[:, None] == jnp.arange(doc_ends.shape[0], dtype=jnp.int32)[None, :]
    ).astype(jnp.int32)
    position = global_index - jnp.sum(doc_onehot * doc_starts[None, :], axis=1)
    adapter = jnp.sum(doc_onehot * document_adapter[None, :], axis=1)
    adapt_cols = jnp.arange(query_adapt_in.shape[1], dtype=jnp.int32) // RANK
    adapt_mask = (adapter[:, None] == adapt_cols[None, :]).astype(jnp.float32)
    inverse = jnp.exp(
        jnp.arange(head_dim // 2, dtype=jnp.float32) * (-2.0 * math.log(theta_base) / head_dim)
    )
    angle = position.astype(jnp.float32)[:, None] * inverse[None, :]
    cosine = jnp.cos(angle)
    sine = jnp.sin(angle)
    query_index = jnp.concatenate([global_index] * groups)
    query_doc = jnp.concatenate([doc_of] * groups)

    def visible(key_index):
        key_doc = segment_of(key_index, doc_ends)
        return (
            (query_doc[:, None] == key_doc[None, :])
            & (key_index[None, :] <= query_index[:, None])
            & (key_index[None, :] >= 0)
        )

    def piece_index(first_row, shard_count):
        grid = (
            jnp.arange(tok_rows, dtype=jnp.int32)[None, :] * ctx_count
            + first_row
            + jnp.arange(shard_count, dtype=jnp.int32)[:, None]
        )
        return grid.reshape(-1)

    normed, norm_back = jax.vjp(lambda values: rms_gain(values, attn_gain), x_rows)
    normed_b = normed.astype(jnp.bfloat16)
    query_raw, query_side = column(
        normed_b, query_weight, query_adapt_in, query_adapt_out, adapt_mask
    )
    key_raw, key_side = column(normed_b, key_weight, key_adapt_in, key_adapt_out, adapt_mask)
    value_raw, value_side = column(
        normed_b, value_weight, value_adapt_in, value_adapt_out, adapt_mask
    )
    query_heads, query_back = jax.vjp(
        lambda values: head_prep(values, query_gain, cosine, sine), query_raw
    )
    key_heads, key_back = jax.vjp(lambda values: head_prep(values, key_gain, cosine, sine), key_raw)
    query_block = (
        query_heads.astype(jnp.bfloat16)
        .reshape(tok_rows, kv_heads, groups, head_dim)
        .transpose(1, 2, 0, 3)
        .reshape(kv_heads, groups * tok_rows, head_dim)
    )
    key_flat = key_heads.astype(jnp.bfloat16).reshape(tok_rows, kv_width)
    value_flat = value_raw.astype(jnp.bfloat16)

    def scores_for(key_rows):
        return (
            jnp.einsum(
                "hqd,khd->hqk",
                query_block,
                key_rows.reshape(-1, kv_heads, head_dim),
                preferred_element_type=jnp.float32,
            )
            * score_scale
        )

    def total_update(carry_now, key_rows, seen):
        run_max, run_total = carry_now
        scores = scores_for(key_rows)
        new_max = jnp.maximum(run_max, jnp.max(jnp.where(seen, scores, masked_score), axis=-1))
        run_total = run_total * jnp.exp(run_max - new_max) + jnp.sum(
            jnp.where(seen, jnp.exp(scores - new_max[..., None]), 0.0), axis=-1
        )
        return (new_max, run_total)

    def value_update(acc_now, key_rows, value_rows, seen, log_totals):
        scores = scores_for(key_rows)
        weights = jnp.where(seen, jnp.exp(scores - log_totals[..., None]), 0.0).astype(jnp.bfloat16)
        return acc_now + jnp.einsum(
            "hqk,khd->hqd",
            weights,
            value_rows.reshape(-1, kv_heads, head_dim),
            preferred_element_type=jnp.float32,
        )

    start_max = jnp.full((kv_heads, groups * tok_rows), masked_score, jnp.float32)
    start_total = jnp.zeros((kv_heads, groups * tok_rows), jnp.float32)
    start_acc = jnp.zeros((kv_heads, groups * tok_rows, head_dim), jnp.float32)
    keys_all, values_all = (
        lax.all_gather(key_flat.reshape(1, tok_rows, kv_width), "ctx", axis=0, tiled=True),
        lax.all_gather(value_flat.reshape(1, tok_rows, kv_width), "ctx", axis=0, tiled=True),
    )

    def total_step(carry_now, blocks, first_row):
        return total_update(
            carry_now, blocks[0], visible(piece_index(first_row, blocks[0].shape[0]))
        )

    run_max, run_total = grouped(total_step, (start_max, start_total), (keys_all,), block_limit)
    log_totals = run_max + jnp.log(run_total)

    def value_step(acc_now, blocks, first_row):
        return value_update(
            acc_now,
            blocks[0],
            blocks[1],
            visible(piece_index(first_row, blocks[0].shape[0])),
            log_totals,
        )

    attended = grouped(value_step, start_acc, (keys_all, values_all), block_limit)
    attn_rows = (
        attended.reshape(kv_heads, groups, tok_rows, head_dim)
        .transpose(2, 0, 1, 3)
        .reshape(tok_rows, kv_heads * groups * head_dim)
    )
    attn_b = attn_rows.astype(jnp.bfloat16)
    head_part, out_side_sum = (
        lax.psum(
            jnp.dot(attn_b, out_weight, preferred_element_type=jnp.float32).astype(jnp.bfloat16),
            "wa",
        ).astype(jnp.float32),
        lax.psum(
            jnp.dot(attn_b, out_adapt_in, preferred_element_type=jnp.float32).astype(jnp.bfloat16),
            "wa",
        ).astype(jnp.float32),
    )
    out_side = (adapt_mask * out_side_sum).astype(jnp.bfloat16)
    mixed = (
        x_rows + head_part + jnp.dot(out_side, out_adapt_out, preferred_element_type=jnp.float32)
    )
    ffn_normed, ffn_norm_back = jax.vjp(lambda values: rms_gain(values, ffn_gain), mixed)
    ffn_normed_b = ffn_normed.astype(jnp.bfloat16)
    gate_raw, gate_side = column(
        ffn_normed_b, gate_weight, gate_adapt_in, gate_adapt_out, adapt_mask
    )
    upper_raw, upper_side = column(ffn_normed_b, up_weight, up_adapt_in, up_adapt_out, adapt_mask)
    hidden_act, swiglu_back = jax.vjp(swiglu, gate_raw, upper_raw)
    hidden_b = hidden_act.astype(jnp.bfloat16)
    down_part, down_side_sum = (
        lax.psum(
            jnp.dot(hidden_b, down_weight, preferred_element_type=jnp.float32).astype(jnp.bfloat16),
            "wa",
        ).astype(jnp.float32),
        lax.psum(
            jnp.dot(hidden_b, down_adapt_in, preferred_element_type=jnp.float32).astype(
                jnp.bfloat16
            ),
            "wa",
        ).astype(jnp.float32),
    )
    down_side = (adapt_mask * down_side_sum).astype(jnp.bfloat16)
    block_out = (
        mixed + down_part + jnp.dot(down_side, down_adapt_out, preferred_element_type=jnp.float32)
    ).astype(jnp.bfloat16)
    grad_rows = grad_branch.astype(jnp.float32)
    grad_hidden, down_in_grad, down_out_grad = column_back(
        hidden_b, down_weight, down_adapt_in, down_adapt_out, down_side, grad_branch, adapt_mask
    )
    grad_gate, grad_upper = swiglu_back(grad_hidden)
    gate_part, gate_in_grad, gate_out_grad = column_back(
        ffn_normed_b,
        gate_weight,
        gate_adapt_in,
        gate_adapt_out,
        gate_side,
        grad_gate.astype(jnp.bfloat16),
        adapt_mask,
    )
    upper_part, up_in_grad, up_out_grad = column_back(
        ffn_normed_b,
        up_weight,
        up_adapt_in,
        up_adapt_out,
        upper_side,
        grad_upper.astype(jnp.bfloat16),
        adapt_mask,
    )
    ffn_input_grad = lax.psum((gate_part + upper_part).astype(jnp.bfloat16), "wa").astype(
        jnp.float32
    )
    grad_mixed = grad_rows + ffn_norm_back(ffn_input_grad)[0]
    grad_mixed_b = grad_mixed.astype(jnp.bfloat16)
    grad_attn, out_in_grad, out_out_grad = column_back(
        attn_b, out_weight, out_adapt_in, out_adapt_out, out_side, grad_mixed_b, adapt_mask
    )
    grad_block = (
        grad_attn.astype(jnp.bfloat16)
        .reshape(tok_rows, kv_heads, groups, head_dim)
        .transpose(1, 2, 0, 3)
        .reshape(kv_heads, groups * tok_rows, head_dim)
    )
    row_delta = jnp.sum(grad_block.astype(jnp.float32) * attended, axis=-1)

    def score_grads(key_rows, value_rows, seen):
        key_heads_blk = key_rows.reshape(-1, kv_heads, head_dim)
        value_heads_blk = value_rows.reshape(-1, kv_heads, head_dim)
        scores = (
            jnp.einsum(
                "hqd,khd->hqk", query_block, key_heads_blk, preferred_element_type=jnp.float32
            )
            * score_scale
        )
        weights = jnp.where(seen, jnp.exp(scores - log_totals[..., None]), 0.0)
        grad_weights = jnp.einsum(
            "hqd,khd->hqk", grad_block, value_heads_blk, preferred_element_type=jnp.float32
        )
        grad_scores = (weights * (grad_weights - row_delta[..., None])).astype(jnp.bfloat16)
        return (weights, grad_scores, key_heads_blk)

    def kv_grad_of(weights, grad_scores, row_count):
        value_grad = jnp.einsum(
            "hqk,hqd->khd",
            weights.astype(jnp.bfloat16),
            grad_block,
            preferred_element_type=jnp.float32,
        )
        key_grad = (
            jnp.einsum("hqk,hqd->khd", grad_scores, query_block, preferred_element_type=jnp.float32)
            * score_scale
        )
        return jnp.concatenate(
            [key_grad.reshape(row_count, kv_width), value_grad.reshape(row_count, kv_width)], axis=1
        )

    def query_step(acc_now, blocks, first_row):
        weights, grad_scores, key_heads_blk = score_grads(
            blocks[0].reshape(-1, kv_width),
            blocks[1].reshape(-1, kv_width),
            visible(piece_index(first_row, blocks[0].shape[0])),
        )
        return (
            acc_now
            + jnp.einsum(
                "hqk,khd->hqd", grad_scores, key_heads_blk, preferred_element_type=jnp.float32
            )
            * score_scale
        )

    grad_queries = grouped(query_step, start_acc, (keys_all, values_all), block_limit)
    flat_keys = keys_all.reshape(-1, kv_width)
    flat_values = values_all.reshape(-1, kv_width)
    shard_span = tok_rows * lax.axis_size("ctx") // tok_rows
    group_size = block_limit
    while shard_span % group_size:
        group_size = group_size // 2
    block_rows = group_size * tok_rows

    def one_block(offset):
        key_rows = lax.dynamic_slice_in_dim(flat_keys, offset, block_rows, 0)
        value_rows = lax.dynamic_slice_in_dim(flat_values, offset, block_rows, 0)
        flat_index = offset + jnp.arange(block_rows, dtype=jnp.int32)
        key_index = flat_index % tok_rows * ctx_count + flat_index // tok_rows
        weights, grad_scores, key_heads_blk = score_grads(key_rows, value_rows, visible(key_index))
        return kv_grad_of(weights, grad_scores, block_rows)

    offsets = (
        jnp.arange(tok_rows * lax.axis_size("ctx") // block_rows, dtype=jnp.int32) * block_rows
    )
    key_value_grads = lax.psum_scatter(
        lax.map(one_block, offsets).reshape(tok_rows * lax.axis_size("ctx"), 2 * kv_width),
        "ctx",
        scatter_dimension=0,
        tiled=True,
    )
    grad_query_heads = (
        grad_queries.reshape(kv_heads, groups, tok_rows, head_dim)
        .transpose(2, 0, 1, 3)
        .reshape(tok_rows, kv_heads * groups, head_dim)
    )
    grad_query_raw = query_back(grad_query_heads)[0].astype(jnp.bfloat16)
    grad_key_raw = key_back(key_value_grads[:, :kv_width].reshape(tok_rows, kv_heads, head_dim))[
        0
    ].astype(jnp.bfloat16)
    grad_value_raw = key_value_grads[:, kv_width:].astype(jnp.bfloat16)
    query_part, query_in_grad, query_out_grad = column_back(
        normed_b,
        query_weight,
        query_adapt_in,
        query_adapt_out,
        query_side,
        grad_query_raw,
        adapt_mask,
    )
    key_part, key_in_grad, key_out_grad = column_back(
        normed_b, key_weight, key_adapt_in, key_adapt_out, key_side, grad_key_raw, adapt_mask
    )
    value_part, value_in_grad, value_out_grad = column_back(
        normed_b,
        value_weight,
        value_adapt_in,
        value_adapt_out,
        value_side,
        grad_value_raw,
        adapt_mask,
    )
    attn_input_grad = lax.psum(
        (query_part + key_part + value_part).astype(jnp.bfloat16), "wa"
    ).astype(jnp.float32)
    input_rows = (grad_mixed + norm_back(attn_input_grad)[0]).astype(jnp.bfloat16)
    output = block_out.reshape(tok_rows, 1, -1)
    input_grad = input_rows.reshape(tok_rows, 1, -1)
    summed_shared = lax.psum(
        (query_in_grad, key_in_grad, value_in_grad, gate_in_grad, up_in_grad), ("ctx", "wa")
    )
    summed_rest = lax.psum(
        (
            query_out_grad,
            key_out_grad,
            value_out_grad,
            out_in_grad,
            out_out_grad,
            gate_out_grad,
            up_out_grad,
            down_in_grad,
            down_out_grad,
        ),
        "ctx",
    )
    return (
        output,
        input_grad,
        summed_shared[0],
        summed_rest[0],
        summed_shared[1],
        summed_rest[1],
        summed_shared[2],
        summed_rest[2],
        summed_rest[3],
        summed_rest[4],
        summed_shared[3],
        summed_rest[5],
        summed_shared[4],
        summed_rest[6],
        summed_rest[7],
        summed_rest[8],
    )


def solution(mesh):
    return jax.shard_map(
        per_device,
        mesh=mesh,
        in_specs=(
            P(None, "ctx", None),
            P(),
            P(None, "wa"),
            P(None, "wa"),
            P(None, "wa"),
            P(),
            P(),
            P("wa", None),
            P(),
            P(None, "wa"),
            P(None, "wa"),
            P("wa", None),
            P(),
            P(None, "wa"),
            P(),
            P(None, "wa"),
            P(),
            P(None, "wa"),
            P("wa", None),
            P(),
            P(),
            P(None, "wa"),
            P(),
            P(None, "wa"),
            P("wa", None),
            P(),
            P(),
            P(),
            P(None, "ctx", None),
        ),
        out_specs=(
            P(None, "ctx", None),
            P(None, "ctx", None),
            P(),
            P(None, "wa"),
            P(),
            P(None, "wa"),
            P(),
            P(None, "wa"),
            P("wa", None),
            P(),
            P(),
            P(None, "wa"),
            P(),
            P(None, "wa"),
            P("wa", None),
            P(),
        ),
        check_vma=False,
    )
```

profile of v0, /device:TPU:0, one launch (start us, length us, event | category | flops | bytes accessed | tf_op | source)
XLA Modules:
  0.0 962.6 jit_solution(16096527078301761847)
XLA Ops:
  26.5 55.5 %all-gather.4.cloned.1.call-done = bf16[16,256,256]{2,1,0:T(8,128)(2,1)} async-done(((bf16[1,256,256]{2,1,0:T(8,128)(2,1)}), bf16[16,256,256]{2,1,0:T(8,128)(2,1)}) %all-gather.4.cloned.1.call-update) | async-done | bytes 2097168 | tf_op jit(solution)/shard_map/all_gather | solution.py:223
  85.9 31.6 %while.48 = (s32[]{:T(128)}, f32[4,512]{1,0:T(4,128)S(1)}, f32[4,512]{1,0:T(4,128)S(1)}, s32[512]{0:T(512)S(1)}, s32[4]{0:T(128)S(1)}, /*index=5*/s32[2]{0:T(128...) while((s32[]{:T(128)}, f32[4,512]{1,0:T(4,128)S(1)}, ...), condition=%wide.region_11.12_spmd.clone, body=%wide.region_7.11_spmd.clone.sunk | while | flops 570462720 | bytes 46581948 | solution.py:83
  93.4 4.5 fusion.296
  109.2 4.5 fusion.296
  117.5 27.3 %all-gather.6.cloned.1.call-done = bf16[4096,256]{1,0:T(8,128)(2,1)} async-done(((bf16[256,256]{1,0:T(8,128)(2,1)}), bf16[4096,256]{1,0:T(8,128)(2,1)}) %all-gather.6.cloned.1.call-update) | async-done | bytes 2097168 | tf_op jit(solution)/shard_map/all_gather | solution.py:224
  149.9 40.4 %while.49 = (s32[]{:T(128)}, f32[4,512,64]{1,2,0:T(8,128)}, s32[512]{0:T(512)S(1)}, s32[4]{0:T(128)}, s32[2]{0:T(128)}, /*index=5*/s32[512]{0:T(512)S(1)}, bf16[...) while((s32[]{:T(128)}, f32[4,512,64]{1,2,0:T(8,128)}, ...), condition=%wide.region_14.15_spmd.clone, body=%wide.region_12.14_spmd.clone.sunk | while | flops 1095002624 | bytes 14010567 | solution.py:83
  162.6 7.4 fusion.303
  182.7 7.6 fusion.303
  199.6 5.3 fusion.91
  205.0 10.1 %all-reduce.22.cloned.1.call-done = (bf16[256,1024]{1,0:T(8,128)(2,1)}, bf16[256,128]{1,0:T(8,128)(2,1)}) async-done(((bf16[256,1024]{1,0:T(8,128)(2,1)}, bf16[256,128]{1,0:T(8,128)(2,1)}), (bf16[256,1024]{1,0:T(8,128)(2,1)}, bf16[256,128]{1,0:T(8,128)(2,1)})) %all-reduce.22.cloned.1.call-update) | async-done | bytes 589840 | tf_op jit(solution)/shard_map/psum | solution.py:252
  235.9 19.4 %all-reduce.14.cloned.1.call-done = bf16[256,1024]{1,0:T(8,128)(2,1)} async-done(((bf16[256,1024]{1,0:T(8,128)(2,1)}), bf16[256,1024]{1,0:T(8,128)(2,1)}) %all-reduce.14.cloned.1.call-update) | async-done | bytes 524304 | tf_op jit(solution)/shard_map/psum | solution.py:312
  263.6 112.1 %while.47 = (s32[]{:T(128)}, f32[2,2048,512]{2,1,0:T(8,128)}, s32[512]{0:T(512)S(1)}, s32[4]{0:T(128)}, s32[2]{0:T(128)S(1)}, /*index=5*/s32[512]{0:T(512)S(1)},...) while((s32[]{:T(128)}, f32[2,2048,512]{2,1,0:T(8,128)}, ...), condition=%wide.region_29.30_spmd, body=%wide.region_27.29_spmd.sunk | while | flops 2195308544 | bytes 100770192 | solution.py:394
  275.3 8.2 fusion.290
  283.5 11.6 %fusion.293 = f32[4,2048,64]{1,2,0:T(8,128)S(1)} fusion(bf16[4,512,64]{1,2,0:T(8,128)(2,1)S(1)} %get-tuple-element.1243, f32[4,2048,512]{2,1,0:T(8,128)} %fusion.290, f32[4,512]{1,0:T(4,128)S(1)} %get-tuple-element.1247, f32[4,512]{1,0:T(4,128)S(1)} %copy-done.111, pred[512,2048]{0,1:T(8,128)(4,1)} %and_and_fusion.8, ...), kind=kOutput, calls=%fused_computation.11.clone.1 | convolution fusion | flops 1099431936 | bytes 21512192 | tf_op jit(solution)/shard_map/while/body/eval_jaxpr/hqk,hqd->khd/dot_general | solution.py:352
  295.1 10.6 %fusion.292 = f32[4,2048,64]{1,2,0:T(8,128)} fusion(bf16[4,512,64]{1,2,0:T(8,128)(2,1)} %copy-done.37, f32[4,2048,512]{2,1,0:T(8,128)} %fusion.290, f32[4,512]{1,0:T(4,128)S(1)} %copy-done.111, pred[512,2048]{0,1:T(8,128)(4,1)S(1)} %copy-done.9), kind=kOutput, calls=%fused_computation.4.clone.1 | convolution fusion | flops 553648128 | bytes 20193280 | tf_op jit(solution)/shard_map/while/body/eval_jaxpr/hqk,hqd->khd/dot_general | solution.py:345
  309.7 5.4 copy.198
  315.1 4.7 constant_dynamic-update-slice_fusion.2
  331.3 8.2 fusion.290
  339.5 11.6 %fusion.293 = f32[4,2048,64]{1,2,0:T(8,128)S(1)} fusion(bf16[4,512,64]{1,2,0:T(8,128)(2,1)S(1)} %get-tuple-element.1243, f32[4,2048,512]{2,1,0:T(8,128)} %fusion.290, f32[4,512]{1,0:T(4,128)S(1)} %get-tuple-element.1247, f32[4,512]{1,0:T(4,128)S(1)} %copy-done.111, pred[512,2048]{0,1:T(8,128)(4,1)} %and_and_fusion.8, ...), kind=kOutput, calls=%fused_computation.11.clone.1 | convolution fusion | flops 1099431936 | bytes 21512192 | tf_op jit(solution)/shard_map/while/body/eval_jaxpr/hqk,hqd->khd/dot_general | solution.py:352
  351.1 10.6 %fusion.292 = f32[4,2048,64]{1,2,0:T(8,128)} fusion(bf16[4,512,64]{1,2,0:T(8,128)(2,1)} %copy-done.37, f32[4,2048,512]{2,1,0:T(8,128)} %fusion.290, f32[4,512]{1,0:T(4,128)S(1)} %copy-done.111, pred[512,2048]{0,1:T(8,128)(4,1)S(1)} %copy-done.9), kind=kOutput, calls=%fused_computation.4.clone.1 | convolution fusion | flops 553648128 | bytes 20193280 | tf_op jit(solution)/shard_map/while/body/eval_jaxpr/hqk,hqd->khd/dot_general | solution.py:345
  365.7 5.4 copy.198
  371.1 4.7 constant_dynamic-update-slice_fusion.2
  384.0 5.0 convolution_convert_fusion
  389.1 67.0 %while.50 = (s32[]{:T(128)}, f32[4,512,64]{1,2,0:T(8,128)}, s32[512]{0:T(512)S(1)}, s32[4]{0:T(128)S(1)}, s32[2]{0:T(128)S(1)}, /*index=5*/s32[512]{0:T(512)S(1)...) while((s32[]{:T(128)}, f32[4,512,64]{1,2,0:T(8,128)}, ...), condition=%wide.region_25.26_spmd.clone, body=%wide.region_23.25_spmd.clone.sunk | while | flops 1640393216 | bytes 48851128 | solution.py:83
  399.9 8.2 fusion.310
  408.0 14.4 %fusion.311 = f32[4,512,64]{1,2,0:T(8,128)} fusion(bf16[2048,4,64]{0,2,1:T(8,128)(2,1)S(1)} %reshape.583, f32[4,2048,512]{2,1,0:T(8,128)} %fusion.310, f32[4,512]{1,0:T(4,128)S(1)} %get-tuple-element.1203, f32[4,512]{1,0:T(4,128)S(1)} %get-tuple-element.1200, pred[512,2048]{0,1:T(8,128)(4,1)} %and_and_fusion.11, bf16[2048,4,64]{0,2,1:T(8,128)(2,1)} %reshape.584, ...), kind=kOutput, calls=%fused_computation.73.clone.1 | convolution fusion | flops 1099300864 | bytes 21250048 | tf_op jit(solution)/shard_map/while/body/eval_jaxpr/hqk,khd->hqd/dot_general | solution.py:367
  433.2 8.2 fusion.310
  441.4 14.6 %fusion.311 = f32[4,512,64]{1,2,0:T(8,128)} fusion(bf16[2048,4,64]{0,2,1:T(8,128)(2,1)S(1)} %reshape.583, f32[4,2048,512]{2,1,0:T(8,128)} %fusion.310, f32[4,512]{1,0:T(4,128)S(1)} %get-tuple-element.1203, f32[4,512]{1,0:T(4,128)S(1)} %get-tuple-element.1200, pred[512,2048]{0,1:T(8,128)(4,1)} %and_and_fusion.11, bf16[2048,4,64]{0,2,1:T(8,128)(2,1)} %reshape.584, ...), kind=kOutput, calls=%fused_computation.73.clone.1 | convolution fusion | flops 1099300864 | bytes 21250048 | tf_op jit(solution)/shard_map/while/body/eval_jaxpr/hqk,khd->hqd/dot_general | solution.py:367
  461.2 94.5 %reduce-scatter.2.cloned.1.call-done = f32[256,512]{1,0:T(8,128)} async-done(((f32[4096,512]{1,0:T(8,128)}), f32[256,512]{1,0:T(8,128)}) %reduce-scatter.2.cloned.1.call-update) | async-done | bytes 524304 | tf_op jit(solution)/shard_map/reduce_scatter | solution.py:393
  577.3 8.0 all-reduce.20.cloned.1.call-done
  591.9 141.2 %all-reduce.16.cloned.1.call-done = (f32[1024,128]{1,0:T(8,128)}, f32[1024,128]{1,0:T(8,128)}, f32[1024,128]{1,0:T(8,128)}, f32[1024,128]{1,0:T(8,128)}, f32[1024,128]{1,0:T(8,128)}) async-done(((f32[1024,128]{1,0:T(8,128)}, f32[1024,128]{1,0:T(8,128)}, f32[1024,128]{1,0:T(8,128)}, f32[1024,128]{1,0:T(8,128)}, f32[1024,128]{1,0:T(8,128)}), (f32[1024,128]{1,0:T(8,128)}, f32[1024,128]{1,0:T(8,128)}, ...) | async-done | bytes 2621456 | tf_op jit(solution)/shard_map/psum | solution.py:436
  733.2 204.8 %all-reduce.18.cloned.1.call-done = (f32[128,512]{1,0:T(8,128)}, f32[128,256]{1,0:T(8,128)}, f32[128,256]{1,0:T(8,128)}, f32[512,128]{1,0:T(8,128)}, f32[128,102...) async-done(((f32[128,512]{1,0:T(8,128)}, f32[128,256]{1,0:T(8,128)}, f32[128,256]{1,0:T(8,128)}, ...) | async-done | bytes 5373968 | tf_op jit(solution)/shard_map/psum | solution.py:439
  (496 shorter events, 220.3 us)
Async XLA Ops:
  7.2 188.9 %copy-start = (bf16[512,1024]{1,0:T(8,128)(2,1)S(1)}, bf16[512,1024]{1,0:T(8,128)(2,1)}, u32[]{:S(2)}) copy-start(bf16[512,1024]{1,0:T(8,128)(2,1)} %param.44) | copy-start | bytes 3145732
  7.2 74.8 %all-gather.4.cloned.1.call-start = ((), (), s32[]{:S(2)}) async-start(), calls=%async_computation.1 | async-start | bytes 2228224 | tf_op jit(solution)/shard_map/all_gather | solution.py:223
  7.3 15.3 %copy-start.95 = (s32[128]{0:T(128)}, s32[128]{0:T(128)S(1)}, u32[]{:S(2)}) copy-start(s32[128]{0:T(128)S(1)} %and_select_fusion) | copy-start | bytes 1540
  18.4 126.4 %all-gather.6.cloned.1.call-start = ((), (), s32[]{:S(2)}) async-start(), calls=%async_computation.4 | async-start | bytes 2228224 | tf_op jit(solution)/shard_map/all_gather | solution.py:224
  21.8 193.3 %all-reduce.22.cloned.1.call-start = ((), (), s32[]{:S(2)}) async-start(), calls=%async_computation.8 | async-start | bytes 1179648 | tf_op jit(solution)/shard_map/psum | solution.py:252
  26.1 55.9 %copy-start.12 = (f32[256,512]{0,1:T(8,128)}, f32[256,512]{0,1:T(8,128)S(1)}, u32[]{:S(2)}) copy-start(f32[256,512]{0,1:T(8,128)S(1)} %copy.146) | copy-start | bytes 1572868
  26.2 59.7 %copy-start.93 = (f32[256,8]{0,1:T(8,128)}, f32[256,8]{0,1:T(8,128)S(1)}, u32[]{:S(2)}) copy-start(f32[256,8]{0,1:T(8,128)S(1)} %multiply_reduce_fusion.4) | copy-start | bytes 24580
  26.2 59.7 %copy-start.91 = (f32[256,8]{0,1:T(8,128)}, f32[256,8]{0,1:T(8,128)S(1)}, u32[]{:S(2)}) copy-start(f32[256,8]{0,1:T(8,128)S(1)} %fusion.101) | copy-start | bytes 24580
  117.5 32.4 %copy-start.83 = (s32[4]{0:T(128)}, s32[4]{0:T(128)S(1)}, u32[]{:S(2)}) copy-start(s32[4]{0:T(128)S(1)} %get-tuple-element.1378) | copy-start | bytes 52
  117.5 32.4 %copy-start.117 = (s32[2]{0:T(128)}, s32[2]{0:T(128)S(1)}, u32[]{:S(2)}) copy-start(s32[2]{0:T(128)S(1)} %get-tuple-element.1386) | copy-start | bytes 28
  149.9 45.3 %copy-start.62 = (bf16[512,128]{1,0:T(8,128)(2,1)S(1)}, bf16[512,128]{1,0:T(8,128)(2,1)}, u32[]{:S(2)}) copy-start(bf16[512,128]{1,0:T(8,128)(2,1)} %param.55) | copy-start | bytes 393220
  197.3 58.0 %all-reduce.14.cloned.1.call-start = ((), (), s32[]{:S(2)}) async-start(), calls=%async_computation.2 | async-start | bytes 1048576 | tf_op jit(solution)/shard_map/psum | solution.py:312
  217.0 40.3 %copy-start.7 = (f32[256,1024]{1,0:T(8,128)}, f32[256,1024]{1,0:T(8,128)S(1)}, u32[]{:S(2)}) copy-start(f32[256,1024]{1,0:T(8,128)S(1)} %get-tuple-element.814) | copy-start | bytes 3145732
  235.3 320.4 %reduce-scatter.2.cloned.1.call-start = ((), (), s32[]{:S(2)}) async-start(), calls=%async_computation.3 | async-start | bytes 8912896 | tf_op jit(solution)/shard_map/reduce_scatter | solution.py:393
  376.5 208.7 %all-reduce.20.cloned.1.call-start = ((), (), s32[]{:S(2)}) async-start(), calls=%async_computation.7 | async-start | bytes 2228224 | tf_op jit(solution)/shard_map/psum | solution.py:274
  389.1 68.3 %copy-start.41 = (f32[256,32]{0,1:T(8,128)S(1)}, f32[256,32]{0,1:T(8,128)}, u32[]{:S(2)}) copy-start(f32[256,32]{0,1:T(8,128)} %copy-done.40) | copy-start | bytes 98308
  389.1 68.3 %copy-start.43 = (f32[256,32]{0,1:T(8,128)S(1)}, f32[256,32]{0,1:T(8,128)}, u32[]{:S(2)}) copy-start(f32[256,32]{0,1:T(8,128)} %copy-done.42) | copy-start | bytes 98308
  389.1 68.4 %copy-start.114 = (f32[64]{0:T(128)S(1)}, f32[64]{0:T(128)}, u32[]{:S(2)}) copy-start(f32[64]{0:T(128)} %param.42) | copy-start | bytes 772
  389.1 69.6 %copy-start.94 = (f32[256,8]{0,1:T(8,128)S(1)}, f32[256,8]{0,1:T(8,128)}, u32[]{:S(2)}) copy-start(f32[256,8]{0,1:T(8,128)} %copy-done.93) | copy-start | bytes 24580
  389.1 69.6 %copy-start.92 = (f32[256,8]{0,1:T(8,128)S(1)}, f32[256,8]{0,1:T(8,128)}, u32[]{:S(2)}) copy-start(f32[256,8]{0,1:T(8,128)} %copy-done.91) | copy-start | bytes 24580
  458.7 98.1 %copy-start.21 = (f32[256,256]{0,1:T(8,128)S(1)}, f32[256,256]{0,1:T(8,128)}, u32[]{:S(2)}) copy-start(f32[256,256]{0,1:T(8,128)} %copy-done.20) | copy-start | bytes 786436
  458.7 98.1 %copy-start.115 = (f32[64]{0:T(128)S(1)}, f32[64]{0:T(128)}, u32[]{:S(2)}) copy-start(f32[64]{0:T(128)} %param.43) | copy-start | bytes 772
  458.7 98.2 %copy-start.104 = (f32[256,4]{0,1:T(4,128)S(1)}, f32[256,4]{0,1:T(4,128)}, u32[]{:S(2)}) copy-start(f32[256,4]{0,1:T(4,128)} %copy-done.103) | copy-start | bytes 12292
  458.7 98.2 %copy-start.102 = (f32[256,4]{0,1:T(4,128)S(1)}, f32[256,4]{0,1:T(4,128)}, u32[]{:S(2)}) copy-start(f32[256,4]{0,1:T(4,128)} %copy-done.101) | copy-start | bytes 12292
  460.3 99.1 %copy-start.74 = (bf16[1024,128]{1,0:T(8,128)(2,1)S(1)}, bf16[1024,128]{1,0:T(8,128)(2,1)}, u32[]{:S(2)}) copy-start(bf16[1024,128]{1,0:T(8,128)(2,1)} %param.53) | copy-start | bytes 786436
  461.2 98.6 %copy-start.75 = (bf16[1024,128]{1,0:T(8,128)(2,1)S(1)}, bf16[1024,128]{1,0:T(8,128)(2,1)}, u32[]{:S(2)}) copy-start(bf16[1024,128]{1,0:T(8,128)(2,1)} %param.51) | copy-start | bytes 786436
  562.8 170.4 %all-reduce.16.cloned.1.call-start = ((), (), s32[]{:S(2)}) async-start(), calls=%async_computation.5 | async-start | bytes 5242880 | tf_op jit(solution)/shard_map/psum | solution.py:436
  568.0 17.2 %copy-start.19 = (bf16[256,1,1024]{2,0,1:T(8,128)(2,1)S(1)}, bf16[256,1,1024]{2,0,1:T(8,128)(2,1)}, u32[]{:S(2)}) copy-start(bf16[256,1,1024]{2,0,1:T(8,128)(2,1)} %param.65) | copy-start | bytes 1572868
  570.5 367.4 %all-reduce.18.cloned.1.call-start = ((), (), s32[]{:S(2)}) async-start(), calls=%async_computation.6 | async-start | bytes 10747904 | tf_op jit(solution)/shard_map/psum | solution.py:439
  573.6 15.0 %copy-start.8 = (f32[256,1024]{1,0:T(8,128)S(1)}, f32[256,1024]{1,0:T(8,128)}, u32[]{:S(2)}) copy-start(f32[256,1024]{1,0:T(8,128)} %copy-done.7) | copy-start | bytes 3145732
  573.6 15.0 %copy-start.36 = (bf16[128,1024]{1,0:T(8,128)(2,1)S(1)}, bf16[128,1024]{1,0:T(8,128)(2,1)}, u32[]{:S(2)}) copy-start(bf16[128,1024]{1,0:T(8,128)(2,1)} %param.62) | copy-start | bytes 786436
  733.2 217.0 %copy-start.59 = (f32[1024,128]{1,0:T(8,128)S(1)}, f32[1024,128]{1,0:T(8,128)}, u32[]{:S(2)}) copy-start(f32[1024,128]{1,0:T(8,128)} %get-tuple-element.1261) | copy-start | bytes 1572868
  (109 other events, 571.1 us)
Sparse Core Ops, SparseCore 0:
  18.5 63.4 all-gather.3
  85.4 59.3 all-gather.5
  197.5 17.5 all-reduce.21
  235.4 19.9 all-reduce.13
  376.6 178.9 reduce-scatter.1
  562.9 22.3 all-reduce.19
  593.8 139.3 all-reduce.15
  740.7 197.1 all-reduce.17
where the time goes:
time: 968 us; the launch traced here: 963 us
  waiting for transfers between devices  561 us (58%)
  matrix products  207 us (21%)
  local copies, waits for them, and re-layouts  108 us (11%)
  other arithmetic  64.9 us (7%)
  between operations  16.1 us (2%)
    psum x1, waiting for transfers between devices, per_device(): lax.psum((query_out_grad, key_out_grad, value_out_grad, out_in_grad, out_...  205 us
    psum x1, waiting for transfers between devices, per_device(): lax.psum((query_in_grad, key_in_grad, value_in_grad, gate_in_grad, up_in_...  141 us
    reduce_scatter x1, waiting for transfers between devices, per_device(): lax.psum_scatter(lax.map(one_block, offsets).reshape(tok_rows * lax.axis_...  94.5 us
    all_gather x1, waiting for transfers between devices, per_device(): lax.all_gather(key_flat.reshape(1, tok_rows, kv_width), 'ctx', axis=0, ti...  55.5 us
    dot_general x4, matrix products, score_grads(): jnp.einsum('hqd,khd->hqk', query_block, key_heads_blk, preferred_element_...  32.7 us
    unnamed x254, local copies, waits for them, and re-layouts  32.5 us
    dot_general x2, matrix products, query_step(): jnp.einsum('hqk,khd->hqd', grad_scores, key_heads_blk, preferred_element_...  29 us
    all_gather x1, waiting for transfers between devices, per_device(): lax.all_gather(value_flat.reshape(1, tok_rows, kv_width), 'ctx', axis=0,...  27.3 us
  transfers between devices with their start and end apart: 8, of which 8 were waited for; matrix products, arithmetic and copies ran while one was open for 16% of the time, Pallas kernels for 0%

commit v1 on v0

v1 whole, which is shorter than its diff:
```python
import functools
import math

import jax
import jax.numpy as jnp
from jax import lax
from jax.experimental import pallas as pl
from jax.experimental.pallas import tpu as pltpu
from jax.sharding import PartitionSpec as P

RANK = 16
DOC_MIN = 200

norm_eps = 1e-05
theta_base = 1000000.0
BF = jnp.bfloat16
F32 = jnp.float32
LOG2E = 1.4426950408889634
VMEM_LIMIT = 56 * 1024 * 1024


def mm(left, right):
    return jnp.dot(left, right, preferred_element_type=F32)


def mm_nt(left, right):
    return lax.dot_general(left, right, (((1,), (1,)), ((), ())), preferred_element_type=F32)


def mm_tn(left, right):
    return lax.dot_general(left, right, (((0,), (0,)), ((), ())), preferred_element_type=F32)


def iota(shape, dim):
    return lax.broadcasted_iota(jnp.int32, shape, dim)


class Cfg:
    def __init__(self, tokens, n_ctx, heads_kv, groups, head_dim, docs, adapt_width, width, hidden):
        self.T = tokens
        self.n = n_ctx
        self.G = heads_kv
        self.lo = n_ctx // heads_kv
        self.groups = groups
        self.hd = head_dim
        self.docs = docs
        self.AW = adapt_width
        self.slots = min(docs, adapt_width // RANK)
        self.S = self.slots * RANK
        self.D = width
        self.F = hidden
        self.R = max(16, min(tokens, 512 // n_ctx))
        self.NT = tokens // self.R
        self.span = self.R * n_ctx
        self.QH = self.G * self.R
        self.KT = n_ctx * self.R


def doc_starts(cfg, meta):
    out = [jnp.int32(0)]
    for j in range(cfg.docs):
        out.append(out[-1] + meta[2 + j] + (DOC_MIN - 1))
    return out


def start_of(starts, token):
    out = jnp.zeros_like(token)
    for s in starts[1:-1]:
        out = jnp.where(token >= s, s, out)
    return out


def end_of(starts, token):
    out = starts[1]
    for j in range(1, len(starts) - 1):
        out = jnp.where(token >= starts[j], starts[j + 1], out)
    return out


def adapter_mask(cfg, meta):
    token = iota((cfg.T, cfg.AW), 0) * cfg.n + meta[0]
    starts = doc_starts(cfg, meta)
    adapter = jnp.full((cfg.T, cfg.AW), meta[2 + cfg.docs], jnp.int32)
    for j in range(1, cfg.docs):
        adapter = jnp.where(token >= starts[j], meta[2 + cfg.docs + j], adapter)
    return (adapter == iota((cfg.T, cfg.AW), 1) // RANK).astype(F32)


def slot_select(cfg, meta):
    row = iota((cfg.AW, cfg.S), 0)
    col = iota((cfg.AW, cfg.S), 1)
    if cfg.S == cfg.AW:
        return (row == col).astype(BF)
    target = jnp.full((cfg.AW, cfg.S), -1, jnp.int32)
    for s in range(cfg.slots):
        mine = meta[2 + cfg.docs + s]
        again = jnp.int32(0)
        for e in range(s):
            again = jnp.where(meta[2 + cfg.docs + e] == mine, 1, again)
        base = jnp.where(again == 1, -4 * cfg.AW, mine * RANK)
        target = jnp.where(col // RANK == s, base + col % RANK, target)
    return (row == target).astype(BF)


def block_mean(values, hd):
    width = values.shape[1]
    ones = (iota((width, width), 0) // hd == iota((width, width), 1) // hd).astype(BF)
    high = values.astype(BF)
    low = (values - high.astype(F32)).astype(BF)
    return (mm(high, ones) + mm(low, ones)) * (1.0 / hd)


def swap_halves(values, hd):
    width = values.shape[1]
    half = hd // 2
    first = iota(values.shape, 1) % hd < half
    return jnp.where(first, pltpu.roll(values, width - half, 1), pltpu.roll(values, half, 1))


def lanes(values, copies):
    return jnp.concatenate([values] * copies, axis=1) if copies > 1 else values


def params(**kw):
    return pltpu.CompilerParams(vmem_limit_bytes=VMEM_LIMIT, **kw)


SMEM = pl.BlockSpec(memory_space=pltpu.SMEM)


def call(kernel, outs, ins, scratch=(), flops=0, bytes_accessed=0, name=None):
    return pl.pallas_call(
        kernel,
        out_shape=[jax.ShapeDtypeStruct(s, d) for s, d in outs],
        in_specs=[SMEM] + [pl.BlockSpec(memory_space=pltpu.VMEM)] * (len(ins) - 1),
        out_specs=[pl.BlockSpec(memory_space=pltpu.VMEM)] * len(outs),
        scratch_shapes=list(scratch),
        compiler_params=params(),
        cost_estimate=pl.CostEstimate(
            flops=flops, bytes_accessed=bytes_accessed, transcendentals=0
        ),
        name=name,
    )(*ins)


def pre_kernel(
    cfg, meta, x_ref, gain, wq, wk, wv, aq, ak, av, bq, bk, bv, qg, kg, cos, sin, *refs
):
    G, hd = cfg.G, cfg.hd
    kv_out, q_out = refs[:G], refs[G : 2 * G]
    qraw_ref, kraw_ref, sides_ref, normed_ref, kv_scr, q_scr = refs[2 * G :]
    hi = meta[0] // cfg.lo
    x = x_ref[...].astype(F32)
    rr = lax.rsqrt(jnp.mean(x * x, axis=-1, keepdims=True) + norm_eps)
    normed = (x * rr * gain[...]).astype(BF)
    normed_ref[...] = normed
    mask = adapter_mask(cfg, meta)
    select = slot_select(cfg, meta)
    raws = []
    for i, (w, a, b) in enumerate(((wq, aq, bq), (wk, ak, bk), (wv, av, bv))):
        side = (mask * mm(normed, a[...])).astype(BF)
        sides_ref[i] = mm(side, select).astype(BF)
        raws.append(mm(normed, w[...]) + mm(side, b[...]))
    qraw, kraw, vraw = raws
    qraw_ref[...] = qraw
    kraw_ref[...] = kraw

    def prep(raw, g):
        copies = raw.shape[1] // hd
        scaled = raw * lax.rsqrt(block_mean(raw * raw, hd) + norm_eps) * lanes(g[...], copies)
        per = raw.shape[1] // cos.shape[1]
        return scaled * lanes(cos[...], per) + swap_halves(scaled, hd) * lanes(sin[...], per)

    query = prep(qraw, qg).astype(BF)
    key = prep(kraw, kg).astype(BF)
    value = vraw.astype(BF)
    gw = cfg.groups * hd
    for h in range(G):
        q_scr[h] = query[:, h * gw : (h + 1) * gw]
        kv_scr[h] = jnp.concatenate(
            [key[:, h * hd : (h + 1) * hd], value[:, h * hd : (h + 1) * hd]], axis=1
        )
    for k in range(G):
        kv_out[k][...] = kv_scr[hi ^ k]
        q_out[k][...] = q_scr[hi ^ k]


def load_tiles(cfg, scr, pieces):
    R = cfg.R
    for p, piece in enumerate(pieces):
        for t in range(cfg.NT):
            scr[t, p * R : (p + 1) * R, :] = piece[t * R : (t + 1) * R, :]


def split_pieces(ref, count):
    return [ref.at[i] for i in range(count)]


def token_in_span(cfg, meta, index):
    hi, lo = meta[0] // cfg.lo, meta[0] % cfg.lo
    piece, row = index // cfg.R, index % cfg.R
    j, k = piece // cfg.G, piece % cfg.G
    return row * cfg.n + (hi ^ k) * cfg.lo + (lo ^ j)


def pad_queries(cfg, qq, side):
    hd = cfg.hd
    wide = qq.astype(F32)
    first = iota(wide.shape, 1) < hd
    rolled = pltpu.roll(wide, hd, 1)
    if side == 0:
        parts = [jnp.where(first, wide, 0.0), jnp.where(first, rolled, 0.0)]
    else:
        parts = [jnp.where(first, 0.0, rolled), jnp.where(first, 0.0, wide)]
    return jnp.concatenate(parts, axis=0).astype(BF)


def query_tile_ranges(cfg, starts, qt):
    first = qt * cfg.span
    s_lo = start_of(starts, first) // cfg.span
    s_full = (start_of(starts, first + cfg.span - 1) + cfg.span - 1) // cfg.span
    return s_lo, jnp.minimum(s_full, qt)


def attend_kernel(cfg, meta, *refs):
    G, T, R, hd = cfg.G, cfg.T, cfg.R, cfg.hd
    q_in, own, others = refs[:G], refs[G], refs[G + 1 : G + cfg.lo]
    rest = refs[G + cfg.lo :]
    o_out, o_all, linv, kv_scr, va_scr, q_scr = rest[:G], *rest[G:]
    pieces = split_pieces(own, G)
    for ref in others:
        pieces = pieces + split_pieces(ref, G)
    load_tiles(cfg, kv_scr, pieces)
    load_tiles(cfg, q_scr, q_in)
    starts = doc_starts(cfg, meta)
    QH = cfg.QH
    scale = hd ** (-0.5) * LOG2E
    key_off = token_in_span(cfg, meta, iota((1, cfg.KT), 1))
    row_off = token_in_span(cfg, meta, iota((2 * QH, 1), 0) % QH)
    lane_first = iota((cfg.KT, 2 * hd), 1) < hd

    def fill(t, carry):
        va_scr[t] = jnp.where(lane_first, 1.0, kv_scr[t].astype(F32)).astype(BF)
        return carry

    lax.fori_loop(0, cfg.NT, fill, 0)
    half = iota((QH, 2 * hd), 1) < hd

    def query_tile(qt, carry):
        queries = pad_queries(cfg, q_scr[qt], 0)
        token = row_off + qt * cfg.span
        first_key = start_of(starts, token)
        s_lo, s_full = query_tile_ranges(cfg, starts, qt)

        def tile(s, acc, masked):
            e = jnp.exp2(mm_nt(queries, kv_scr[s]) * scale)
            if masked:
                key_token = key_off + s * cfg.span
                e = jnp.where((key_token <= token) & (key_token >= first_key), e, 0.0)
            return acc + mm(e.astype(BF), va_scr[s])

        acc = jnp.zeros((2 * QH, 2 * hd), F32)
        acc = lax.fori_loop(s_lo, s_full, lambda s, a: tile(s, a, True), acc)
        acc = lax.fori_loop(s_full, qt, lambda s, a: tile(s, a, False), acc)
        acc = tile(qt, acc, True)
        inv0 = 1.0 / acc[:QH]
        inv1 = 1.0 / acc[QH:]
        out0 = pltpu.roll(acc[:QH], hd, 1) * inv0
        out1 = acc[QH:] * pltpu.roll(inv1, hd, 1)
        out = jnp.where(half, out0, out1).astype(BF)
        inv = jnp.where(half, inv0, pltpu.roll(inv1, hd, 1))
        rows = pl.ds(pl.multiple_of(qt * R, R), R)
        for k in range(G):
            o_out[k][rows, :] = out[k * R : (k + 1) * R]
            o_all[k, rows, :] = out[k * R : (k + 1) * R]
            linv[k, rows, :] = inv[k * R : (k + 1) * R]
        return carry

    lax.fori_loop(0, cfg.NT, query_tile, 0)


def scale_kernel(cfg, meta, *refs):
    G = cfg.G
    for k in range(G):
        refs[G + 1][k] = (refs[k][...].astype(F32) * refs[G][k]).astype(BF)


def grad_query_kernel(cfg, meta, *refs):
    G, T, R, hd = cfg.G, cfg.T, cfg.R, cfg.hd
    q_in, own, others = refs[:G], refs[G], refs[G + 1 : G + cfg.lo]
    go_ref, o_ref = refs[G + cfg.lo : G + cfg.lo + 2]
    rest = refs[G + cfg.lo + 2 :]
    dq_out, kv_scr, q_scr, go_scr, o_scr = rest[:G], *rest[G:]
    pieces = split_pieces(own, G)
    for ref in others:
        pieces = pieces + split_pieces(ref, G)
    load_tiles(cfg, kv_scr, pieces)
    load_tiles(cfg, q_scr, q_in)
    load_tiles(cfg, go_scr, split_pieces(go_ref, G))
    load_tiles(cfg, o_scr, split_pieces(o_ref, G))
    starts = doc_starts(cfg, meta)
    QH = cfg.QH
    scale = hd ** (-0.5) * LOG2E
    key_off = token_in_span(cfg, meta, iota((1, cfg.KT), 1))
    row_off = token_in_span(cfg, meta, iota((2 * QH, 1), 0) % QH)
    half = iota((QH, 2 * hd), 1) < hd

    def query_tile(qt, carry):
        queries = pad_queries(cfg, q_scr[qt], 0)
        grads = pad_queries(cfg, go_scr[qt], 1)
        prod = go_scr[qt].astype(F32) * o_scr[qt].astype(F32)
        delta = jnp.concatenate(
            [
                jnp.sum(jnp.where(half, prod, 0.0), axis=1, keepdims=True),
                jnp.sum(jnp.where(half, 0.0, prod), axis=1, keepdims=True),
            ],
            axis=0,
        )
        token = row_off + qt * cfg.span
        first_key = start_of(starts, token)
        s_lo, s_full = query_tile_ranges(cfg, starts, qt)

        def tile(s, acc, masked):
            kv = kv_scr[s]
            e = jnp.exp2(mm_nt(queries, kv) * scale)
            if masked:
                key_token = key_off + s * cfg.span
                e = jnp.where((key_token <= token) & (key_token >= first_key), e, 0.0)
            ds = e * (mm_nt(grads, kv) - delta)
            return acc + mm(ds.astype(BF), kv)

        acc = jnp.zeros((2 * QH, 2 * hd), F32)
        acc = lax.fori_loop(s_lo, s_full, lambda s, a: tile(s, a, True), acc)
        acc = lax.fori_loop(s_full, qt, lambda s, a: tile(s, a, False), acc)
        acc = tile(qt, acc, True)
        out = jnp.where(half, acc[:QH], pltpu.roll(acc[QH:], hd, 1)) * hd ** (-0.5)
        out = out.astype(BF)
        rows = pl.ds(pl.multiple_of(qt * R, R), R)
        for k in range(G):
            dq_out[k][rows, :] = out[k * R : (k + 1) * R]
        return carry

    lax.fori_loop(0, cfg.NT, query_tile, 0)


def grad_key_kernel(cfg, meta, *refs):
    G, T, R, hd, lo = cfg.G, cfg.T, cfg.R, cfg.hd, cfg.lo
    own = refs[0]
    q_refs, go_refs, o_refs = (refs[1 + i * lo : 1 + (i + 1) * lo] for i in range(3))
    rest = refs[1 + 3 * lo :]
    dkv_out, kv_scr, q_scr, go_scr, o_scr, delta_scr = rest[:G], *rest[G:]
    load_tiles(cfg, kv_scr, split_pieces(own, G))
    for scr, group in ((q_scr, q_refs), (go_scr, go_refs), (o_scr, o_refs)):
        load_tiles(cfg, scr, [piece for ref in group for piece in split_pieces(ref, G)])
    starts = doc_starts(cfg, meta)
    QH = cfg.QH
    scale = hd ** (-0.5) * LOG2E
    pick = (iota((16, 2 * hd), 1) // hd == iota((16, 2 * hd), 0)).astype(BF)

    def deltas(t, carry):
        prod = go_scr[t].astype(F32) * o_scr[t].astype(F32)
        high = prod.astype(BF)
        low = (prod - high.astype(F32)).astype(BF)
        delta_scr[t] = mm_nt(pick, high) + mm_nt(pick, low)
        return carry

    lax.fori_loop(0, cfg.NT, deltas, 0)
    query_off = token_in_span(cfg, meta, iota((1, cfg.KT), 1))
    row_off = token_in_span(cfg, meta, iota((2 * QH, 1), 0) % QH)
    first = iota((QH, 2 * hd), 1) < hd

    def key_tile(kt, carry):
        kv = kv_scr[kt].astype(F32)
        rolled = pltpu.roll(kv, hd, 1)
        keys = jnp.concatenate(
            [jnp.where(first, kv, 0.0), jnp.where(first, 0.0, rolled)], axis=0
        ).astype(BF)
        values = jnp.concatenate(
            [jnp.where(first, rolled, 0.0), jnp.where(first, 0.0, kv)], axis=0
        ).astype(BF)
        key_token = row_off + kt * cfg.span
        end_first = end_of(starts, kt * cfg.span)
        end_last = end_of(starts, (kt + 1) * cfg.span - 1)
        q_full = jnp.maximum(end_first // cfg.span, kt + 1)
        q_stop = (end_last - 1) // cfg.span + 1

        def tile(t, acc, masked):
            grad_keys, grad_values = acc
            queries, grads = q_scr[t], go_scr[t]
            e = jnp.exp2(mm_nt(keys, queries) * scale)
            if masked:
                token = query_off + t * cfg.span
                e = jnp.where((key_token <= token) & (key_token >= start_of(starts, token)), e, 0.0)
            dp = mm_nt(values, grads)
            delta = delta_scr[t]
            ds = jnp.concatenate(
                [
                    (e[:QH] * (dp[:QH] - delta[0:1])).astype(BF),
                    (e[QH:] * (dp[QH:] - delta[1:2])).astype(BF),
                ],
                axis=0,
            )
            return grad_keys + mm(ds, queries), grad_values + mm(e.astype(BF), grads)

        zero = jnp.zeros((2 * QH, 2 * hd), F32)
        acc = tile(kt, (zero, zero), True)
        acc = lax.fori_loop(kt + 1, q_full, lambda t, a: tile(t, a, False), acc)
        acc = lax.fori_loop(q_full, q_stop, lambda t, a: tile(t, a, True), acc)
        grad_keys, grad_values = acc
        gk = (grad_keys[:QH] + pltpu.roll(grad_keys[QH:], hd, 1)) * hd ** (-0.5)
        gv = pltpu.roll(grad_values[:QH], hd, 1) + grad_values[QH:]
        out = jnp.where(first, gk, gv).astype(BF)
        rows = pl.ds(pl.multiple_of(kt * R, R), R)
        for k in range(G):
            dkv_out[k][rows, :] = out[k * R : (k + 1) * R]
        return carry

    lax.fori_loop(0, cfg.NT, key_tile, 0)


def place_pieces(cfg, hi, scr, pieces):
    w = pieces[0].shape[1]
    for k in range(cfg.G):
        at = pl.multiple_of((hi ^ k) * w, w)
        scr[:, pl.ds(at, w)] = pieces[k][...]


def out_kernel(cfg, meta, *refs):
    G = cfg.G
    wo, ao, part, attn = refs[G:]
    place_pieces(cfg, meta[0] // cfg.lo, attn, refs[:G])
    rows = attn[...]
    part[:, : cfg.D] = mm(rows, wo[...]).astype(BF)
    part[:, cfg.D :] = mm(rows, ao[...]).astype(BF)


def ffn_kernel(
    cfg, steps, meta, x_ref, own, other, bo, gain, wg, wu, wd, bg, bu, ag, au, ad, bd, cot_ref,
    mixed_ref, dfn_ref, part_ref, bgate, bup, adown, akeep, asend, oside,
    fn, sg, su, gsd, sgt, sut, gsdt, down, side_sum, dfn, gsg, gsu, a_scr,
):
    step = pl.program_id(0)
    S, D = cfg.S, cfg.D

    @pl.when(step == 0)
    def _():
        mask = adapter_mask(cfg, meta)
        select = slot_select(cfg, meta)
        total = own[...].astype(F32) + other[...].astype(F32)
        out_side = (mask * total[:, D:]).astype(BF)
        oside[...] = mm(out_side, select).astype(BF)
        mixed = x_ref[...].astype(F32) + total[:, :D] + mm(out_side, bo[...])
        mixed_ref[...] = mixed
        rr = lax.rsqrt(jnp.mean(mixed * mixed, axis=-1, keepdims=True) + norm_eps)
        normed = (mixed * rr * gain[...]).astype(BF)
        fn[...] = normed
        side_g = (mask * mm(normed, ag[...])).astype(BF)
        side_u = (mask * mm(normed, au[...])).astype(BF)
        grad_side = (mask * mm_nt(cot_ref[...], bd[...])).astype(BF)
        sg[...] = side_g
        su[...] = side_u
        gsd[...] = grad_side
        sgt[...] = mm(side_g, select).T.astype(BF)
        sut[...] = mm(side_u, select).T.astype(BF)
        gsdt[...] = mm(grad_side, select).T.astype(BF)
        down[...] = jnp.zeros_like(down)
        side_sum[...] = jnp.zeros_like(side_sum)
        dfn[...] = jnp.zeros_like(dfn)
        gsg[...] = jnp.zeros_like(gsg)
        gsu[...] = jnp.zeros_like(gsu)

    normed = fn[...]
    gate = mm(normed, wg[...]) + mm(sg[...], bg[...])
    upper = mm(normed, wu[...]) + mm(su[...], bu[...])
    grad_hidden = mm_nt(cot_ref[...], wd[...]) + mm_nt(gsd[...], ad[...])
    sigma = 1.0 / (1.0 + jnp.exp(-gate))
    silu = gate * sigma
    hidden = (silu * upper).astype(BF)
    grad_gate = (grad_hidden * upper * (sigma + silu * (1.0 - sigma))).astype(BF)
    grad_upper = (grad_hidden * silu).astype(BF)
    down[...] += mm(hidden, wd[...])
    side_sum[...] += mm(hidden, ad[...])
    dfn[...] += mm_nt(grad_gate, wg[...]) + mm_nt(grad_upper, wu[...])
    gsg[...] += mm_nt(grad_gate, bg[...])
    gsu[...] += mm_nt(grad_upper, bu[...])
    bgate[...] = mm(sgt[...], grad_gate).astype(BF)
    bup[...] = mm(sut[...], grad_upper).astype(BF)
    adown[...] = mm(gsdt[...], hidden).astype(BF)

    @pl.when(step == steps - 1)
    def _():
        mask = adapter_mask(cfg, meta)
        select = slot_select(cfg, meta)
        side_g = (mask * gsg[...]).astype(BF)
        side_u = (mask * gsu[...]).astype(BF)
        dfn_ref[...] = (dfn[...] + mm_nt(side_g, ag[...]) + mm_nt(side_u, au[...])).astype(BF)
        part_ref[:, :D] = down[...].astype(BF)
        part_ref[:, D:] = side_sum[...].astype(BF)
        a_scr[:S, :] = mm(mm(side_g, select).T.astype(BF), fn[...])
        a_scr[S:, :] = mm(mm(side_u, select).T.astype(BF), fn[...])
        half = D // 2
        keep = pl.ds(pl.multiple_of(meta[1] * half, half), half)
        send = pl.ds(pl.multiple_of((1 - meta[1]) * half, half), half)
        akeep[...] = a_scr[:, keep].astype(BF)
        asend[...] = a_scr[:, send].astype(BF)


def ffn_call(cfg, meta, x, own, other, bo, gain, wg, wu, wd, bg, bu, ag, au, ad, bd, cot):
    T, D, F, AW, S = cfg.T, cfg.D, cfg.F, cfg.AW, cfg.S
    tile = 256
    steps = F // tile
    whole = lambda shape: pl.BlockSpec(shape, lambda i: (0,) * len(shape))
    cols = lambda rows: pl.BlockSpec((rows, tile), lambda i: (0, i))
    rows = lambda width: pl.BlockSpec((tile, width), lambda i: (i, 0))
    outs = [
        ((T, D), F32),
        ((T, D), BF),
        ((T, D + AW), BF),
        ((S, F), BF),
        ((S, F), BF),
        ((S, F), BF),
        ((2 * S, D // 2), BF),
        ((2 * S, D // 2), BF),
        ((T, S), BF),
    ]
    out_specs = [
        whole((T, D)),
        whole((T, D)),
        whole((T, D + AW)),
        cols(S),
        cols(S),
        cols(S),
        whole((2 * S, D // 2)),
        whole((2 * S, D // 2)),
        whole((T, S)),
    ]
    flops = 2 * T * D * F * 6
    return pl.pallas_call(
        functools.partial(ffn_kernel, cfg, steps),
        grid=(steps,),
        out_shape=[jax.ShapeDtypeStruct(s, d) for s, d in outs],
        in_specs=[
            SMEM,
            whole((T, D)),
            whole((T, D + AW)),
            whole((T, D + AW)),
            whole((AW, D)),
            whole((1, D)),
            cols(D),
            cols(D),
            rows(D),
            cols(AW),
            cols(AW),
            whole((D, AW)),
            whole((D, AW)),
            rows(AW),
            whole((AW, D)),
            whole((T, D)),
        ],
        out_specs=out_specs,
        scratch_shapes=[
            pltpu.VMEM((T, D), BF),
            pltpu.VMEM((T, AW), BF),
            pltpu.VMEM((T, AW), BF),
            pltpu.VMEM((T, AW), BF),
            pltpu.VMEM((S, T), BF),
            pltpu.VMEM((S, T), BF),
            pltpu.VMEM((S, T), BF),
            pltpu.VMEM((T, D), F32),
            pltpu.VMEM((T, AW), F32),
            pltpu.VMEM((T, D), F32),
            pltpu.VMEM((T, AW), F32),
            pltpu.VMEM((T, AW), F32),
            pltpu.VMEM((2 * S, D), F32),
        ],
        compiler_params=params(dimension_semantics=("arbitrary",)),
        cost_estimate=pl.CostEstimate(
            flops=flops, bytes_accessed=3 * D * F * 2, transcendentals=T * F
        ),
        name="ffn",
    )(meta, x, own, other, bo, gain, wg, wu, wd, bg, bu, ag, au, ad, bd, cot)


def mixed_grad_kernel(cfg, meta, *refs):
    G, D = cfg.G, cfg.D
    mixed_ref, own, other, cot, gain = refs[:5]
    o_in = refs[5 : 5 + G]
    wo, ao, bo, oside = refs[5 + G : 9 + G]
    rest = refs[9 + G :]
    gm_ref, ograds, go_out, attn, go_scr, gm_scr = rest[0], rest[1], rest[2 : 2 + G], *rest[2 + G :]
    hi = meta[0] // cfg.lo
    mixed = mixed_ref[...]
    w = (own[...].astype(F32) + other[...].astype(F32)) * gain[...]
    rr = lax.rsqrt(jnp.mean(mixed * mixed, axis=-1, keepdims=True) + norm_eps)
    inner = jnp.mean(w * mixed, axis=-1, keepdims=True)
    gm = cot[...].astype(F32) + rr * w - (rr * rr * rr * inner) * mixed
    gm_ref[...] = gm
    gmb = gm.astype(BF)
    gm_scr[...] = gmb
    mask = adapter_mask(cfg, meta)
    select = slot_select(cfg, meta)
    grad_side = (mask * mm_nt(gmb, bo[...])).astype(BF)
    go = (mm_nt(gmb, wo[...]) + mm_nt(grad_side, ao[...])).astype(BF)
    w = cfg.groups * cfg.hd
    for h in range(G):
        go_scr[h] = go[:, h * w : (h + 1) * w]
    for k in range(G):
        go_out[k][...] = go_scr[hi ^ k]
    place_pieces(cfg, hi, attn, o_in)
    ograds[0] = mm(mm(grad_side, select).T.astype(BF), attn[...]).astype(BF)
    half = D // 2
    mine = gm_scr[:, pl.ds(pl.multiple_of(meta[1] * half, half), half)]
    ograds[1] = mm(oside[...].astype(F32).T.astype(BF), mine).astype(BF)


def output_kernel(cfg, meta, mixed, own, other, bd, cot, out_ref, dgrad):
    D = cfg.D
    total = own[...].astype(F32) + other[...].astype(F32)
    mask = adapter_mask(cfg, meta)
    side = (mask * total[:, D:]).astype(BF)
    out_ref[...] = (mixed[...] + total[:, :D] + mm(side, bd[...])).astype(BF)
    half = D // 2
    mine = cot[:, pl.ds(pl.multiple_of(meta[1] * half, half), half)]
    dgrad[...] = mm(mm(side, slot_select(cfg, meta)).T.astype(BF), mine).astype(BF)


def qkv_grad_kernel(cfg, meta, *refs):
    G, D, S, hd = cfg.G, cfg.D, cfg.S, cfg.hd
    dq_in, dkv_in = refs[:G], refs[G : 2 * G]
    (
        normed, qraw, kraw, sides, cos, sin, qg, kg, wq, wk, wv, aq, ak, av, bq, bk, bv,
        part, bgrad, akeep, asend, dq_scr, dkv_scr, a_scr,
    ) = refs[2 * G :]
    hi = meta[0] // cfg.lo
    place_pieces(cfg, hi, dq_scr, dq_in)
    place_pieces(cfg, hi, dkv_scr, dkv_in)
    mask = adapter_mask(cfg, meta)
    select = slot_select(cfg, meta)

    def back(grad, raw, g):
        copies = raw.shape[1] // hd
        per = raw.shape[1] // cos.shape[1]
        un = grad * lanes(cos[...], per) - swap_halves(grad, hd) * lanes(sin[...], per)
        w = un * lanes(g[...], copies)
        rr = lax.rsqrt(block_mean(raw * raw, hd) + norm_eps)
        return rr * w - rr * rr * rr * raw * block_mean(w * raw, hd)

    dkv = dkv_scr[...]
    dk = jnp.concatenate([dkv[:, 2 * h * hd : (2 * h + 1) * hd] for h in range(G)], axis=1)
    dv = jnp.concatenate([dkv[:, (2 * h + 1) * hd : (2 * h + 2) * hd] for h in range(G)], axis=1)
    gq = back(dq_scr[...].astype(F32), qraw[...], qg).astype(BF)
    gk = back(dk.astype(F32), kraw[...], kg).astype(BF)
    total = jnp.zeros((cfg.T, D), F32)
    at = 0
    for i, (g, w, a, b) in enumerate(((gq, wq, aq, bq), (gk, wk, ak, bk), (dv, wv, av, bv))):
        grad_side = (mask * mm_nt(g, b[...])).astype(BF)
        total = total + mm_nt(g, w[...]) + mm_nt(grad_side, a[...])
        a_scr[i * S : (i + 1) * S, :] = mm(mm(grad_side, select).T.astype(BF), normed[...])
        width = g.shape[1]
        bgrad[:, at : at + width] = mm(sides[i].astype(F32).T.astype(BF), g).astype(BF)
        at = at + width
    part[...] = total.astype(BF)
    half = D // 2
    keep = pl.ds(pl.multiple_of(meta[1] * half, half), half)
    send = pl.ds(pl.multiple_of((1 - meta[1]) * half, half), half)
    akeep[...] = a_scr[:, keep].astype(BF)
    asend[...] = a_scr[:, send].astype(BF)


def input_grad_kernel(cfg, meta, x_ref, gain, gm, own, other, out):
    x = x_ref[...].astype(F32)
    w = (own[...].astype(F32) + other[...].astype(F32)) * gain[...]
    rr = lax.rsqrt(jnp.mean(x * x, axis=-1, keepdims=True) + norm_eps)
    inner = jnp.mean(w * x, axis=-1, keepdims=True)
    out[...] = (gm[...] + rr * w - (rr * rr * rr * inner) * x).astype(BF)


class Units:
    def __init__(self, cfg, shared, private):
        self.n = cfg.n
        self.high = cfg.S // 16
        self.us = self._layout(shared, 0)
        self.up = self._layout(private, 0)
        self.u = self.us + self.up
        self.shared, self.private = shared, private

    def _layout(self, widths, _):
        count = sum(w // 128 for w in widths) * self.high
        return -(-count // self.n)

    def places(self, which):
        widths, per, base = (
            (self.shared, self.us, 0) if which == 0 else (self.private, self.up, self.us)
        )
        at, out = 0, []
        for w in widths:
            spots = []
            for c in range(w // 128):
                for a in range(self.high):
                    spots.append((at // per, base + at % per, a, c))
                    at += 1
            out.append(spots)
        return out

    def spare(self):
        out = []
        for widths, per, base in ((self.shared, self.us, 0), (self.private, self.up, self.us)):
            count = sum(w // 128 for w in widths) * self.high
            out += [(i // per, base + i % per) for i in range(count, per * self.n)]
        return out


def pack(units, idx, out, arrays):
    for spots, values in zip(units.places(0) + units.places(1), arrays):
        for chunk, off, a, c in spots:
            out[chunk ^ idx, off] = values[a * 16 : a * 16 + 16, c * 128 : c * 128 + 128]
    for chunk, off in units.spare():
        out[chunk ^ idx, off] = jnp.zeros((16, 128), BF)


def add_halves(keep, got, count):
    total = (keep[...].astype(F32) + got[...].astype(F32)).astype(BF)
    rows = total.shape[0] // count
    return [total[i * rows : (i + 1) * rows] for i in range(count)]


def pack_ffn_kernel(cfg, units, meta, keep, got, bdown, ograds, bgate, bup, adown, out):
    shared = add_halves(keep, got, 2) + [bdown[...], ograds[1]]
    pack(units, meta[0], out, shared + [bgate[...], bup[...], adown[...], ograds[0]])


def pack_qkv_kernel(cfg, units, qw, kw, meta, keep, got, bgrad, out):
    private = [bgrad[:, :qw], bgrad[:, qw : qw + kw], bgrad[:, qw + kw :]]
    pack(units, meta[0], out, add_halves(keep, got, 3) + private)


def unpack(units, idx, ref, spots, base=0):
    cols = {}
    for chunk, off, a, c in spots:
        cols.setdefault(c, []).append(ref[chunk ^ idx, off - base])
    return jnp.concatenate([jnp.concatenate(cols[c], axis=0) for c in sorted(cols)], axis=1)


def expand_kernel(cfg, units, plan, meta, own, other, *outs):
    idx, wa = meta[0], meta[1]
    select = slot_select(cfg, meta)

    def write(out, values, transposed, at):
        full = mm(select, values)
        if transposed:
            out[at : at + full.shape[1], :] = full.T
        else:
            out[:, at : at + full.shape[1]] = full

    for (which, i, transposed), out in zip(plan, outs):
        spots = units.places(which)[i]
        mine = unpack(units, idx, own, spots)
        if which == 1:
            write(out, mine, transposed, 0)
        else:
            theirs = unpack(units, idx, other, spots)
            width = mine.shape[1]
            write(out, jnp.where(wa == 0, mine, theirs), transposed, 0)
            write(out, jnp.where(wa == 0, theirs, mine), transposed, width)


def swap_cores(value):
    return lax.ppermute(value, "wa", [(0, 1), (1, 0)])


def permute(cfg, value, bits):
    return lax.ppermute(value, "ctx", [(i, i ^ bits) for i in range(cfg.n)])


def sum_chunks(cfg, cur):
    bits = []
    size = cfg.n // 2
    while size >= 1:
        half = cur.shape[0] // 2
        got = permute(cfg, cur[half:], size)
        cur = (cur[:half].astype(F32) + got.astype(F32)).astype(BF)
        bits.append(size)
        size //= 2
    for size in reversed(bits):
        cur = jnp.concatenate([cur, permute(cfg, cur, size)], axis=0)
    return cur


def per_device(
    hidden_in, attn_gain, query_weight, key_weight, value_weight, query_gain, key_gain, out_weight,
    ffn_gain, gate_weight, up_weight, down_weight, query_adapt_in, query_adapt_out, key_adapt_in,
    key_adapt_out, value_adapt_in, value_adapt_out, out_adapt_in, out_adapt_out, gate_adapt_in,
    gate_adapt_out, up_adapt_in, up_adapt_out, down_adapt_in, down_adapt_out, document_extra,
    document_adapter, cotangent,
):
    head_dim = query_gain.shape[0]
    cfg = Cfg(
        tokens=hidden_in.shape[0],
        n_ctx=lax.axis_size("ctx"),
        heads_kv=key_weight.shape[1] // head_dim,
        groups=query_weight.shape[1] // key_weight.shape[1],
        head_dim=head_dim,
        docs=document_extra.shape[0],
        adapt_width=query_adapt_in.shape[1],
        width=hidden_in.shape[2],
        hidden=gate_weight.shape[1],
    )
    T, D, G, S, AW, n, lo = cfg.T, cfg.D, cfg.G, cfg.S, cfg.AW, cfg.n, cfg.lo
    gw = cfg.groups * head_dim
    QW, KW = query_weight.shape[1], key_weight.shape[1]
    ctx_index = lax.axis_index("ctx")
    meta = jnp.concatenate(
        [
            jnp.stack([ctx_index, lax.axis_index("wa")]).astype(jnp.int32),
            document_extra,
            document_adapter,
        ]
    )
    x = hidden_in.reshape(T, D)
    cot = cotangent.reshape(T, D)
    gain_a = attn_gain.reshape(1, D)
    gain_f = ffn_gain.reshape(1, D)
    qg = query_gain.reshape(1, head_dim)
    kg = key_gain.reshape(1, head_dim)

    token = jnp.arange(T, dtype=jnp.int32) * n + ctx_index
    lengths = document_extra + (DOC_MIN - 1)
    starts = jnp.cumsum(lengths) - lengths
    position = token - jnp.max(jnp.where(token[:, None] >= starts[None, :], starts[None, :], 0), axis=1)
    half = head_dim // 2
    lane = jnp.arange(2 * head_dim, dtype=jnp.int32)
    inverse = jnp.exp((lane % half).astype(F32) * (-2.0 * math.log(theta_base) / head_dim))
    angle = position.astype(F32)[:, None] * inverse[None, :]
    cos = jnp.cos(angle)
    sin = jnp.sin(angle) * jnp.where(lane % head_dim < half, -1.0, 1.0)[None, :]

    piece = ((T, gw), BF)
    pre = call(
        functools.partial(pre_kernel, cfg),
        [piece] * (2 * G) + [((T, QW), F32), ((T, KW), F32), ((3, T, S), BF), ((T, D), BF)],
        [
            meta, x, gain_a, query_weight, key_weight, value_weight, query_adapt_in, key_adapt_in,
            value_adapt_in, query_adapt_out, key_adapt_out, value_adapt_out, qg, kg, cos, sin,
        ],
        scratch=[pltpu.VMEM((G, T, gw), BF), pltpu.VMEM((G, T, gw), BF)],
        flops=2 * T * D * (QW + 2 * KW),
        bytes_accessed=2 * D * (QW + 2 * KW),
        name="pre",
    )
    kv_send, q_send = pre[:G], pre[G : 2 * G]
    qraw, kraw, sides, normed = pre[2 * G :]

    def to_heads(pieces):
        return [pieces[0]] + [permute(cfg, pieces[k], k * lo) for k in range(1, G)]

    def to_plane(value):
        return [value] + [permute(cfg, value, j) for j in range(1, lo)]

    kv = to_plane(jnp.stack(to_heads(kv_send)))
    q = to_heads(q_send)
    tiles = lambda rows: pltpu.VMEM((cfg.NT, rows, gw), BF)
    attn = call(
        functools.partial(attend_kernel, cfg),
        [piece] * G + [((G, T, gw), BF), ((G, T, gw), F32)],
        [meta] + q + kv,
        scratch=[tiles(cfg.KT), tiles(cfg.KT), tiles(cfg.QH)],
        flops=2 * T * G * T * n * 2 * gw,
        name="attend",
    )
    o_send, o_all, linv = attn[:G], attn[G], attn[G + 1]
    o = to_heads(o_send)
    (opart,) = call(
        functools.partial(out_kernel, cfg),
        [((T, D + AW), BF)],
        [meta] + o + [out_weight, out_adapt_in],
        scratch=[pltpu.VMEM((T, QW), BF)],
        flops=2 * T * D * QW,
        bytes_accessed=2 * D * QW,
        name="out_proj",
    )
    ffn = ffn_call(
        cfg, meta, x, opart, swap_cores(opart), out_adapt_out, gain_f, gate_weight, up_weight,
        down_weight, gate_adapt_out, up_adapt_out, gate_adapt_in, up_adapt_in, down_adapt_in,
        down_adapt_out, cot,
    )
    mixed, dfn, dpart, bgate, bup, adown, akeep, asend, oside = ffn
    mg = call(
        functools.partial(mixed_grad_kernel, cfg),
        [((T, D), F32), ((2, S, D // 2), BF)] + [piece] * G,
        [meta, mixed, dfn, swap_cores(dfn), cot, gain_f]
        + o
        + [out_weight, out_adapt_in, out_adapt_out, oside],
        scratch=[pltpu.VMEM((T, QW), BF), pltpu.VMEM((G, T, gw), BF), pltpu.VMEM((T, D), BF)],
        flops=2 * T * D * QW,
        bytes_accessed=2 * D * QW,
        name="mixed_grad",
    )
    grad_mixed, ograds, go_send = mg[0], mg[1], mg[2:]
    go_heads = to_heads(go_send)
    (go_all,) = call(
        functools.partial(scale_kernel, cfg),
        [((G, T, gw), BF)],
        [meta] + go_heads + [linv],
        bytes_accessed=8 * G * T * gw,
        name="scale",
    )
    q_plane = to_plane(jnp.stack(q))
    o_plane = to_plane(o_all)
    go_plane = to_plane(go_all)
    dq_send = call(
        functools.partial(grad_query_kernel, cfg),
        [piece] * G,
        [meta] + q + kv + [go_all, o_all],
        scratch=[tiles(cfg.KT), tiles(cfg.QH), tiles(cfg.QH), tiles(cfg.QH)],
        flops=2 * T * G * T * n * 3 * gw,
        name="grad_query",
    )
    dq = to_heads(dq_send)
    dkv_send = call(
        functools.partial(grad_key_kernel, cfg),
        [piece] * G,
        [meta, kv[0]] + q_plane + go_plane + o_plane,
        scratch=[tiles(cfg.QH), tiles(cfg.KT), tiles(cfg.KT), tiles(cfg.KT)]
        + [pltpu.VMEM((cfg.NT, 16, cfg.KT), F32)],
        flops=2 * T * G * T * n * 4 * gw,
        name="grad_key",
    )
    dkv = to_heads(dkv_send)

    out_rows, bdown = call(
        functools.partial(output_kernel, cfg),
        [((T, D), BF), ((S, D // 2), BF)],
        [meta, mixed, dpart, swap_cores(dpart), down_adapt_out, cot],
        name="output",
    )
    units_f = Units(cfg, [D // 2] * 4, [cfg.F] * 3 + [QW])
    qkv = call(
        functools.partial(qkv_grad_kernel, cfg),
        [((T, D), BF), ((S, QW + 2 * KW), BF), ((3 * S, D // 2), BF), ((3 * S, D // 2), BF)],
        [meta]
        + dq
        + dkv
        + [
            normed, qraw, kraw, sides, cos, sin, qg, kg, query_weight, key_weight, value_weight,
            query_adapt_in, key_adapt_in, value_adapt_in, query_adapt_out, key_adapt_out,
            value_adapt_out,
        ],
        scratch=[
            pltpu.VMEM((T, QW), BF),
            pltpu.VMEM((T, 2 * KW), BF),
            pltpu.VMEM((3 * S, D), F32),
        ],
        flops=2 * T * D * (QW + 2 * KW),
        bytes_accessed=2 * D * (QW + 2 * KW),
        name="qkv_grad",
    )
    dnormed, bqkv, akeep_q, asend_q = qkv
    (input_rows,) = call(
        functools.partial(input_grad_kernel, cfg),
        [((T, D), BF)],
        [meta, x, gain_a, grad_mixed, dnormed, swap_cores(dnormed)],
        name="input_grad",
    )

    def reduce_and_expand(units, pack_in, pack_kern, plan, outs, tag):
        (buffer,) = call(pack_kern, [((n, units.u, 16, 128), BF)], [meta] + pack_in, name="pack_" + tag)
        total = sum_chunks(cfg, buffer)
        theirs = swap_cores(total[:, : units.us])
        return call(
            functools.partial(expand_kernel, cfg, units, plan),
            outs,
            [meta, total, theirs],
            name="expand_" + tag,
        )

    grads_f = reduce_and_expand(
        units_f,
        [akeep, swap_cores(asend), bdown, ograds, bgate, bup, adown],
        functools.partial(pack_ffn_kernel, cfg, units_f),
        [(0, 0, True), (0, 1, True), (0, 2, False), (0, 3, False)]
        + [(1, 0, False), (1, 1, False), (1, 2, True), (1, 3, True)],
        [((D, AW), F32), ((D, AW), F32), ((AW, D), F32), ((AW, D), F32)]
        + [((AW, cfg.F), F32), ((AW, cfg.F), F32), ((cfg.F, AW), F32), ((QW, AW), F32)],
        "ffn",
    )
    gate_in, up_in, down_out, out_out, gate_out, up_out, down_in, out_in = grads_f
    units_q = Units(cfg, [D // 2] * 3, [QW, KW, KW])
    grads_q = reduce_and_expand(
        units_q,
        [akeep_q, swap_cores(asend_q), bqkv],
        functools.partial(pack_qkv_kernel, cfg, units_q, QW, KW),
        [(0, 0, True), (0, 1, True), (0, 2, True), (1, 0, False), (1, 1, False), (1, 2, False)],
        [((D, AW), F32)] * 3 + [((AW, QW), F32), ((AW, KW), F32), ((AW, KW), F32)],
        "qkv",
    )
    query_in, key_in, value_in, query_out, key_out, value_out = grads_q
    return (
        out_rows.reshape(T, 1, D),
        input_rows.reshape(T, 1, D),
        query_in,
        query_out,
        key_in,
        key_out,
        value_in,
        value_out,
        out_in,
        out_out,
        gate_in,
        gate_out,
        up_in,
        up_out,
        down_in,
        down_out,
    )


def solution(mesh):
    return jax.shard_map(
        per_device,
        mesh=mesh,
        in_specs=(
            P(None, "ctx", None), P(), P(None, "wa"), P(None, "wa"), P(None, "wa"), P(), P(),
            P("wa", None), P(), P(None, "wa"), P(None, "wa"), P("wa", None), P(), P(None, "wa"),
            P(), P(None, "wa"), P(), P(None, "wa"), P("wa", None), P(), P(), P(None, "wa"), P(),
            P(None, "wa"), P("wa", None), P(), P(), P(), P(None, "ctx", None),
        ),
        out_specs=(
            P(None, "ctx", None), P(None, "ctx", None), P(), P(None, "wa"), P(), P(None, "wa"), P(),
            P(None, "wa"), P("wa", None), P(), P(), P(None, "wa"), P(), P(None, "wa"),
            P("wa", None), P(),
        ),
        check_vma=False,
    )
```

time: 968 us -> 261 us (0.27)
  waiting for transfers between devices: 561 us -> 79.9 us
  matrix products: 207 us -> 0 us
  Pallas kernels: 0 us -> 99.5 us
  local copies, waits for them, and re-layouts: 108 us -> 9.83 us
  starting transfers between devices: 0.91 us -> 62.5 us
  other arithmetic: 64.9 us -> 5.59 us
  between operations: 16.1 us -> 1.25 us
    psum x5 -> x0, waiting for transfers between devices: 383 us -> none  [the longest x1 205 us: per_device(): lax.psum((query_out_grad, key_out_grad, value_out_grad, out_in_grad, out_...]
    dot_general x70 -> x0, matrix products: 207 us -> none  [the longest x4 32.7 us: score_grads(): jnp.einsum('hqd,khd->hqk', query_block, key_heads_blk, preferred_element_...]
    pallas_call x0 -> x15, Pallas kernels: none -> 99.5 us  [the longest x14 80.6 us: call(): pl.pallas_call(kernel, out_shape=[jax.ShapeDtypeStruct(s, d) for s, d in...]
    reduce_scatter x1 -> x0, waiting for transfers between devices: 94.5 us -> none  [per_device(): lax.psum_scatter(lax.map(one_block, offsets).reshape(tok_rows * lax.axis_...]
    all_gather x2 -> x0, waiting for transfers between devices: 82.8 us -> none  [the longest x1 55.5 us: per_device(): lax.all_gather(key_flat.reshape(1, tok_rows, kv_width), 'ctx', axis=0, ti...]
    ppermute x0 -> x54, waiting for transfers between devices: none -> 79.9 us  [the longest x46 75.1 us: permute(): return lax.ppermute(value, 'ctx', [(i, i ^ bits) for i in range(cfg.n)])]
    ppermute x0 -> x54, starting transfers between devices: none -> 62.5 us  [the longest x46 61.1 us: permute(): return lax.ppermute(value, 'ctx', [(i, i ^ bits) for i in range(cfg.n)])]
    dynamic_slice x20 -> x0, local copies, waits for them, and re-layouts: 26.9 us -> none  [the longest x14 18.7 us: grouped(): result, unused = lax.scan(advance, carry_in, (stacked, offsets))]
  transfers between devices with their start and end apart: 8 -> 54, of which waited for: 8 -> 27; matrix products, arithmetic and copies ran while one was open for 16% -> 1% of each run, Pallas kernels for 0% -> 22%
where the time goes in v1:
time: 261 us; the launch traced here: 259 us
  Pallas kernels  99.5 us (38%)
  waiting for transfers between devices  79.9 us (31%)
  starting transfers between devices  62.5 us (24%)
  local copies, waits for them, and re-layouts  9.83 us (4%)
  other arithmetic  5.59 us (2%)
    pallas_call x14, Pallas kernels, call(): pl.pallas_call(kernel, out_shape=[jax.ShapeDtypeStruct(s, d) for s, d in...  80.6 us
    ppermute x46, waiting for transfers between devices, permute(): return lax.ppermute(value, 'ctx', [(i, i ^ bits) for i in range(cfg.n)])  75.1 us
    ppermute x46, starting transfers between devices, permute(): return lax.ppermute(value, 'ctx', [(i, i ^ bits) for i in range(cfg.n)])  61.1 us
    pallas_call x1, Pallas kernels, ffn_call(): pl.pallas_call(functools.partial(ffn_kernel, cfg, steps), grid=(steps,),...  19 us
    unnamed x98, local copies, waits for them, and re-layouts  7.39 us
  transfers between devices with their start and end apart: 54, of which 27 were waited for; matrix products, arithmetic and copies ran while one was open for 1% of the time, Pallas kernels for 22%

profile of v1, /device:TPU:0, one launch (start us, length us, event | category | flops | bytes accessed | tf_op | source)
XLA Modules:
  0.0 258.7 jit_solution(4457286690659307407)
XLA Ops:
  4.8 5.6 %pre.1 = (bf16[256,128]{1,0:T(8,128)(2,1)}, bf16[256,128]{1,0:T(8,128)(2,1)}, bf16[256,128]{1,0:T(8,128)(2,1)}, bf16[256,128]{1,0:T(8,128)(2,1)}, bf16[256,128]{...) custom-call(s32[10]{0:T(128)} %pad_add_fusion.meta, ...), custom_call_target="tpu_custom_call" | custom-call | flops 536870912 | bytes 2097152 | tf_op jit(solution)/shard_map/pre/pallas_call | solution.py:132
  10.4 5.1 %collective-permute-start.5 = (bf16[256,128]{1,0:T(8,128)(2,1)}, bf16[256,128]{1,0:T(8,128)(2,1)S(1)}, u32[]{:S(2)}, u32[]{:S(2)}) collective-permute-start(bf16[256,128]{1,0:T(8,128)(2,1)} %get-tuple-element.84), channel_id=1, source_target_pairs={{0,24},{2,26},{4,28},{6,30},{8,16},{10,18},{12,20},{14,22},{16,8},... | collective-permute-start | bytes 196616 | tf_op jit(solution)/shard_map/ppermute | solution.py:772
  16.1 2.2 collective-permute-done.5
  18.3 3.0 %collective-permute-done.4 = bf16[256,128]{1,0:T(8,128)(2,1)S(1)} collective-permute-done((bf16[256,128]{1,0:T(8,128)(2,1)}, bf16[256,128]{1,0:T(8,128)(2,1)S(1)}, u32[]{:S(2)}, u32[]{:S(2)}) %collective-permute-start.4) | collective-permute-done | bytes 65568 | tf_op jit(solution)/shard_map/ppermute | solution.py:772
  26.8 2.2 collective-permute-start.1
  30.2 2.7 %collective-permute-start.2 = (bf16[256,128]{1,0:T(8,128)(2,1)}, bf16[256,128]{1,0:T(8,128)(2,1)S(1)}, u32[]{:S(2)}, u32[]{:S(2)}) collective-permute-start(bf16[256,128]{1,0:T(8,128)(2,1)} %get-tuple-element.80), channel_id=1, source_target_pairs={{0,24},{2,26},{4,28},{6,30},{8,16},{10,18},{12,20},{14,22},{16,8},... | collective-permute-start | bytes 196616 | tf_op jit(solution)/shard_map/ppermute | solution.py:772
  33.6 2.9 %collective-permute-done.2.refs_3_ = bf16[256,128]{1,0:T(8,128)(2,1)S(1)} collective-permute-done((bf16[256,128]{1,0:T(8,128)(2,1)}, bf16[256,128]{1,0:T(8,128)(2,1)S(1)}, u32[]{:S(2)}, u32[]{:S(2)}) %collective-permute-start.2) | collective-permute-done | bytes 65568 | tf_op jit(solution)/shard_map/ppermute | solution.py:772
  38.0 11.9 %attend.1 = (bf16[256,128]{1,0:T(8,128)(2,1)}, bf16[256,128]{1,0:T(8,128)(2,1)}, bf16[256,128]{1,0:T(8,128)(2,1)}, bf16[256,128]{1,0:T(8,128)(2,1)}, bf16[4,256,...) custom-call(s32[10]{0:T(128)} %pad_add_fusion.meta, bf16[256,128]{1,0:T(8,128)(2,1)} %get-tuple-element.77.refs_0_, ...), custom_call_target="tpu_custom_call" | custom-call | flops 2147483648 | tf_op jit(solution)/shard_map/attend/pallas_call | solution.py:132
  49.8 2.7 %collective-permute-start.10 = (bf16[256,128]{1,0:T(8,128)(2,1)}, bf16[256,128]{1,0:T(8,128)(2,1)S(1)}, u32[]{:S(2)}, u32[]{:S(2)}) collective-permute-start(bf16[256,128]{1,0:T(8,128)(2,1)} %get-tuple-element.87), channel_id=1, source_target_pairs={{0,16},{2,18},{4,20},{6,22},{8,24},{10,26},{12,28},{14,30},{16,0},... | collective-permute-start | bytes 196616 | tf_op jit(solution)/shard_map/ppermute | solution.py:772
  55.9 2.9 %collective-permute-done.11.refs_3_.refs_8_ = bf16[256,128]{1,0:T(8,128)(2,1)S(1)} collective-permute-done((bf16[256,128]{1,0:T(8,128)(2,1)}, bf16[256,128]{1,0:T(8,128)(2,1)S(1)}, u32[]{:S(2)}, u32[]{:S(2)}) %collective-permute-start.11) | collective-permute-done | bytes 65568 | tf_op jit(solution)/shard_map/ppermute | solution.py:772
  59.5 2.7 %out_proj.1.own = bf16[256,1152]{1,0:T(8,128)(2,1)} custom-call(s32[10]{0:T(128)} %pad_add_fusion.meta, bf16[256,128]{1,0:T(8,128)(2,1)} %get-tuple-element.85.refs_0_.refs_5_, bf16[256,128]{1,0:T(8,128)(2,1)} %copy-done.7, bf16[256,128]{1,0:T(8,128)(2,1)} %copy-done.8, bf16[256,128]{1,0:T(8,128)(2,1)} %copy-done.9, bf16[512,1024]{1,0:T(8,128)(2,1)} %refs_9_.1, ...), custom_call_target="tpu_custom_call" | custom-call | flops 268435456 | bytes 1048576 | tf_op jit(solution)/shard_map/out_proj/pallas_call | solution.py:132
  62.2 2.2 collective-permute-done.12.other
  65.2 19.0 %ffn.1 = (f32[256,1024]{1,0:T(8,128)}, bf16[256,1024]{1,0:T(8,128)(2,1)}, bf16[256,1152]{1,0:T(8,128)(2,1)}, bf16[64,2304]{1,0:T(8,128)(2,1)}, bf16[64,2304]{1,0...) custom-call(s32[10]{0:T(128)} %pad_add_fusion.meta, ...), custom_call_target="tpu_custom_call" | custom-call | flops 7247757312 | bytes 14155776 | tf_op jit(solution)/shard_map/ffn/pallas_call | solution.py:538
  87.2 4.6 %mixed_grad.1 = (f32[256,1024]{1,0:T(8,128)}, bf16[2,64,512]{2,1,0:T(8,128)(2,1)}, bf16[256,128]{1,0:T(8,128)(2,1)}, bf16[256,128]{1,0:T(8,128)(2,1)}, bf16[256,...) custom-call(s32[10]{0:T(128)} %pad_add_fusion.meta, f32[256,1024]{1,0:T(8,128)} %get-tuple-element.89.mixed.refs_0_, ...), custom_call_target="tpu_custom_call" | custom-call | flops 268435456 | bytes 1048576 | tf_op jit(solution)/shard_map/mixed_grad/pallas_call | solution.py:132
  91.8 2.2 collective-permute-start.16
  94.0 2.2 collective-permute-start.17
  103.7 3.0 %output.1 = (bf16[256,1024]{1,0:T(8,128)(2,1)}, bf16[64,512]{1,0:T(8,128)(2,1)}) custom-call(s32[10]{0:T(128)} %pad_add_fusion.meta, f32[256,1024]{1,0:T(8,128)} %get-tuple-element.89.mixed.refs_0_, bf16[256,1152]{1,0:T(8,128)(2,1)} %get-tuple-element.90.own, bf16[256,1152]{1,0:T(8,128)(2,1)} %copy-done.4, bf16[128,1024]{1,0:T(8,128)(2,1)} %bd.3, ...), custom_call_target="tpu_custom_call" | custom-call | tf_op jit(solution)/shard_map/output/pallas_call | solution.py:132
  106.7 2.6 pack_ffn.1
  116.9 2.5 collective-permute-start.26
  119.4 4.6 %collective-permute-done.28.refs_11_ = bf16[4,256,128]{2,1,0:T(8,128)(2,1)S(1)} collective-permute-done((bf16[4,256,128]{2,1,0:T(8,128)(2,1)S(1)}, bf16[4,256,128]{2,1,0:T(8,128)(2,1)S(1)}, u32[]{:S(2)}, u32[]{:S(2)}) %collective-permute-start.28) | collective-permute-done | bytes 262176 | tf_op jit(solution)/shard_map/ppermute | solution.py:772
  124.0 13.5 %grad_query.1 = (bf16[256,128]{1,0:T(8,128)(2,1)}, bf16[256,128]{1,0:T(8,128)(2,1)}, bf16[256,128]{1,0:T(8,128)(2,1)}, bf16[256,128]{1,0:T(8,128)(2,1)}) custom-call(s32[10]{0:T(128)} %pad_add_fusion.meta, bf16[256,128]{1,0:T(8,128)(2,1)} %get-tuple-element.77.refs_0_, bf16[256,128]{1,0:T(8,128)(2,1)} %copy-done.23, bf16[256,128]{1,0:T(8,128)(2,1)} %copy-done.25, ...), custom_call_target="tpu_custom_call" | custom-call | flops 3221225472 | tf_op jit(solution)/shard_map/grad_query/pallas_call | solution.py:132
  142.7 16.1 %grad_key.1 = (bf16[256,128]{1,0:T(8,128)(2,1)}, bf16[256,128]{1,0:T(8,128)(2,1)}, bf16[256,128]{1,0:T(8,128)(2,1)}, bf16[256,128]{1,0:T(8,128)(2,1)}) custom-call(s32[10]{0:T(128)} %pad_add_fusion.meta, bf16[4,256,128]{2,1,0:T(8,128)(2,1)} %copy-done.10, bf16[4,256,128]{2,1,0:T(8,128)(2,1)} %copy-done.11, bf16[4,256,128]{2,1,0:T(8,128)(2,1)} %copy-done.37, ...), custom_call_target="tpu_custom_call" | custom-call | flops 4294967296 | tf_op jit(solution)/shard_map/grad_key/pallas_call | solution.py:132
  163.7 2.3 collective-permute-done.31.refs_6_
  168.7 6.7 %qkv_grad.1 = (bf16[256,1024]{1,0:T(8,128)(2,1)}, bf16[64,1024]{1,0:T(8,128)(2,1)}, bf16[192,512]{1,0:T(8,128)(2,1)}, bf16[192,512]{1,0:T(8,128)(2,1)}) custom-call(s32[10]{0:T(128)} %pad_add_fusion.meta, bf16[256,128]{1,0:T(8,128)(2,1)} %get-tuple-element.101.refs_0_, bf16[256,128]{1,0:T(8,128)(2,1)} %copy-done.16, bf16[256,128]{1,0:T(8,128)(2,1)} %copy-done.17, ...), custom_call_target="tpu_custom_call" | custom-call | flops 536870912 | bytes 2097152 | tf_op jit(solution)/shard_map/qkv_grad/pallas_call | solution.py:132
  183.1 7.1 %collective-permute-done.35 = bf16[8,5,16,128]{3,2,1,0:T(8,128)(2,1)S(1)} collective-permute-done((bf16[8,5,16,128]{3,2,1,0:T(8,128)(2,1)S(1)}, bf16[8,5,16,128]{3,2,1,0:T(8,128)(2,1)S(1)}, u32[]{:S(2)}, u32[]{:S(2)}) %collective-permute-start.35) | collective-permute-done | bytes 163872 | tf_op jit(solution)/shard_map/ppermute | solution.py:772
  190.7 4.1 %collective-permute-done.36 = bf16[4,5,16,128]{3,2,1,0:T(8,128)(2,1)S(1)} collective-permute-done((bf16[4,5,16,128]{3,2,1,0:T(8,128)(2,1)S(1)}, bf16[4,5,16,128]{3,2,1,0:T(8,128)(2,1)S(1)}, u32[]{:S(2)}, u32[]{:S(2)}) %collective-permute-start.36) | collective-permute-done | bytes 81952 | tf_op jit(solution)/shard_map/ppermute | solution.py:772
  203.0 3.5 %collective-permute-done.50 = bf16[2,19,16,128]{3,2,1,0:T(8,128)(2,1)S(1)} collective-permute-done((bf16[2,19,16,128]{3,2,1,0:T(8,128)(2,1)S(1)}, bf16[2,19,16,128]{3,2,1,0:T(8,128)(2,1)S(1)}, u32[]{:S(2)}, u32[]{:S(2)}) %collective-permute-start.50) | collective-permute-done | bytes 155680 | tf_op jit(solution)/shard_map/ppermute | solution.py:772
  215.0 3.3 %collective-permute-start.52 = (bf16[8,19,16,128]{3,2,1,0:T(8,128)(2,1)S(1)}, bf16[8,19,16,128]{3,2,1,0:T(8,128)(2,1)S(1)}, u32[]{:S(2)}, u32[]{:S(2)}) collective-permute-start(bf16[8,19,16,128]{3,2,1,0:T(8,128)(2,1)S(1)} %pad_maximum_fusion), channel_id=1, source_target_pairs={{0,16},{2,18},{4,20},{6,22},{8,24},{10,26},{12,28},{14,30},{16,0},... | collective-permute-start | bytes 1867784 | tf_op jit(solution)/shard_map/ppermute | solution.py:772
  220.2 24.2 %collective-permute-done.52 = bf16[8,19,16,128]{3,2,1,0:T(8,128)(2,1)S(1)} collective-permute-done((bf16[8,19,16,128]{3,2,1,0:T(8,128)(2,1)S(1)}, bf16[8,19,16,128]{3,2,1,0:T(8,128)(2,1)S(1)}, u32[]{:S(2)}, u32[]{:S(2)}) %collective-permute-start.52) | collective-permute-done | bytes 622624 | tf_op jit(solution)/shard_map/ppermute | solution.py:772
  247.1 3.0 %input_grad.1 = bf16[256,1024]{1,0:T(8,128)(2,1)} custom-call(s32[10]{0:T(128)} %pad_add_fusion.meta, bf16[256,1024]{1,0:T(8,128)(2,1)} %bitcast.24, f32[1,1024]{1,0:T(1,128)} %bitcast.38, f32[256,1024]{1,0:T(8,128)} %get-tuple-element.94.gm, bf16[256,1024]{1,0:T(8,128)(2,1)} %get-tuple-element.113.own, bf16[256,1024]{1,0:T(8,128)(2,1)} %copy-done.5), custom_call_target="tpu_custom_call" | custom-call | tf_op jit(solution)/shard_map/input_grad/pallas_call | solution.py:132
  250.7 2.8 %expand_qkv.1 = (f32[1024,128]{1,0:T(8,128)}, f32[1024,128]{1,0:T(8,128)}, f32[1024,128]{1,0:T(8,128)}, f32[128,512]{1,0:T(8,128)}, f32[128,256]{1,0:T(8,128)}, /*index=5*/f32[128,256]{1,0:T(8,128)}) custom-call(s32[10]{0:T(128)} %pad_add_fusion.meta, bf16[16,5,16,128]{3,2,1,0:T(8,128)(2,1)} %copy-done.3, bf16[16,3,16,128]{3,2,1,0:T(8,128)(2,1)} %copy-done.13), custom_call_target="tpu_custom_call" | custom-call | tf_op jit(solution)/shard_map/expand_qkv/pallas_call | solution.py:132
  254.2 4.5 %expand_ffn.1 = (f32[1024,128]{1,0:T(8,128)}, f32[1024,128]{1,0:T(8,128)}, f32[128,1024]{1,0:T(8,128)}, f32[128,1024]{1,0:T(8,128)}, f32[128,2304]{1,0:T(8,128)}...) custom-call(s32[10]{0:T(128)} %pad_add_fusion.meta, bf16[16,19,16,128]{3,2,1,0:T(8,128)(2,1)} %copy-done.1, ...), custom_call_target="tpu_custom_call" | custom-call | tf_op jit(solution)/shard_map/expand_ffn/pallas_call | solution.py:132
  (226 shorter events, 79.8 us)
Async XLA Ops:
  10.4 7.9 %collective-permute-start.5 = (bf16[256,128]{1,0:T(8,128)(2,1)}, bf16[256,128]{1,0:T(8,128)(2,1)S(1)}, u32[]{:S(2)}, u32[]{:S(2)}) collective-permute-start(bf16[256,128]{1,0:T(8,128)(2,1)} %get-tuple-element.84), channel_id=1, source_target_pairs={{0,24},{2,26},{4,28},{6,30},{8,16},{10,18},{12,20},{14,22},{16,8},... | collective-permute-start | bytes 196616 | tf_op jit(solution)/shard_map/ppermute | solution.py:772
  22.2 14.3 %collective-permute-start.6 = (bf16[4,256,128]{2,1,0:T(8,128)(2,1)S(1)}, bf16[4,256,128]{2,1,0:T(8,128)(2,1)S(1)}, u32[]{:S(2)}, u32[]{:S(2)}) collective-permute-start(bf16[4,256,128]{2,1,0:T(8,128)(2,1)S(1)} %pad_maximum_fusion.2.refs_4_.refs_0_), channel_id=1, source_target_pairs={{0,2},{2,0},{4,6},{6,4},{8,10},{10,8},{12,14},{14,12},{16,18},{18,... | collective-permute-start | bytes 786440 | tf_op jit(solution)/shard_map/ppermute | solution.py:772
  23.8 13.4 %collective-permute-start.7 = (bf16[4,256,128]{2,1,0:T(8,128)(2,1)S(1)}, bf16[4,256,128]{2,1,0:T(8,128)(2,1)S(1)}, u32[]{:S(2)}, u32[]{:S(2)}) collective-permute-start(bf16[4,256,128]{2,1,0:T(8,128)(2,1)S(1)} %pad_maximum_fusion.2.refs_4_.refs_0_), channel_id=1, source_target_pairs={{0,4},{2,6},{4,0},{6,2},{8,12},{10,14},{12,8},{14,10},{16,20},{18,... | collective-permute-start | bytes 786440 | tf_op jit(solution)/shard_map/ppermute | solution.py:772
  25.3 11.9 %collective-permute-start.8 = (bf16[4,256,128]{2,1,0:T(8,128)(2,1)S(1)}, bf16[4,256,128]{2,1,0:T(8,128)(2,1)S(1)}, u32[]{:S(2)}, u32[]{:S(2)}) collective-permute-start(bf16[4,256,128]{2,1,0:T(8,128)(2,1)S(1)} %pad_maximum_fusion.2.refs_4_.refs_0_), channel_id=1, source_target_pairs={{0,6},{2,4},{4,2},{6,0},{8,14},{10,12},{12,10},{14,8},{16,22},{18,... | collective-permute-start | bytes 786440 | tf_op jit(solution)/shard_map/ppermute | solution.py:772
  26.8 6.8 %collective-permute-start.1 = (bf16[256,128]{1,0:T(8,128)(2,1)}, bf16[256,128]{1,0:T(8,128)(2,1)S(1)}, u32[]{:S(2)}, u32[]{:S(2)}) collective-permute-start(bf16[256,128]{1,0:T(8,128)(2,1)} %get-tuple-element.79), channel_id=1, source_target_pairs={{0,16},{2,18},{4,20},{6,22},{8,24},{10,26},{12,28},{14,30},{16,0},... | collective-permute-start | bytes 196616 | tf_op jit(solution)/shard_map/ppermute | solution.py:772
  84.4 13.5 %collective-permute-start.13 = (bf16[256,1152]{1,0:T(8,128)(2,1)}, bf16[256,1152]{1,0:T(8,128)(2,1)S(1)}, u32[]{:S(2)}, u32[]{:S(2)}) collective-permute-start(bf16[256,1152]{1,0:T(8,128)(2,1)} %get-tuple-element.90.own), channel_id=1, source_target_pairs={{0,1},{1,0},{2,3},{3,2},{4,5},{5,4},{6,7},{7,6},{8,9},{9,8},{10,11... | collective-permute-start | bytes 1769480 | tf_op jit(solution)/shard_map/ppermute | solution.py:768
  84.8 11.5 %collective-permute-start.44 = (bf16[128,512]{1,0:T(8,128)(2,1)}, bf16[128,512]{1,0:T(8,128)(2,1)S(1)}, u32[]{:S(2)}, u32[]{:S(2)}) collective-permute-start(bf16[128,512]{1,0:T(8,128)(2,1)} %get-tuple-element.124), channel_id=1, source_target_pairs={{0,1},{1,0},{2,3},{3,2},{4,5},{5,4},{6,7},{7,6},{8,9},{9,8},{10,11... | collective-permute-start | bytes 393224 | tf_op jit(solution)/shard_map/ppermute | solution.py:768
  91.8 7.6 %collective-permute-start.15 = (bf16[256,128]{1,0:T(8,128)(2,1)}, bf16[256,128]{1,0:T(8,128)(2,1)S(1)}, u32[]{:S(2)}, u32[]{:S(2)}) collective-permute-start(bf16[256,128]{1,0:T(8,128)(2,1)} %get-tuple-element.96), channel_id=1, source_target_pairs={{0,8},{2,10},{4,12},{6,14},{8,0},{10,2},{12,4},{14,6},{16,24},{18,... | collective-permute-start | bytes 196616 | tf_op jit(solution)/shard_map/ppermute | solution.py:772
  91.8 8.8 %collective-permute-start.16 = (bf16[256,128]{1,0:T(8,128)(2,1)}, bf16[256,128]{1,0:T(8,128)(2,1)S(1)}, u32[]{:S(2)}, u32[]{:S(2)}) collective-permute-start(bf16[256,128]{1,0:T(8,128)(2,1)} %get-tuple-element.97), channel_id=1, source_target_pairs={{0,16},{2,18},{4,20},{6,22},{8,24},{10,26},{12,28},{14,30},{16,0},... | collective-permute-start | bytes 196616 | tf_op jit(solution)/shard_map/ppermute | solution.py:772
  94.0 8.1 %collective-permute-start.17 = (bf16[256,128]{1,0:T(8,128)(2,1)}, bf16[256,128]{1,0:T(8,128)(2,1)S(1)}, u32[]{:S(2)}, u32[]{:S(2)}) collective-permute-start(bf16[256,128]{1,0:T(8,128)(2,1)} %get-tuple-element.98), channel_id=1, source_target_pairs={{0,24},{2,26},{4,28},{6,30},{8,16},{10,18},{12,20},{14,22},{16,8},... | collective-permute-start | bytes 196616 | tf_op jit(solution)/shard_map/ppermute | solution.py:772
  96.3 16.1 %collective-permute-start.21 = (bf16[4,256,128]{2,1,0:T(8,128)(2,1)S(1)}, bf16[4,256,128]{2,1,0:T(8,128)(2,1)S(1)}, u32[]{:S(2)}, u32[]{:S(2)}) collective-permute-start(bf16[4,256,128]{2,1,0:T(8,128)(2,1)S(1)} %pad_maximum_fusion.3.refs_1_), channel_id=1, source_target_pairs={{0,2},{2,0},{4,6},{6,4},{8,10},{10,8},{12,14},{14,12},{16,18},{18,... | collective-permute-start | bytes 786440 | tf_op jit(solution)/shard_map/ppermute | solution.py:772
  97.9 15.1 %collective-permute-start.22 = (bf16[4,256,128]{2,1,0:T(8,128)(2,1)S(1)}, bf16[4,256,128]{2,1,0:T(8,128)(2,1)S(1)}, u32[]{:S(2)}, u32[]{:S(2)}) collective-permute-start(bf16[4,256,128]{2,1,0:T(8,128)(2,1)S(1)} %pad_maximum_fusion.3.refs_1_), channel_id=1, source_target_pairs={{0,4},{2,6},{4,0},{6,2},{8,12},{10,14},{12,8},{14,10},{16,20},{18,... | collective-permute-start | bytes 786440 | tf_op jit(solution)/shard_map/ppermute | solution.py:772
  99.4 15.1 %collective-permute-start.23 = (bf16[4,256,128]{2,1,0:T(8,128)(2,1)S(1)}, bf16[4,256,128]{2,1,0:T(8,128)(2,1)S(1)}, u32[]{:S(2)}, u32[]{:S(2)}) collective-permute-start(bf16[4,256,128]{2,1,0:T(8,128)(2,1)S(1)} %pad_maximum_fusion.3.refs_1_), channel_id=1, source_target_pairs={{0,6},{2,4},{4,2},{6,0},{8,14},{10,12},{12,10},{14,8},{16,22},{18,... | collective-permute-start | bytes 786440 | tf_op jit(solution)/shard_map/ppermute | solution.py:772
  100.7 16.2 %collective-permute-start.27 = (bf16[4,256,128]{2,1,0:T(8,128)(2,1)S(1)}, bf16[4,256,128]{2,1,0:T(8,128)(2,1)S(1)}, u32[]{:S(2)}, u32[]{:S(2)}) collective-permute-start(bf16[4,256,128]{2,1,0:T(8,128)(2,1)S(1)} %copy-done.36), channel_id=1, source_target_pairs={{0,2},{2,0},{4,6},{6,4},{8,10},{10,8},{12,14},{14,12},{16,18},{18,... | collective-permute-start | bytes 786440 | tf_op jit(solution)/shard_map/ppermute | solution.py:772
  102.2 21.8 %collective-permute-start.28 = (bf16[4,256,128]{2,1,0:T(8,128)(2,1)S(1)}, bf16[4,256,128]{2,1,0:T(8,128)(2,1)S(1)}, u32[]{:S(2)}, u32[]{:S(2)}) collective-permute-start(bf16[4,256,128]{2,1,0:T(8,128)(2,1)S(1)} %copy-done.36), channel_id=1, source_target_pairs={{0,4},{2,6},{4,0},{6,2},{8,12},{10,14},{12,8},{14,10},{16,20},{18,... | collective-permute-start | bytes 786440 | tf_op jit(solution)/shard_map/ppermute | solution.py:772
  112.4 25.0 %collective-permute-start.29 = (bf16[4,256,128]{2,1,0:T(8,128)(2,1)S(1)}, bf16[4,256,128]{2,1,0:T(8,128)(2,1)S(1)}, u32[]{:S(2)}, u32[]{:S(2)}) collective-permute-start(bf16[4,256,128]{2,1,0:T(8,128)(2,1)S(1)} %copy-done.36), channel_id=1, source_target_pairs={{0,6},{2,4},{4,2},{6,0},{8,14},{10,12},{12,10},{14,8},{16,22},{18,... | collective-permute-start | bytes 786440 | tf_op jit(solution)/shard_map/ppermute | solution.py:772
  113.0 26.5 %collective-permute-start.24 = (bf16[4,256,128]{2,1,0:T(8,128)(2,1)}, bf16[4,256,128]{2,1,0:T(8,128)(2,1)S(1)}, u32[]{:S(2)}, u32[]{:S(2)}) collective-permute-start(bf16[4,256,128]{2,1,0:T(8,128)(2,1)} %scale.1.refs_8_.refs_5_), channel_id=1, source_target_pairs={{0,2},{2,0},{4,6},{6,4},{8,10},{10,8},{12,14},{14,12},{16,18},{18,... | collective-permute-start | bytes 786440 | tf_op jit(solution)/shard_map/ppermute | solution.py:772
  114.5 26.0 %collective-permute-start.25 = (bf16[4,256,128]{2,1,0:T(8,128)(2,1)}, bf16[4,256,128]{2,1,0:T(8,128)(2,1)S(1)}, u32[]{:S(2)}, u32[]{:S(2)}) collective-permute-start(bf16[4,256,128]{2,1,0:T(8,128)(2,1)} %scale.1.refs_8_.refs_5_), channel_id=1, source_target_pairs={{0,4},{2,6},{4,0},{6,2},{8,12},{10,14},{12,8},{14,10},{16,20},{18,... | collective-permute-start | bytes 786440 | tf_op jit(solution)/shard_map/ppermute | solution.py:772
  116.9 25.1 %collective-permute-start.26 = (bf16[4,256,128]{2,1,0:T(8,128)(2,1)}, bf16[4,256,128]{2,1,0:T(8,128)(2,1)S(1)}, u32[]{:S(2)}, u32[]{:S(2)}) collective-permute-start(bf16[4,256,128]{2,1,0:T(8,128)(2,1)} %scale.1.refs_8_.refs_5_), channel_id=1, source_target_pairs={{0,6},{2,4},{4,2},{6,0},{8,14},{10,12},{12,10},{14,8},{16,22},{18,... | collective-permute-start | bytes 786440 | tf_op jit(solution)/shard_map/ppermute | solution.py:772
  124.0 37.7 %collective-permute-start.45 = (bf16[8,19,16,128]{3,2,1,0:T(8,128)(2,1)S(1)}, bf16[8,19,16,128]{3,2,1,0:T(8,128)(2,1)S(1)}, u32[]{:S(2)}, u32[]{:S(2)}) collective-permute-start(bf16[8,19,16,128]{3,2,1,0:T(8,128)(2,1)S(1)} %slice.82), channel_id=1, source_target_pairs={{0,16},{2,18},{4,20},{6,22},{8,24},{10,26},{12,28},{14,30},{16,0},... | collective-permute-start | bytes 1867784 | tf_op jit(solution)/shard_map/ppermute | solution.py:772
  137.5 22.4 %collective-permute-start.18 = (bf16[256,128]{1,0:T(8,128)(2,1)}, bf16[256,128]{1,0:T(8,128)(2,1)S(1)}, u32[]{:S(2)}, u32[]{:S(2)}) collective-permute-start(bf16[256,128]{1,0:T(8,128)(2,1)} %get-tuple-element.102), channel_id=1, source_target_pairs={{0,8},{2,10},{4,12},{6,14},{8,0},{10,2},{12,4},{14,6},{16,24},{18,... | collective-permute-start | bytes 196616 | tf_op jit(solution)/shard_map/ppermute | solution.py:772
  139.4 24.0 %collective-permute-start.19 = (bf16[256,128]{1,0:T(8,128)(2,1)}, bf16[256,128]{1,0:T(8,128)(2,1)S(1)}, u32[]{:S(2)}, u32[]{:S(2)}) collective-permute-start(bf16[256,128]{1,0:T(8,128)(2,1)} %get-tuple-element.103), channel_id=1, source_target_pairs={{0,16},{2,18},{4,20},{6,22},{8,24},{10,26},{12,28},{14,30},{16,0},... | collective-permute-start | bytes 196616 | tf_op jit(solution)/shard_map/ppermute | solution.py:772
  140.5 23.2 %collective-permute-start.20 = (bf16[256,128]{1,0:T(8,128)(2,1)}, bf16[256,128]{1,0:T(8,128)(2,1)S(1)}, u32[]{:S(2)}, u32[]{:S(2)}) collective-permute-start(bf16[256,128]{1,0:T(8,128)(2,1)} %get-tuple-element.104), channel_id=1, source_target_pairs={{0,24},{2,26},{4,28},{6,30},{8,16},{10,18},{12,20},{14,22},{16,8},... | collective-permute-start | bytes 196616 | tf_op jit(solution)/shard_map/ppermute | solution.py:772
  163.4 18.0 %collective-permute-start.46 = (bf16[4,19,16,128]{3,2,1,0:T(8,128)(2,1)S(1)}, bf16[4,19,16,128]{3,2,1,0:T(8,128)(2,1)S(1)}, u32[]{:S(2)}, u32[]{:S(2)}) collective-permute-start(bf16[4,19,16,128]{3,2,1,0:T(8,128)(2,1)S(1)} %slice.84), channel_id=1, source_target_pairs={{0,8},{2,10},{4,12},{6,14},{8,0},{10,2},{12,4},{14,6},{16,24},{18,... | collective-permute-start | bytes 933896 | tf_op jit(solution)/shard_map/ppermute | solution.py:772
  175.4 70.8 %collective-permute-start.33 = (bf16[256,1024]{1,0:T(8,128)(2,1)}, bf16[256,1024]{1,0:T(8,128)(2,1)S(1)}, u32[]{:S(2)}, u32[]{:S(2)}) collective-permute-start(bf16[256,1024]{1,0:T(8,128)(2,1)} %get-tuple-element.113.own), channel_id=1, source_target_pairs={{0,1},{1,0},{2,3},{3,2},{4,5},{5,4},{6,7},{7,6},{8,9},{9,8},{10,11... | collective-permute-start | bytes 1572872 | tf_op jit(solution)/shard_map/ppermute | solution.py:768
  180.7 9.6 %collective-permute-start.35 = (bf16[8,5,16,128]{3,2,1,0:T(8,128)(2,1)S(1)}, bf16[8,5,16,128]{3,2,1,0:T(8,128)(2,1)S(1)}, u32[]{:S(2)}, u32[]{:S(2)}) collective-permute-start(bf16[8,5,16,128]{3,2,1,0:T(8,128)(2,1)S(1)} %slice.73), channel_id=1, source_target_pairs={{0,16},{2,18},{4,20},{6,22},{8,24},{10,26},{12,28},{14,30},{16,0},... | collective-permute-start | bytes 491528 | tf_op jit(solution)/shard_map/ppermute | solution.py:772
  181.5 8.9 %collective-permute-start.47 = (bf16[2,19,16,128]{3,2,1,0:T(8,128)(2,1)S(1)}, bf16[2,19,16,128]{3,2,1,0:T(8,128)(2,1)S(1)}, u32[]{:S(2)}, u32[]{:S(2)}) collective-permute-start(bf16[2,19,16,128]{3,2,1,0:T(8,128)(2,1)S(1)} %slice.86), channel_id=1, source_target_pairs={{0,4},{2,6},{4,0},{6,2},{8,12},{10,14},{12,8},{14,10},{16,20},{18,... | collective-permute-start | bytes 466952 | tf_op jit(solution)/shard_map/ppermute | solution.py:772
  206.5 8.4 %collective-permute-start.51 = (bf16[4,19,16,128]{3,2,1,0:T(8,128)(2,1)S(1)}, bf16[4,19,16,128]{3,2,1,0:T(8,128)(2,1)S(1)}, u32[]{:S(2)}, u32[]{:S(2)}) collective-permute-start(bf16[4,19,16,128]{3,2,1,0:T(8,128)(2,1)S(1)} %pad_maximum_fusion.1), channel_id=1, source_target_pairs={{0,8},{2,10},{4,12},{6,14},{8,0},{10,2},{12,4},{14,6},{16,24},{18,... | collective-permute-start | bytes 933896 | tf_op jit(solution)/shard_map/ppermute | solution.py:772
  210.9 7.4 %collective-permute-start.41 = (bf16[4,5,16,128]{3,2,1,0:T(8,128)(2,1)S(1)}, bf16[4,5,16,128]{3,2,1,0:T(8,128)(2,1)S(1)}, u32[]{:S(2)}, u32[]{:S(2)}) collective-permute-start(bf16[4,5,16,128]{3,2,1,0:T(8,128)(2,1)S(1)} %pad_maximum_fusion.6), channel_id=1, source_target_pairs={{0,8},{2,10},{4,12},{6,14},{8,0},{10,2},{12,4},{14,6},{16,24},{18,... | collective-permute-start | bytes 245768 | tf_op jit(solution)/shard_map/ppermute | solution.py:772
  215.0 29.3 %collective-permute-start.52 = (bf16[8,19,16,128]{3,2,1,0:T(8,128)(2,1)S(1)}, bf16[8,19,16,128]{3,2,1,0:T(8,128)(2,1)S(1)}, u32[]{:S(2)}, u32[]{:S(2)}) collective-permute-start(bf16[8,19,16,128]{3,2,1,0:T(8,128)(2,1)S(1)} %pad_maximum_fusion), channel_id=1, source_target_pairs={{0,16},{2,18},{4,20},{6,22},{8,24},{10,26},{12,28},{14,30},{16,0},... | collective-permute-start | bytes 1867784 | tf_op jit(solution)/shard_map/ppermute | solution.py:772
  218.4 27.7 %collective-permute-start.42 = (bf16[8,5,16,128]{3,2,1,0:T(8,128)(2,1)S(1)}, bf16[8,5,16,128]{3,2,1,0:T(8,128)(2,1)S(1)}, u32[]{:S(2)}, u32[]{:S(2)}) collective-permute-start(bf16[8,5,16,128]{3,2,1,0:T(8,128)(2,1)S(1)} %pad_maximum_fusion.4), channel_id=1, source_target_pairs={{0,16},{2,18},{4,20},{6,22},{8,24},{10,26},{12,28},{14,30},{16,0},... | collective-permute-start | bytes 491528 | tf_op jit(solution)/shard_map/ppermute | solution.py:772
  244.5 9.0 %collective-permute-start.53 = (bf16[16,4,16,128]{3,2,1,0:T(8,128)(2,1)S(1)}, bf16[16,4,16,128]{3,2,1,0:T(8,128)(2,1)S(1)}, u32[]{:S(2)}, u32[]{:S(2)}) collective-permute-start(bf16[16,4,16,128]{3,2,1,0:T(8,128)(2,1)S(1)} %slice.89), channel_id=1, source_target_pairs={{0,1},{1,0},{2,3},{3,2},{4,5},{5,4},{6,7},{7,6},{8,9},{9,8},{10,11... | collective-permute-start | bytes 786440 | tf_op jit(solution)/shard_map/ppermute | solution.py:768
  (68 other events, 422.2 us)

commit v2 on v1

--- a/solution.py
+++ b/solution.py
@@ -16,7 +16,8 @@
 BF = jnp.bfloat16
 F32 = jnp.float32
 LOG2E = 1.4426950408889634
-VMEM_LIMIT = 56 * 1024 * 1024
+VMEM_SMALL = 20 * 1024 * 1024
+VMEM_LARGE = 56 * 1024 * 1024
 
 
 def mm(left, right):
@@ -56,6 +57,20 @@
         self.KT = n_ctx * self.R
 
 
+class Meta:
+    def __init__(self, extra, adapter):
+        self.refs, self.docs = (extra, adapter), extra.shape[0]
+
+    def __getitem__(self, i):
+        if i < 2:
+            return lax.axis_index(("ctx", "wa")[i])
+        return self.refs[(i - 2) // self.docs][(i - 2) % self.docs]
+
+
+def with_meta(kernel):
+    return lambda extra, adapter, *refs: kernel(Meta(extra, adapter), *refs)
+
+
 def doc_starts(cfg, meta):
     out = [jnp.int32(0)]
     for j in range(cfg.docs):
@@ -121,35 +136,44 @@
     return jnp.concatenate([values] * copies, axis=1) if copies > 1 else values
 
 
-def params(**kw):
-    return pltpu.CompilerParams(vmem_limit_bytes=VMEM_LIMIT, **kw)
+def params(large=False, **kw):
+    limit = VMEM_SMALL if lax.axis_size("ctx") <= 16 and not large else VMEM_LARGE
+    return pltpu.CompilerParams(vmem_limit_bytes=limit, **kw)
 
 
 SMEM = pl.BlockSpec(memory_space=pltpu.SMEM)
 
 
-def call(kernel, outs, ins, scratch=(), flops=0, bytes_accessed=0, name=None):
+def cost(us):
+    return pl.CostEstimate(flops=int(us * 1.15e9), bytes_accessed=0, transcendentals=0)
+
+
+def call(kernel, outs, ins, scratch=(), us=1.0, name=None, large=False):
+    ins = [*ins[0], *ins[1:]]
     return pl.pallas_call(
-        kernel,
+        with_meta(kernel),
         out_shape=[jax.ShapeDtypeStruct(s, d) for s, d in outs],
-        in_specs=[SMEM] + [pl.BlockSpec(memory_space=pltpu.VMEM)] * (len(ins) - 1),
+        in_specs=[SMEM] * 2 + [pl.BlockSpec(memory_space=pltpu.VMEM)] * (len(ins) - 2),
         out_specs=[pl.BlockSpec(memory_space=pltpu.VMEM)] * len(outs),
         scratch_shapes=list(scratch),
-        compiler_params=params(),
-        cost_estimate=pl.CostEstimate(
-            flops=flops, bytes_accessed=bytes_accessed, transcendentals=0
-        ),
+        compiler_params=params(large),
+        cost_estimate=cost(us),
         name=name,
     )(*ins)
 
 
 def pre_kernel(
-    cfg, meta, x_ref, gain, wq, wk, wv, aq, ak, av, bq, bk, bv, qg, kg, cos, sin, *refs
+    cfg, meta, x_ref, gain, wq, wk, wv, aq, ak, av, bq, bk, bv, qg, kg, inverse, *refs
 ):
     G, hd = cfg.G, cfg.hd
     kv_out, q_out = refs[:G], refs[G : 2 * G]
-    qraw_ref, kraw_ref, sides_ref, normed_ref, kv_scr, q_scr = refs[2 * G :]
+    qraw_ref, kraw_ref, sides_ref, normed_ref, cos, sin, kv_scr, q_scr = refs[2 * G :]
     hi = meta[0] // cfg.lo
+    shape = cos.shape
+    token = iota(shape, 0) * cfg.n + meta[0]
+    angle = (token - start_of(doc_starts(cfg, meta), token)).astype(F32) * inverse[...]
+    cos[...] = jnp.cos(angle)
+    sin[...] = jnp.sin(angle) * jnp.where(iota(shape, 1) % hd < hd // 2, -1.0, 1.0)
     x = x_ref[...].astype(F32)
     rr = lax.rsqrt(jnp.mean(x * x, axis=-1, keepdims=True) + norm_eps)
     normed = (x * rr * gain[...]).astype(BF)
@@ -194,6 +218,10 @@
 
 def split_pieces(ref, count):
     return [ref.at[i] for i in range(count)]
+
+
+def message_pieces(cfg, ref):
+    return [ref.at[pl.ds(k * cfg.T, cfg.T)] for k in range(cfg.G)]
 
 
 def token_in_span(cfg, meta, index):
@@ -279,10 +307,32 @@
     lax.fori_loop(0, cfg.NT, query_tile, 0)
 
 
+def head_sums(cfg, prod):
+    pick = (iota((16, prod.shape[1]), 1) // cfg.hd == iota((16, prod.shape[1]), 0)).astype(BF)
+    high = prod.astype(BF)
+    low = (prod - high.astype(F32)).astype(BF)
+    return mm_nt(pick, high) + mm_nt(pick, low)
+
+
 def scale_kernel(cfg, meta, *refs):
-    G = cfg.G
+    G, T, R, NT, QH = cfg.G, cfg.T, cfg.R, cfg.NT, cfg.QH
+    go, linv, o_all, out, scr, delta = refs[:G], refs[G], refs[G + 1], refs[G + 2], *refs[G + 3 :]
+    delta[...] = jnp.zeros_like(delta)
     for k in range(G):
-        refs[G + 1][k] = (refs[k][...].astype(F32) * refs[G][k]).astype(BF)
+        scaled = (go[k][...].astype(F32) * linv[k]).astype(BF)
+        out[k * T : (k + 1) * T, :] = scaled
+        prod = scaled.astype(F32) * o_all[k].astype(F32)
+        for t in range(NT):
+            scr[t, k * R : (k + 1) * R, :] = prod[t * R : (t + 1) * R]
+    for t in range(NT):
+        sums = head_sums(cfg, scr[t])
+        for h in range(cfg.groups):
+            delta[h * NT + t : h * NT + t + 1, :QH] = sums[h : h + 1]
+    high = delta[...].astype(BF)
+    at = G * T
+    rows = cfg.groups * NT
+    out[at : at + rows, :] = high
+    out[at + rows : at + 2 * rows, :] = (delta[...] - high.astype(F32)).astype(BF)
 
 
 def grad_query_kernel(cfg, meta, *refs):
@@ -296,7 +346,7 @@
         pieces = pieces + split_pieces(ref, G)
     load_tiles(cfg, kv_scr, pieces)
     load_tiles(cfg, q_scr, q_in)
-    load_tiles(cfg, go_scr, split_pieces(go_ref, G))
+    load_tiles(cfg, go_scr, message_pieces(cfg, go_ref))
     load_tiles(cfg, o_scr, split_pieces(o_ref, G))
     starts = doc_starts(cfg, meta)
     QH = cfg.QH
@@ -346,25 +396,23 @@
 def grad_key_kernel(cfg, meta, *refs):
     G, T, R, hd, lo = cfg.G, cfg.T, cfg.R, cfg.hd, cfg.lo
     own = refs[0]
-    q_refs, go_refs, o_refs = (refs[1 + i * lo : 1 + (i + 1) * lo] for i in range(3))
-    rest = refs[1 + 3 * lo :]
-    dkv_out, kv_scr, q_scr, go_scr, o_scr, delta_scr = rest[:G], *rest[G:]
+    q_refs, go_refs = (refs[1 + i * lo : 1 + (i + 1) * lo] for i in range(2))
+    rest = refs[1 + 2 * lo :]
+    dkv_out, kv_scr, q_scr, go_scr, delta_scr = rest[:G], *rest[G:]
     load_tiles(cfg, kv_scr, split_pieces(own, G))
-    for scr, group in ((q_scr, q_refs), (go_scr, go_refs), (o_scr, o_refs)):
-        load_tiles(cfg, scr, [piece for ref in group for piece in split_pieces(ref, G)])
+    load_tiles(cfg, q_scr, [piece for ref in q_refs for piece in split_pieces(ref, G)])
+    load_tiles(cfg, go_scr, [piece for ref in go_refs for piece in message_pieces(cfg, ref)])
     starts = doc_starts(cfg, meta)
-    QH = cfg.QH
+    QH, NT = cfg.QH, cfg.NT
     scale = hd ** (-0.5) * LOG2E
-    pick = (iota((16, 2 * hd), 1) // hd == iota((16, 2 * hd), 0)).astype(BF)
-
-    def deltas(t, carry):
-        prod = go_scr[t].astype(F32) * o_scr[t].astype(F32)
-        high = prod.astype(BF)
-        low = (prod - high.astype(F32)).astype(BF)
-        delta_scr[t] = mm_nt(pick, high) + mm_nt(pick, low)
-        return carry
-
-    lax.fori_loop(0, cfg.NT, deltas, 0)
+    rows = cfg.groups * NT
+    for j in range(lo):
+        sums = go_refs[j][G * T : G * T + 2 * rows, :].astype(F32)
+        sums = sums[:rows] + sums[rows:]
+        for t in range(NT):
+            for h in range(cfg.groups):
+                at = h * NT + t
+                delta_scr[t, h : h + 1, j * QH : (j + 1) * QH] = sums[at : at + 1, :QH]
     query_off = token_in_span(cfg, meta, iota((1, cfg.KT), 1))
     row_off = token_in_span(cfg, meta, iota((2 * QH, 1), 0) % QH)
     first = iota((QH, 2 * hd), 1) < hd
@@ -435,12 +483,14 @@
 
 
 def ffn_kernel(
-    cfg, steps, meta, x_ref, own, other, bo, gain, wg, wu, wd, bg, bu, ag, au, ad, bd, cot_ref,
-    mixed_ref, dfn_ref, part_ref, bgate, bup, adown, akeep, asend, oside,
-    fn, sg, su, gsd, sgt, sut, gsdt, down, side_sum, dfn, gsg, gsu, a_scr,
+    cfg, units, steps, meta, x_ref, own, other, bo, gain, wg, wu, wd, bg, bu, ag, au, ad, bd, cot_ref,
+    mixed_ref, dfn_ref, part_ref, oside, *refs,
 ):
     step = pl.program_id(0)
     S, D = cfg.S, cfg.D
+    chunks, refs = refs[: units.n], refs[units.n :]
+    fn, sg, su, gsd, sgt, sut, gsdt, down, side_sum, dfn, gsg, gsu, grads = refs
+    flip = meta[0] % cfg.lo
 
     @pl.when(step == 0)
     def _():
@@ -483,9 +533,9 @@
     dfn[...] += mm_nt(grad_gate, wg[...]) + mm_nt(grad_upper, wu[...])
     gsg[...] += mm_nt(grad_gate, bg[...])
     gsu[...] += mm_nt(grad_upper, bu[...])
-    bgate[...] = mm(sgt[...], grad_gate).astype(BF)
-    bup[...] = mm(sut[...], grad_upper).astype(BF)
-    adown[...] = mm(gsdt[...], hidden).astype(BF)
+    for i, (left, right) in enumerate(((sgt, grad_gate), (sut, grad_upper), (gsdt, hidden))):
+        first = step * (right.shape[1] // 128)
+        units.store(grads, flip, 1, i, mm(left[...], right).astype(BF), first)
 
     @pl.when(step == steps - 1)
     def _():
@@ -496,16 +546,16 @@
         dfn_ref[...] = (dfn[...] + mm_nt(side_g, ag[...]) + mm_nt(side_u, au[...])).astype(BF)
         part_ref[:, :D] = down[...].astype(BF)
         part_ref[:, D:] = side_sum[...].astype(BF)
-        a_scr[:S, :] = mm(mm(side_g, select).T.astype(BF), fn[...])
-        a_scr[S:, :] = mm(mm(side_u, select).T.astype(BF), fn[...])
-        half = D // 2
-        keep = pl.ds(pl.multiple_of(meta[1] * half, half), half)
-        send = pl.ds(pl.multiple_of((1 - meta[1]) * half, half), half)
-        akeep[...] = a_scr[:, keep].astype(BF)
-        asend[...] = a_scr[:, send].astype(BF)
-
-
-def ffn_call(cfg, meta, x, own, other, bo, gain, wg, wu, wd, bg, bu, ag, au, ad, bd, cot):
+        side_d = (mask * side_sum[...]).astype(BF)
+        for i, (side, right) in enumerate(((side_g, fn), (side_u, fn), (side_d, cot_ref))):
+            left = mm(side, select).T.astype(BF)
+            units.store(grads, flip, 0, i, mm(left, right[...]).astype(BF), 0)
+        units.clear_spare(grads, flip)
+        for j, chunk in enumerate(chunks):
+            chunk[...] = grads[j]
+
+
+def ffn_call(cfg, units, meta, x, own, other, bo, gain, wg, wu, wd, bg, bu, ag, au, ad, bd, cot):
     T, D, F, AW, S = cfg.T, cfg.D, cfg.F, cfg.AW, cfg.S
     tile = 256
     steps = F // tile
@@ -516,30 +566,20 @@
         ((T, D), F32),
         ((T, D), BF),
         ((T, D + AW), BF),
-        ((S, F), BF),
-        ((S, F), BF),
-        ((S, F), BF),
-        ((2 * S, D // 2), BF),
-        ((2 * S, D // 2), BF),
         ((T, S), BF),
-    ]
+    ] + [((units.u, 16, 128), BF)] * units.n
     out_specs = [
         whole((T, D)),
         whole((T, D)),
         whole((T, D + AW)),
-        cols(S),
-        cols(S),
-        cols(S),
-        whole((2 * S, D // 2)),
-        whole((2 * S, D // 2)),
         whole((T, S)),
-    ]
-    flops = 2 * T * D * F * 6
+    ] + [whole((units.u, 16, 128))] * units.n
     return pl.pallas_call(
-        functools.partial(ffn_kernel, cfg, steps),
+        with_meta(functools.partial(ffn_kernel, cfg, units, steps)),
         grid=(steps,),
         out_shape=[jax.ShapeDtypeStruct(s, d) for s, d in outs],
         in_specs=[
+            SMEM,
             SMEM,
             whole((T, D)),
             whole((T, D + AW)),
@@ -571,14 +611,12 @@
             pltpu.VMEM((T, D), F32),
             pltpu.VMEM((T, AW), F32),
             pltpu.VMEM((T, AW), F32),
-            pltpu.VMEM((2 * S, D), F32),
+            pltpu.VMEM((units.n, units.u, 16, 128), BF),
         ],
         compiler_params=params(dimension_semantics=("arbitrary",)),
-        cost_estimate=pl.CostEstimate(
-            flops=flops, bytes_accessed=3 * D * F * 2, transcendentals=T * F
-        ),
+        cost_estimate=cost(19),
         name="ffn",
-    )(meta, x, own, other, bo, gain, wg, wu, wd, bg, bu, ag, au, ad, bd, cot)
+    )(*meta, x, own, other, bo, gain, wg, wu, wd, bg, bu, ag, au, ad, bd, cot)
 
 
 def mixed_grad_kernel(cfg, meta, *refs):
@@ -613,56 +651,69 @@
     ograds[1] = mm(oside[...].astype(F32).T.astype(BF), mine).astype(BF)
 
 
-def output_kernel(cfg, meta, mixed, own, other, bd, cot, out_ref, dgrad):
+def output_kernel(cfg, meta, mixed, own, other, bd, out_ref):
     D = cfg.D
     total = own[...].astype(F32) + other[...].astype(F32)
-    mask = adapter_mask(cfg, meta)
-    side = (mask * total[:, D:]).astype(BF)
+    side = (adapter_mask(cfg, meta) * total[:, D:]).astype(BF)
     out_ref[...] = (mixed[...] + total[:, :D] + mm(side, bd[...])).astype(BF)
-    half = D // 2
-    mine = cot[:, pl.ds(pl.multiple_of(meta[1] * half, half), half)]
-    dgrad[...] = mm(mm(side, slot_select(cfg, meta)).T.astype(BF), mine).astype(BF)
-
-
-def qkv_grad_kernel(cfg, meta, *refs):
-    G, D, S, hd = cfg.G, cfg.D, cfg.S, cfg.hd
-    dq_in, dkv_in = refs[:G], refs[G : 2 * G]
+
+
+def head_back(cfg, cos, sin, grad, raw, g):
+    hd = cfg.hd
+    copies = raw.shape[1] // hd
+    per = raw.shape[1] // cos.shape[1]
+    un = grad * lanes(cos[...], per) - swap_halves(grad, hd) * lanes(sin[...], per)
+    w = un * lanes(g[...], copies)
+    rr = lax.rsqrt(block_mean(raw * raw, hd) + norm_eps)
+    return rr * w - rr * rr * rr * raw * block_mean(w * raw, hd)
+
+
+def half_lanes(cfg, meta):
+    half = cfg.D // 2
+    keep = pl.ds(pl.multiple_of(meta[1] * half, half), half)
+    send = pl.ds(pl.multiple_of((1 - meta[1]) * half, half), half)
+    return keep, send
+
+
+def query_back_kernel(cfg, meta, *refs):
+    G, S = cfg.G, cfg.S
+    normed, raw, sides, cos, sin, gain, w, a, b, part, bgrad, akeep, asend, dq_scr, a_scr = refs[G:]
+    place_pieces(cfg, meta[0] // cfg.lo, dq_scr, refs[:G])
+    g = head_back(cfg, cos, sin, dq_scr[...].astype(F32), raw[...], gain).astype(BF)
+    select = slot_select(cfg, meta)
+    grad_side = (adapter_mask(cfg, meta) * mm_nt(g, b[...])).astype(BF)
+    part[...] = mm_nt(g, w[...]) + mm_nt(grad_side, a[...])
+    a_scr[...] = mm(mm(grad_side, select).T.astype(BF), normed[...])
+    bgrad[...] = mm(sides[0].astype(F32).T.astype(BF), g).astype(BF)
+    keep, send = half_lanes(cfg, meta)
+    akeep[...] = a_scr[:, keep].astype(BF)
+    asend[...] = a_scr[:, send].astype(BF)
+
+
+def key_value_back_kernel(cfg, meta, *refs):
+    G, S, hd = cfg.G, cfg.S, cfg.hd
     (
-        normed, qraw, kraw, sides, cos, sin, qg, kg, wq, wk, wv, aq, ak, av, bq, bk, bv,
-        part, bgrad, akeep, asend, dq_scr, dkv_scr, a_scr,
-    ) = refs[2 * G :]
-    hi = meta[0] // cfg.lo
-    place_pieces(cfg, hi, dq_scr, dq_in)
-    place_pieces(cfg, hi, dkv_scr, dkv_in)
+        normed, raw, sides, cos, sin, gain, wk, wv, ak, av, bk, bv, qpart,
+        part, bgrad, akeep, asend, dkv_scr, a_scr,
+    ) = refs[G:]
+    place_pieces(cfg, meta[0] // cfg.lo, dkv_scr, refs[:G])
     mask = adapter_mask(cfg, meta)
     select = slot_select(cfg, meta)
-
-    def back(grad, raw, g):
-        copies = raw.shape[1] // hd
-        per = raw.shape[1] // cos.shape[1]
-        un = grad * lanes(cos[...], per) - swap_halves(grad, hd) * lanes(sin[...], per)
-        w = un * lanes(g[...], copies)
-        rr = lax.rsqrt(block_mean(raw * raw, hd) + norm_eps)
-        return rr * w - rr * rr * rr * raw * block_mean(w * raw, hd)
-
     dkv = dkv_scr[...]
     dk = jnp.concatenate([dkv[:, 2 * h * hd : (2 * h + 1) * hd] for h in range(G)], axis=1)
     dv = jnp.concatenate([dkv[:, (2 * h + 1) * hd : (2 * h + 2) * hd] for h in range(G)], axis=1)
-    gq = back(dq_scr[...].astype(F32), qraw[...], qg).astype(BF)
-    gk = back(dk.astype(F32), kraw[...], kg).astype(BF)
-    total = jnp.zeros((cfg.T, D), F32)
-    at = 0
-    for i, (g, w, a, b) in enumerate(((gq, wq, aq, bq), (gk, wk, ak, bk), (dv, wv, av, bv))):
+    gk = head_back(cfg, cos, sin, dk.astype(F32), raw[...], gain).astype(BF)
+    total = qpart[...]
+    width = gk.shape[1]
+    for i, (g, w, a, b) in enumerate(((gk, wk, ak, bk), (dv, wv, av, bv))):
         grad_side = (mask * mm_nt(g, b[...])).astype(BF)
         total = total + mm_nt(g, w[...]) + mm_nt(grad_side, a[...])
         a_scr[i * S : (i + 1) * S, :] = mm(mm(grad_side, select).T.astype(BF), normed[...])
-        width = g.shape[1]
-        bgrad[:, at : at + width] = mm(sides[i].astype(F32).T.astype(BF), g).astype(BF)
-        at = at + width
+        bgrad[:, i * width : (i + 1) * width] = mm(
+            sides[i + 1].astype(F32).T.astype(BF), g
+        ).astype(BF)
     part[...] = total.astype(BF)
-    half = D // 2
-    keep = pl.ds(pl.multiple_of(meta[1] * half, half), half)
-    send = pl.ds(pl.multiple_of((1 - meta[1]) * half, half), half)
+    keep, send = half_lanes(cfg, meta)
     akeep[...] = a_scr[:, keep].astype(BF)
     asend[...] = a_scr[:, send].astype(BF)
 
@@ -676,17 +727,15 @@
 
 
 class Units:
-    def __init__(self, cfg, shared, private):
-        self.n = cfg.n
+    def __init__(self, cfg, n, shared, private):
+        self.n = n
         self.high = cfg.S // 16
-        self.us = self._layout(shared, 0)
-        self.up = self._layout(private, 0)
+        self.shared, self.private = shared, private
+        self.us, self.up = self.per_chunk(shared), self.per_chunk(private)
         self.u = self.us + self.up
-        self.shared, self.private = shared, private
-
-    def _layout(self, widths, _):
-        count = sum(w // 128 for w in widths) * self.high
-        return -(-count // self.n)
+
+    def per_chunk(self, widths):
+        return -(-sum(w // 128 for w in widths) * self.high // self.n)
 
     def places(self, which):
         widths, per, base = (
@@ -709,13 +758,28 @@
             out += [(i // per, base + i % per) for i in range(count, per * self.n)]
         return out
 
-
-def pack(units, idx, out, arrays):
-    for spots, values in zip(units.places(0) + units.places(1), arrays):
-        for chunk, off, a, c in spots:
-            out[chunk ^ idx, off] = values[a * 16 : a * 16 + 16, c * 128 : c * 128 + 128]
-    for chunk, off in units.spare():
-        out[chunk ^ idx, off] = jnp.zeros((16, 128), BF)
+    def store(self, out, flip, which, array, values, first):
+        widths, per, base = (
+            (self.shared, self.us, 0) if which == 0 else (self.private, self.up, self.us)
+        )
+        at = sum(w // 128 for w in widths[:array]) * self.high + first * self.high
+        for c in range(values.shape[1] // 128):
+            for a in range(self.high):
+                unit = at + c * self.high + a
+                out[(unit // per) ^ flip, base + unit % per] = values[
+                    a * 16 : a * 16 + 16, c * 128 : c * 128 + 128
+                ]
+
+    def clear_spare(self, out, flip):
+        for chunk, off in self.spare():
+            out[chunk ^ flip, off] = jnp.zeros((16, 128), BF)
+
+
+def pack(units, out, flip, arrays):
+    for i, values in enumerate(arrays):
+        which = int(i >= len(units.shared))
+        units.store(out, flip, which, i - which * len(units.shared), values, 0)
+    units.clear_spare(out, flip)
 
 
 def add_halves(keep, got, count):
@@ -724,26 +788,30 @@
     return [total[i * rows : (i + 1) * rows] for i in range(count)]
 
 
-def pack_ffn_kernel(cfg, units, meta, keep, got, bdown, ograds, bgate, bup, adown, out):
-    shared = add_halves(keep, got, 2) + [bdown[...], ograds[1]]
-    pack(units, meta[0], out, shared + [bgate[...], bup[...], adown[...], ograds[0]])
-
-
-def pack_qkv_kernel(cfg, units, qw, kw, meta, keep, got, bgrad, out):
-    private = [bgrad[:, :qw], bgrad[:, qw : qw + kw], bgrad[:, qw + kw :]]
-    pack(units, meta[0], out, add_halves(keep, got, 3) + private)
-
-
-def unpack(units, idx, ref, spots, base=0):
+def pack_qkv_kernel(cfg, units, meta, keep_q, got_q, keep, got, ograds, bq, bkv, *outs):
+    scr, outs = outs[-1], outs[:-1]
+    kw = bkv.shape[1] // 2
+    shared = add_halves(keep_q, got_q, 1) + add_halves(keep, got, 2) + [ograds[1]]
+    private = [ograds[0], bq[...], bkv[:, :kw], bkv[:, kw:]]
+    pack(units, scr, meta[0] % cfg.lo, shared + private)
+    for j, out in enumerate(outs):
+        out[...] = scr[j]
+
+
+def unpack(ref, spots, place):
     cols = {}
     for chunk, off, a, c in spots:
-        cols.setdefault(c, []).append(ref[chunk ^ idx, off - base])
+        cols.setdefault(c, []).append(ref[place(chunk), off])
     return jnp.concatenate([jnp.concatenate(cols[c], axis=0) for c in sorted(cols)], axis=1)
 
 
-def expand_kernel(cfg, units, plan, meta, own, other, *outs):
-    idx, wa = meta[0], meta[1]
+def expand_kernel(cfg, units, plan, halves, meta, *refs):
+    own_in, other, outs, own = refs[: cfg.lo], refs[cfg.lo], refs[cfg.lo + 1 : -1], refs[-1]
+    for j in range(cfg.lo):
+        own[j] = own_in[j][...]
+    wa = meta[1]
     select = slot_select(cfg, meta)
+    place = lambda chunk: chunk ^ (meta[0] % cfg.lo)
 
     def write(out, values, transposed, at):
         full = mm(select, values)
@@ -754,36 +822,38 @@
 
     for (which, i, transposed), out in zip(plan, outs):
         spots = units.places(which)[i]
-        mine = unpack(units, idx, own, spots)
+        mine = unpack(own, spots, place)
         if which == 1:
             write(out, mine, transposed, 0)
         else:
-            theirs = unpack(units, idx, other, spots)
+            theirs = unpack(other, spots, place)
+            if not halves:
+                total = mine.astype(F32) + theirs.astype(F32)
+                write(out, total.astype(BF), transposed, 0)
+                continue
             width = mine.shape[1]
             write(out, jnp.where(wa == 0, mine, theirs), transposed, 0)
             write(out, jnp.where(wa == 0, theirs, mine), transposed, width)
 
 
+def upper_bits(cfg):
+    bits, bit = [], cfg.n // 2
+    while bit >= cfg.lo:
+        bits.append(bit)
+        bit //= 2
+    return bits
+
+
+def after(*values):
+    return lax.optimization_barrier(values)
+
+
 def swap_cores(value):
     return lax.ppermute(value, "wa", [(0, 1), (1, 0)])
 
 
 def permute(cfg, value, bits):
     return lax.ppermute(value, "ctx", [(i, i ^ bits) for i in range(cfg.n)])
-
-
-def sum_chunks(cfg, cur):
-    bits = []
-    size = cfg.n // 2
-    while size >= 1:
-        half = cur.shape[0] // 2
-        got = permute(cfg, cur[half:], size)
-        cur = (cur[:half].astype(F32) + got.astype(F32)).astype(BF)
-        bits.append(size)
-        size //= 2
-    for size in reversed(bits):
-        cur = jnp.concatenate([cur, permute(cfg, cur, size)], axis=0)
-    return cur
 
 
 def per_device(
@@ -808,14 +878,7 @@
     T, D, G, S, AW, n, lo = cfg.T, cfg.D, cfg.G, cfg.S, cfg.AW, cfg.n, cfg.lo
     gw = cfg.groups * head_dim
     QW, KW = query_weight.shape[1], key_weight.shape[1]
-    ctx_index = lax.axis_index("ctx")
-    meta = jnp.concatenate(
-        [
-            jnp.stack([ctx_index, lax.axis_index("wa")]).astype(jnp.int32),
-            document_extra,
-            document_adapter,
-        ]
-    )
+    meta = (document_extra, document_adapter)
     x = hidden_in.reshape(T, D)
     cot = cotangent.reshape(T, D)
     gain_a = attn_gain.reshape(1, D)
@@ -823,35 +886,32 @@
     qg = query_gain.reshape(1, head_dim)
     kg = key_gain.reshape(1, head_dim)
 
-    token = jnp.arange(T, dtype=jnp.int32) * n + ctx_index
-    lengths = document_extra + (DOC_MIN - 1)
-    starts = jnp.cumsum(lengths) - lengths
-    position = token - jnp.max(jnp.where(token[:, None] >= starts[None, :], starts[None, :], 0), axis=1)
-    half = head_dim // 2
-    lane = jnp.arange(2 * head_dim, dtype=jnp.int32)
-    inverse = jnp.exp((lane % half).astype(F32) * (-2.0 * math.log(theta_base) / head_dim))
-    angle = position.astype(F32)[:, None] * inverse[None, :]
-    cos = jnp.cos(angle)
-    sin = jnp.sin(angle) * jnp.where(lane % head_dim < half, -1.0, 1.0)[None, :]
+    lane = jnp.arange(2 * head_dim, dtype=jnp.int32) % (head_dim // 2)
+    inverse = jnp.exp(lane.astype(F32) * (-2.0 * math.log(theta_base) / head_dim))[None, :]
 
     piece = ((T, gw), BF)
     pre = call(
         functools.partial(pre_kernel, cfg),
-        [piece] * (2 * G) + [((T, QW), F32), ((T, KW), F32), ((3, T, S), BF), ((T, D), BF)],
+        [piece] * (2 * G)
+        + [((T, QW), F32), ((T, KW), F32), ((3, T, S), BF), ((T, D), BF)]
+        + [((T, 2 * head_dim), F32)] * 2,
         [
             meta, x, gain_a, query_weight, key_weight, value_weight, query_adapt_in, key_adapt_in,
-            value_adapt_in, query_adapt_out, key_adapt_out, value_adapt_out, qg, kg, cos, sin,
+            value_adapt_in, query_adapt_out, key_adapt_out, value_adapt_out, qg, kg, inverse,
         ],
         scratch=[pltpu.VMEM((G, T, gw), BF), pltpu.VMEM((G, T, gw), BF)],
-        flops=2 * T * D * (QW + 2 * KW),
-        bytes_accessed=2 * D * (QW + 2 * KW),
+        us=6,
         name="pre",
+        large=True,
     )
     kv_send, q_send = pre[:G], pre[G : 2 * G]
-    qraw, kraw, sides, normed = pre[2 * G :]
+    qraw, kraw, sides, normed, cos, sin = pre[2 * G :]
 
     def to_heads(pieces):
         return [pieces[0]] + [permute(cfg, pieces[k], k * lo) for k in range(1, G)]
+
+    def add(values):
+        return sum(value.astype(F32) for value in values).astype(BF)
 
     def to_plane(value):
         return [value] + [permute(cfg, value, j) for j in range(1, lo)]
@@ -864,26 +924,30 @@
         [piece] * G + [((G, T, gw), BF), ((G, T, gw), F32)],
         [meta] + q + kv,
         scratch=[tiles(cfg.KT), tiles(cfg.KT), tiles(cfg.QH)],
-        flops=2 * T * G * T * n * 2 * gw,
+        us=12,
         name="attend",
     )
     o_send, o_all, linv = attn[:G], attn[G], attn[G + 1]
     o = to_heads(o_send)
+    q_stack, _ = after(jnp.stack(q), o_send[0])
+    q_plane = to_plane(q_stack)
     (opart,) = call(
         functools.partial(out_kernel, cfg),
         [((T, D + AW), BF)],
         [meta] + o + [out_weight, out_adapt_in],
         scratch=[pltpu.VMEM((T, QW), BF)],
-        flops=2 * T * D * QW,
-        bytes_accessed=2 * D * QW,
+        us=3,
         name="out_proj",
     )
+    units_f = Units(cfg, lo, [D] * 3, [cfg.F] * 3)
     ffn = ffn_call(
-        cfg, meta, x, opart, swap_cores(opart), out_adapt_out, gain_f, gate_weight, up_weight,
+        cfg, units_f, meta, x, opart, swap_cores(opart), out_adapt_out, gain_f, gate_weight, up_weight,
         down_weight, gate_adapt_out, up_adapt_out, gate_adapt_in, up_adapt_in, down_adapt_in,
         down_adapt_out, cot,
     )
-    mixed, dfn, dpart, bgate, bup, adown, akeep, asend, oside = ffn
+    mixed, dfn, dpart, oside, *parts_f = ffn
+    dfn, *q_plane = after(dfn, *q_plane)
+    parts_f = [parts_f[0]] + [permute(cfg, parts_f[j], j) for j in range(1, lo)]
     mg = call(
         functools.partial(mixed_grad_kernel, cfg),
         [((T, D), F32), ((2, S, D // 2), BF)] + [piece] * G,
@@ -891,109 +955,140 @@
         + o
         + [out_weight, out_adapt_in, out_adapt_out, oside],
         scratch=[pltpu.VMEM((T, QW), BF), pltpu.VMEM((G, T, gw), BF), pltpu.VMEM((T, D), BF)],
-        flops=2 * T * D * QW,
-        bytes_accessed=2 * D * QW,
+        us=4.5,
         name="mixed_grad",
     )
     grad_mixed, ograds, go_send = mg[0], mg[1], mg[2:]
     go_heads = to_heads(go_send)
+    dpart, _ = after(dpart, go_send[0])
+    (out_rows,) = call(
+        functools.partial(output_kernel, cfg),
+        [((T, D), BF)],
+        [meta, mixed, dpart, swap_cores(dpart), down_adapt_out],
+        us=2,
+        name="output",
+    )
+    out_rows, *both = after(out_rows, *parts_f, *go_heads)
+    parts_f, go_heads = both[:lo], both[lo:]
+    sum_f = add(parts_f)
+    message = G * T + -(-2 * cfg.groups * cfg.NT // 16) * 16
     (go_all,) = call(
         functools.partial(scale_kernel, cfg),
-        [((G, T, gw), BF)],
-        [meta] + go_heads + [linv],
-        bytes_accessed=8 * G * T * gw,
+        [((message, gw), BF)],
+        [meta] + go_heads + [linv, o_all],
+        scratch=[
+            pltpu.VMEM((cfg.NT, cfg.QH, gw), F32),
+            pltpu.VMEM((cfg.groups * cfg.NT, gw), F32),
+        ],
+        us=2,
         name="scale",
     )
-    q_plane = to_plane(jnp.stack(q))
-    o_plane = to_plane(o_all)
     go_plane = to_plane(go_all)
     dq_send = call(
         functools.partial(grad_query_kernel, cfg),
         [piece] * G,
         [meta] + q + kv + [go_all, o_all],
         scratch=[tiles(cfg.KT), tiles(cfg.QH), tiles(cfg.QH), tiles(cfg.QH)],
-        flops=2 * T * G * T * n * 3 * gw,
+        us=13.5,
         name="grad_query",
     )
+    near, far = upper_bits(cfg)[1], upper_bits(cfg)[0]
+    got_f, *dq_send = after(permute(cfg, sum_f, near), *dq_send)
+    sum_f = add([sum_f, got_f])
     dq = to_heads(dq_send)
     dkv_send = call(
         functools.partial(grad_key_kernel, cfg),
         [piece] * G,
-        [meta, kv[0]] + q_plane + go_plane + o_plane,
-        scratch=[tiles(cfg.QH), tiles(cfg.KT), tiles(cfg.KT), tiles(cfg.KT)]
+        [meta, kv[0]] + q_plane + go_plane,
+        scratch=[tiles(cfg.QH), tiles(cfg.KT), tiles(cfg.KT)]
         + [pltpu.VMEM((cfg.NT, 16, cfg.KT), F32)],
-        flops=2 * T * G * T * n * 4 * gw,
+        us=16,
         name="grad_key",
     )
+    got_f, *both = after(permute(cfg, sum_f, far), *dq, *dkv_send)
+    dq, dkv_send = both[:G], both[G:]
+    sum_f = add([sum_f, got_f])
     dkv = to_heads(dkv_send)
-
-    out_rows, bdown = call(
-        functools.partial(output_kernel, cfg),
-        [((T, D), BF), ((S, D // 2), BF)],
-        [meta, mixed, dpart, swap_cores(dpart), down_adapt_out, cot],
-        name="output",
-    )
-    units_f = Units(cfg, [D // 2] * 4, [cfg.F] * 3 + [QW])
-    qkv = call(
-        functools.partial(qkv_grad_kernel, cfg),
-        [((T, D), BF), ((S, QW + 2 * KW), BF), ((3 * S, D // 2), BF), ((3 * S, D // 2), BF)],
+    pieces_f = to_plane(sum_f)
+
+    qpart, bgrad_q, akeep_q, asend_q = call(
+        functools.partial(query_back_kernel, cfg),
+        [((T, D), F32), ((S, QW), BF), ((S, D // 2), BF), ((S, D // 2), BF)],
         [meta]
         + dq
+        + [
+            normed, qraw, sides, cos, sin, qg, query_weight, query_adapt_in, query_adapt_out,
+        ],
+        scratch=[pltpu.VMEM((T, QW), BF), pltpu.VMEM((S, D), F32)],
+        us=3.5,
+        name="query_back",
+    )
+    dnormed, bgrad_kv, akeep_kv, asend_kv = call(
+        functools.partial(key_value_back_kernel, cfg),
+        [((T, D), BF), ((S, 2 * KW), BF), ((2 * S, D // 2), BF), ((2 * S, D // 2), BF)],
+        [meta]
         + dkv
         + [
-            normed, qraw, kraw, sides, cos, sin, qg, kg, query_weight, key_weight, value_weight,
-            query_adapt_in, key_adapt_in, value_adapt_in, query_adapt_out, key_adapt_out,
-            value_adapt_out,
+            normed, kraw, sides, cos, sin, kg, key_weight, value_weight, key_adapt_in,
+            value_adapt_in, key_adapt_out, value_adapt_out, qpart,
         ],
-        scratch=[
-            pltpu.VMEM((T, QW), BF),
-            pltpu.VMEM((T, 2 * KW), BF),
-            pltpu.VMEM((3 * S, D), F32),
-        ],
-        flops=2 * T * D * (QW + 2 * KW),
-        bytes_accessed=2 * D * (QW + 2 * KW),
-        name="qkv_grad",
-    )
-    dnormed, bqkv, akeep_q, asend_q = qkv
+        scratch=[pltpu.VMEM((T, 2 * KW), BF), pltpu.VMEM((2 * S, D), F32)],
+        us=4.5,
+        name="key_value_back",
+    )
     (input_rows,) = call(
         functools.partial(input_grad_kernel, cfg),
         [((T, D), BF)],
         [meta, x, gain_a, grad_mixed, dnormed, swap_cores(dnormed)],
+        us=3,
         name="input_grad",
     )
 
-    def reduce_and_expand(units, pack_in, pack_kern, plan, outs, tag):
-        (buffer,) = call(pack_kern, [((n, units.u, 16, 128), BF)], [meta] + pack_in, name="pack_" + tag)
-        total = sum_chunks(cfg, buffer)
-        theirs = swap_cores(total[:, : units.us])
+    def expand(units, pieces, plan, halves, outs, name):
+        theirs = swap_cores(jnp.stack([value[: units.us] for value in pieces]))
         return call(
-            functools.partial(expand_kernel, cfg, units, plan),
+            functools.partial(expand_kernel, cfg, units, plan, halves),
             outs,
-            [meta, total, theirs],
-            name="expand_" + tag,
+            [meta] + pieces + [theirs],
+            scratch=[pltpu.VMEM((units.n, units.u, 16, 128), BF)],
+            us=4,
+            name=name,
         )
 
-    grads_f = reduce_and_expand(
+    units_q = Units(cfg, lo, [D // 2] * 4, [QW, QW, KW, KW])
+    dnormed, bgrad_kv, *pieces_f = after(dnormed, bgrad_kv, *pieces_f)
+    parts_q = call(
+        functools.partial(pack_qkv_kernel, cfg, units_q),
+        [((units_q.u, 16, 128), BF)] * lo,
+        [meta, akeep_q, swap_cores(asend_q), akeep_kv, swap_cores(asend_kv), ograds, bgrad_q]
+        + [bgrad_kv],
+        scratch=[pltpu.VMEM((lo, units_q.u, 16, 128), BF)],
+        us=2,
+        name="pack_qkv",
+    )
+    sum_q = add([parts_q[0]] + [permute(cfg, parts_q[j], j) for j in range(1, lo)])
+    for bit in upper_bits(cfg):
+        sum_q = add([sum_q, permute(cfg, sum_q, bit)])
+    pieces_q = to_plane(sum_q)
+    gate_in, up_in, down_out, gate_out, up_out, down_in = expand(
         units_f,
-        [akeep, swap_cores(asend), bdown, ograds, bgate, bup, adown],
-        functools.partial(pack_ffn_kernel, cfg, units_f),
-        [(0, 0, True), (0, 1, True), (0, 2, False), (0, 3, False)]
-        + [(1, 0, False), (1, 1, False), (1, 2, True), (1, 3, True)],
-        [((D, AW), F32), ((D, AW), F32), ((AW, D), F32), ((AW, D), F32)]
-        + [((AW, cfg.F), F32), ((AW, cfg.F), F32), ((cfg.F, AW), F32), ((QW, AW), F32)],
-        "ffn",
-    )
-    gate_in, up_in, down_out, out_out, gate_out, up_out, down_in, out_in = grads_f
-    units_q = Units(cfg, [D // 2] * 3, [QW, KW, KW])
-    grads_q = reduce_and_expand(
+        pieces_f,
+        [(0, 0, True), (0, 1, True), (0, 2, False), (1, 0, False), (1, 1, False), (1, 2, True)],
+        False,
+        [((D, AW), F32), ((D, AW), F32), ((AW, D), F32)]
+        + [((AW, cfg.F), F32), ((AW, cfg.F), F32), ((cfg.F, AW), F32)],
+        "expand_ffn",
+    )
+    query_in, key_in, value_in, out_out, out_in, query_out, key_out, value_out = expand(
         units_q,
-        [akeep_q, swap_cores(asend_q), bqkv],
-        functools.partial(pack_qkv_kernel, cfg, units_q, QW, KW),
-        [(0, 0, True), (0, 1, True), (0, 2, True), (1, 0, False), (1, 1, False), (1, 2, False)],
-        [((D, AW), F32)] * 3 + [((AW, QW), F32), ((AW, KW), F32), ((AW, KW), F32)],
-        "qkv",
-    )
-    query_in, key_in, value_in, query_out, key_out, value_out = grads_q
+        pieces_q,
+        [(0, 0, True), (0, 1, True), (0, 2, True), (0, 3, False)]
+        + [(1, 0, True), (1, 1, False), (1, 2, False), (1, 3, False)],
+        True,
+        [((D, AW), F32)] * 3
+        + [((AW, D), F32), ((QW, AW), F32), ((AW, QW), F32), ((AW, KW), F32), ((AW, KW), F32)],
+        "expand_qkv",
+    )
     return (
         out_rows.reshape(T, 1, D),
         input_rows.reshape(T, 1, D),

time: 261 us -> 189 us (0.72); the launches traced: 259 us -> 191 us
  waiting for transfers between devices: 79.9 us -> 51.8 us
  Pallas kernels: 99.5 us -> 80.2 us
  local copies, waits for them, and re-layouts: 9.83 us -> 1.1 us
  starting transfers between devices: 62.5 us -> 54 us
  other arithmetic: 5.59 us -> 2 us
    ppermute x46 -> x43, waiting for transfers between devices: 75.1 us -> 49.9 us  [permute(): return lax.ppermute(value, 'ctx', [(i, i ^ bits) for i in range(cfg.n)])]
    pallas_call x15, Pallas kernels: 99.5 us -> 80.2 us  [the longest x14 63.3 us: call(): pl.pallas_call(with_meta(kernel), out_shape=[jax.ShapeDtypeStruct(s, d) f...]
    ppermute x46 -> x43, starting transfers between devices: 61.1 us -> 52.8 us  [permute(): return lax.ppermute(value, 'ctx', [(i, i ^ bits) for i in range(cfg.n)])]
    unnamed x98 -> x78, local copies, waits for them, and re-layouts: 7.39 us -> 1.05 us
    ppermute x8, waiting for transfers between devices: 4.84 us -> 1.92 us  [swap_cores(): return lax.ppermute(value, 'wa', [(0, 1), (1, 0)])]
  transfers between devices with their start and end apart: 54 -> 51, of which waited for: 27 -> 19; matrix products, arithmetic and copies ran while one was open for 1% -> 0% of each run, Pallas kernels for 22% -> 30%
where the time goes in v2:
time: 189 us; the launch traced here: 191 us
  Pallas kernels  80.2 us (42%)
  starting transfers between devices  54 us (29%)
  waiting for transfers between devices  51.8 us (27%)
  other arithmetic  2 us (1%)
    pallas_call x14, Pallas kernels, call(): pl.pallas_call(with_meta(kernel), out_shape=[jax.ShapeDtypeStruct(s, d) f...  63.3 us
    ppermute x43, starting transfers between devices, permute(): return lax.ppermute(value, 'ctx', [(i, i ^ bits) for i in range(cfg.n)])  52.8 us
    ppermute x43, waiting for transfers between devices, permute(): return lax.ppermute(value, 'ctx', [(i, i ^ bits) for i in range(cfg.n)])  49.9 us
    pallas_call x1, Pallas kernels, ffn_call(): pl.pallas_call(with_meta(functools.partial(ffn_kernel, cfg, units, steps)...  16.9 us
  transfers between devices with their start and end apart: 51, of which 19 were waited for; matrix products, arithmetic and copies ran while one was open for 0% of the time, Pallas kernels for 30%

profile of v2, /device:TPU:0, one launch (start us, length us, event | category | flops | bytes accessed | tf_op | source)
XLA Modules:
  0.0 190.5 jit_solution(13803557265205800242)
XLA Ops:
  1.2 5.9 %pre.1 = (bf16[256,128]{1,0:T(8,128)(2,1)}, bf16[256,128]{1,0:T(8,128)(2,1)}, bf16[256,128]{1,0:T(8,128)(2,1)}, bf16[256,128]{1,0:T(8,128)(2,1)}, bf16[256,128]{...) custom-call(s32[4]{0:T(128)} %extra.29, ...), custom_call_target="tpu_custom_call" | custom-call | flops 6899999744 | tf_op jit(solution)/shard_map/pre/pallas_call | solution.py:153
  7.1 3.1 %collective-permute-start.3 = (bf16[256,128]{1,0:T(8,128)(2,1)}, bf16[256,128]{1,0:T(8,128)(2,1)S(1)}, u32[]{:S(2)}, u32[]{:S(2)}) collective-permute-start(bf16[256,128]{1,0:T(8,128)(2,1)} %get-tuple-element.124), channel_id=1, source_target_pairs={{0,8},{2,10},{4,12},{6,14},{8,0},{10,2},{12,4},{14,6},{16,24},{18,... | collective-permute-start | bytes 196616 | tf_op jit(solution)/shard_map/ppermute | solution.py:856
  10.2 2.6 %collective-permute-start.4 = (bf16[256,128]{1,0:T(8,128)(2,1)}, bf16[256,128]{1,0:T(8,128)(2,1)S(1)}, u32[]{:S(2)}, u32[]{:S(2)}) collective-permute-start(bf16[256,128]{1,0:T(8,128)(2,1)} %get-tuple-element.125), channel_id=1, source_target_pairs={{0,16},{2,18},{4,20},{6,22},{8,24},{10,26},{12,28},{14,30},{16,0},... | collective-permute-start | bytes 196616 | tf_op jit(solution)/shard_map/ppermute | solution.py:856
  12.8 4.9 %collective-permute-done.4 = bf16[256,128]{1,0:T(8,128)(2,1)S(1)} collective-permute-done((bf16[256,128]{1,0:T(8,128)(2,1)}, bf16[256,128]{1,0:T(8,128)(2,1)S(1)}, u32[]{:S(2)}, u32[]{:S(2)}) %collective-permute-start.4) | collective-permute-done | bytes 65568 | tf_op jit(solution)/shard_map/ppermute | solution.py:856
  20.0 2.5 %collective-permute-start.8 = (bf16[4,256,128]{2,1,0:T(8,128)(2,1)S(1)}, bf16[4,256,128]{2,1,0:T(8,128)(2,1)S(1)}, u32[]{:S(2)}, u32[]{:S(2)}) collective-permute-start(bf16[4,256,128]{2,1,0:T(8,128)(2,1)S(1)} %pad_maximum_fusion.1.refs_4_.refs_0_), channel_id=1, source_target_pairs={{0,6},{2,4},{4,2},{6,0},{8,14},{10,12},{12,10},{14,8},{16,22},{18,... | collective-permute-start | bytes 786440 | tf_op jit(solution)/shard_map/ppermute | solution.py:856
  23.5 2.3 %collective-permute-start.1 = (bf16[256,128]{1,0:T(8,128)(2,1)}, bf16[256,128]{1,0:T(8,128)(2,1)S(1)}, u32[]{:S(2)}, u32[]{:S(2)}) collective-permute-start(bf16[256,128]{1,0:T(8,128)(2,1)} %get-tuple-element.121), channel_id=1, source_target_pairs={{0,16},{2,18},{4,20},{6,22},{8,24},{10,26},{12,28},{14,30},{16,0},... | collective-permute-start | bytes 196616 | tf_op jit(solution)/shard_map/ppermute | solution.py:856
  25.9 2.1 %collective-permute-done.refs_1_ = bf16[256,128]{1,0:T(8,128)(2,1)S(1)} collective-permute-done((bf16[256,128]{1,0:T(8,128)(2,1)}, bf16[256,128]{1,0:T(8,128)(2,1)S(1)}, u32[]{:S(2)}, u32[]{:S(2)}) %collective-permute-start) | collective-permute-done | bytes 65568 | tf_op jit(solution)/shard_map/ppermute | solution.py:856
  29.8 4.5 %collective-permute-done.2.refs_3_ = bf16[256,128]{1,0:T(8,128)(2,1)S(1)} collective-permute-done((bf16[256,128]{1,0:T(8,128)(2,1)}, bf16[256,128]{1,0:T(8,128)(2,1)S(1)}, u32[]{:S(2)}, u32[]{:S(2)}) %collective-permute-start.2) | collective-permute-done | bytes 65568 | tf_op jit(solution)/shard_map/ppermute | solution.py:856
  35.2 11.3 %attend.1 = (bf16[256,128]{1,0:T(8,128)(2,1)S(1)}, bf16[256,128]{1,0:T(8,128)(2,1)S(1)}, bf16[256,128]{1,0:T(8,128)(2,1)S(1)}, bf16[256,128]{1,0:T(8,128)(2,1)S(...) custom-call(s32[4]{0:T(128)S(1)} %copy-done.27, s32[4]{0:T(128)S(1)} %copy-done.28, ...), custom_call_target="tpu_custom_call" | custom-call | flops 13799999488 | tf_op jit(solution)/shard_map/attend/pallas_call | solution.py:153
  46.6 2.3 %collective-permute-start.10 = (bf16[256,128]{1,0:T(8,128)(2,1)S(1)}, bf16[256,128]{1,0:T(8,128)(2,1)S(1)}, u32[]{:S(2)}, u32[]{:S(2)}) collective-permute-start(bf16[256,128]{1,0:T(8,128)(2,1)S(1)} %get-tuple-element.129), channel_id=1, source_target_pairs={{0,16},{2,18},{4,20},{6,22},{8,24},{10,26},{12,28},{14,30},{16,0},... | collective-permute-start | bytes 196616 | tf_op jit(solution)/shard_map/ppermute | solution.py:856
  48.9 2.0 %collective-permute-start.11 = (bf16[256,128]{1,0:T(8,128)(2,1)S(1)}, bf16[256,128]{1,0:T(8,128)(2,1)S(1)}, u32[]{:S(2)}, u32[]{:S(2)}) collective-permute-start(bf16[256,128]{1,0:T(8,128)(2,1)S(1)} %get-tuple-element.130), channel_id=1, source_target_pairs={{0,24},{2,26},{4,28},{6,30},{8,16},{10,18},{12,20},{14,22},{16,8},... | collective-permute-start | bytes 196616 | tf_op jit(solution)/shard_map/ppermute | solution.py:856
  50.9 2.4 %collective-permute-done.10.refs_2_.refs_7_ = bf16[256,128]{1,0:T(8,128)(2,1)S(1)} collective-permute-done((bf16[256,128]{1,0:T(8,128)(2,1)S(1)}, bf16[256,128]{1,0:T(8,128)(2,1)S(1)}, u32[]{:S(2)}, u32[]{:S(2)}) %collective-permute-start.10) | collective-permute-done | bytes 65568 | tf_op jit(solution)/shard_map/ppermute | solution.py:856
  56.3 2.5 %collective-permute-start.15 = (bf16[4,256,128]{2,1,0:T(8,128)(2,1)S(1)}, bf16[4,256,128]{2,1,0:T(8,128)(2,1)S(1)}, u32[]{:S(2)}, u32[]{:S(2)}) collective-permute-start(bf16[4,256,128]{2,1,0:T(8,128)(2,1)S(1)} %pad_maximum_fusion.2.refs_1_), channel_id=1, source_target_pairs={{0,6},{2,4},{4,2},{6,0},{8,14},{10,12},{12,10},{14,8},{16,22},{18,... | collective-permute-start | bytes 786440 | tf_op jit(solution)/shard_map/ppermute | solution.py:856
  60.0 16.9 %ffn.1 = (f32[256,1024]{1,0:T(8,128)S(1)}, bf16[256,1024]{1,0:T(8,128)(2,1)S(1)}, bf16[256,1152]{1,0:T(8,128)(2,1)S(1)}, bf16[256,64]{1,0:T(8,128)(2,1)S(1)}, bf...) custom-call(s32[4]{0:T(128)S(1)} %copy-done.27, ...), custom_call_target="tpu_custom_call" | custom-call | flops 21849999360 | tf_op jit(solution)/shard_map/ffn/pallas_call | solution.py:577
  77.0 1.9 collective-permute-done.16.refs_2_
  78.9 2.0 %mixed_grad.1 = (f32[256,1024]{1,0:T(8,128)S(1)}, bf16[2,64,512]{2,1,0:T(8,128)(2,1)S(1)}, bf16[256,128]{1,0:T(8,128)(2,1)S(1)}, bf16[256,128]{1,0:T(8,128)(2,1)...) custom-call(s32[4]{0:T(128)S(1)} %copy-done.27, s32[4]{0:T(128)S(1)} %copy-done.28, ...), custom_call_target="tpu_custom_call" | custom-call | flops 5175000064 | tf_op jit(solution)/shard_map/mixed_grad/pallas_call | solution.py:153
  84.9 6.6 %collective-permute-done.18 = bf16[78,16,128]{2,1,0:T(8,128)(2,1)S(1)} collective-permute-done((bf16[78,16,128]{2,1,0:T(8,128)(2,1)S(1)}, bf16[78,16,128]{2,1,0:T(8,128)(2,1)S(1)}, u32[]{:S(2)}, u32[]{:S(2)}) %collective-permute-start.18) | collective-permute-done | bytes 319520 | tf_op jit(solution)/shard_map/ppermute | solution.py:856
  95.8 3.3 %collective-permute-done.19 = bf16[78,16,128]{2,1,0:T(8,128)(2,1)S(1)} collective-permute-done((bf16[78,16,128]{2,1,0:T(8,128)(2,1)S(1)}, bf16[78,16,128]{2,1,0:T(8,128)(2,1)S(1)}, u32[]{:S(2)}, u32[]{:S(2)}) %collective-permute-start.19) | collective-permute-done | bytes 319520 | tf_op jit(solution)/shard_map/ppermute | solution.py:856
  104.9 13.1 %grad_query.1 = (bf16[256,128]{1,0:T(8,128)(2,1)S(1)}, bf16[256,128]{1,0:T(8,128)(2,1)S(1)}, bf16[256,128]{1,0:T(8,128)(2,1)S(1)}, bf16[256,128]{1,0:T(8,128)(2,1)S(1)}) custom-call(s32[4]{0:T(128)S(1)} %copy-done.27, s32[4]{0:T(128)S(1)} %copy-done.28, bf16[256,128]{1,0:T(8,128)(2,1)S(1)} %copy-done.1, bf16[256,128]{1,0:T(8,128)(2,1)S(1)} %collective-permute-done.refs_1_, ...), custom_call_target="tpu_custom_call" | custom-call | flops 15525000192 | tf_op jit(solution)/shard_map/grad_query/pallas_call | solution.py:153
  123.4 13.9 %grad_key.1 = (bf16[256,128]{1,0:T(8,128)(2,1)S(1)}, bf16[256,128]{1,0:T(8,128)(2,1)S(1)}, bf16[256,128]{1,0:T(8,128)(2,1)S(1)}, bf16[256,128]{1,0:T(8,128)(2,1)S(1)}) custom-call(s32[4]{0:T(128)S(1)} %copy-done.27, s32[4]{0:T(128)S(1)} %copy-done.28, bf16[4,256,128]{2,1,0:T(8,128)(2,1)S(1)} %pad_maximum_fusion.1.refs_4_.refs_0_, ...), custom_call_target="tpu_custom_call" | custom-call | flops 18400000000 | tf_op jit(solution)/shard_map/grad_key/pallas_call | solution.py:153
  137.4 2.9 %collective-permute-done.25 = bf16[78,16,128]{2,1,0:T(8,128)(2,1)S(1)} collective-permute-done((bf16[78,16,128]{2,1,0:T(8,128)(2,1)S(1)}, bf16[78,16,128]{2,1,0:T(8,128)(2,1)S(1)}, u32[]{:S(2)}, u32[]{:S(2)}) %collective-permute-start.25) | collective-permute-done | bytes 319520 | tf_op jit(solution)/shard_map/ppermute | solution.py:856
  143.0 2.4 %collective-permute-start.33 = (bf16[256,128]{1,0:T(8,128)(2,1)S(1)}, bf16[256,128]{1,0:T(8,128)(2,1)S(1)}, u32[]{:S(2)}, u32[]{:S(2)}) collective-permute-start(bf16[256,128]{1,0:T(8,128)(2,1)S(1)} %get-tuple-element.177), channel_id=1, source_target_pairs={{0,16},{2,18},{4,20},{6,22},{8,24},{10,26},{12,28},{14,30},{16,0},... | collective-permute-start | bytes 196616 | tf_op jit(solution)/shard_map/ppermute | solution.py:856
  145.4 2.0 %collective-permute-start.34 = (bf16[256,128]{1,0:T(8,128)(2,1)S(1)}, bf16[256,128]{1,0:T(8,128)(2,1)S(1)}, u32[]{:S(2)}, u32[]{:S(2)}) collective-permute-start(bf16[256,128]{1,0:T(8,128)(2,1)S(1)} %get-tuple-element.178), channel_id=1, source_target_pairs={{0,24},{2,26},{4,28},{6,30},{8,16},{10,18},{12,20},{14,22},{16,8},... | collective-permute-start | bytes 196616 | tf_op jit(solution)/shard_map/ppermute | solution.py:856
  147.6 2.4 %query_back.1 = (f32[256,1024]{1,0:T(8,128)S(1)}, bf16[64,512]{1,0:T(8,128)(2,1)S(1)}, bf16[64,512]{1,0:T(8,128)(2,1)S(1)}, bf16[64,512]{1,0:T(8,128)(2,1)S(1)}) custom-call(s32[4]{0:T(128)S(1)} %copy-done.27, s32[4]{0:T(128)S(1)} %copy-done.28, bf16[256,128]{1,0:T(8,128)(2,1)S(1)} %get-tuple-element.184.refs_0_, ...), custom_call_target="tpu_custom_call" | custom-call | flops 4024999936 | tf_op jit(solution)/shard_map/query_back/pallas_call | solution.py:153
  151.5 2.5 %key_value_back.1 = (bf16[256,1024]{1,0:T(8,128)(2,1)S(1)}, bf16[64,512]{1,0:T(8,128)(2,1)S(1)}, bf16[128,512]{1,0:T(8,128)(2,1)S(1)}, bf16[128,512]{1,0:T(8,128)(2,1)S(1)}) custom-call(s32[4]{0:T(128)S(1)} %copy-done.27, s32[4]{0:T(128)S(1)} %copy-done.28, bf16[256,128]{1,0:T(8,128)(2,1)S(1)} %get-tuple-element.175.refs_0_, ...), custom_call_target="tpu_custom_call" | custom-call | flops 5175000064 | tf_op jit(solution)/shard_map/key_value_back/pallas_call | solution.py:153
  161.3 2.5 %collective-permute-done.41 = bf16[28,16,128]{2,1,0:T(8,128)(2,1)S(1)} collective-permute-done((bf16[28,16,128]{2,1,0:T(8,128)(2,1)S(1)}, bf16[28,16,128]{2,1,0:T(8,128)(2,1)S(1)}, u32[]{:S(2)}, u32[]{:S(2)}) %collective-permute-start.41) | collective-permute-done | bytes 114720 | tf_op jit(solution)/shard_map/ppermute | solution.py:856
  163.8 2.0 %collective-permute-done.42 = bf16[28,16,128]{2,1,0:T(8,128)(2,1)S(1)} collective-permute-done((bf16[28,16,128]{2,1,0:T(8,128)(2,1)S(1)}, bf16[28,16,128]{2,1,0:T(8,128)(2,1)S(1)}, u32[]{:S(2)}, u32[]{:S(2)}) %collective-permute-start.42) | collective-permute-done | bytes 114720 | tf_op jit(solution)/shard_map/ppermute | solution.py:856
  166.1 6.5 %collective-permute-done.44 = bf16[28,16,128]{2,1,0:T(8,128)(2,1)S(1)} collective-permute-done((bf16[28,16,128]{2,1,0:T(8,128)(2,1)S(1)}, bf16[28,16,128]{2,1,0:T(8,128)(2,1)S(1)}, u32[]{:S(2)}, u32[]{:S(2)}) %collective-permute-start.44) | collective-permute-done | bytes 114720 | tf_op jit(solution)/shard_map/ppermute | solution.py:856
  174.6 2.9 %collective-permute-done.45 = bf16[28,16,128]{2,1,0:T(8,128)(2,1)S(1)} collective-permute-done((bf16[28,16,128]{2,1,0:T(8,128)(2,1)S(1)}, bf16[28,16,128]{2,1,0:T(8,128)(2,1)S(1)}, u32[]{:S(2)}, u32[]{:S(2)}) %collective-permute-start.45) | collective-permute-done | bytes 114720 | tf_op jit(solution)/shard_map/ppermute | solution.py:856
  181.1 2.3 %collective-permute-done.48.refs_3_ = bf16[28,16,128]{2,1,0:T(8,128)(2,1)S(1)} collective-permute-done((bf16[28,16,128]{2,1,0:T(8,128)(2,1)S(1)}, bf16[28,16,128]{2,1,0:T(8,128)(2,1)S(1)}, u32[]{:S(2)}, u32[]{:S(2)}) %collective-permute-start.48) | collective-permute-done | bytes 114720 | tf_op jit(solution)/shard_map/ppermute | solution.py:856
  184.7 3.3 %expand_ffn.1 = (f32[1024,128]{1,0:T(8,128)}, f32[1024,128]{1,0:T(8,128)}, f32[128,1024]{1,0:T(8,128)}, f32[128,2304]{1,0:T(8,128)}, f32[128,2304]{1,0:T(8,128)}, /*index=5*/f32[2304,128]{1,0:T(8,128)}) custom-call(s32[4]{0:T(128)S(1)} %copy-done.27, s32[4]{0:T(128)S(1)} %copy-done.28, bf16[78,16,128]{2,1,0:T(8,128)(2,1)S(1)} %add_convert_fusion.refs_0_, ...), custom_call_target="tpu_custom_call" | custom-call | flops 4600000000 | tf_op jit(solution)/shard_map/expand_ffn/pallas_call | solution.py:153
  188.0 2.5 %expand_qkv.1 = (f32[1024,128]{1,0:T(8,128)}, f32[1024,128]{1,0:T(8,128)}, f32[1024,128]{1,0:T(8,128)}, f32[128,1024]{1,0:T(8,128)}, f32[512,128]{1,0:T(8,128)},...) custom-call(s32[4]{0:T(128)S(1)} %copy-done.27, s32[4]{0:T(128)S(1)} %copy-done.28, ...), custom_call_target="tpu_custom_call" | custom-call | flops 4600000000 | tf_op jit(solution)/shard_map/expand_qkv/pallas_call | solution.py:153
  (182 shorter events, 48.6 us)
Async XLA Ops:
  10.2 7.5 %collective-permute-start.4 = (bf16[256,128]{1,0:T(8,128)(2,1)}, bf16[256,128]{1,0:T(8,128)(2,1)S(1)}, u32[]{:S(2)}, u32[]{:S(2)}) collective-permute-start(bf16[256,128]{1,0:T(8,128)(2,1)} %get-tuple-element.125), channel_id=1, source_target_pairs={{0,16},{2,18},{4,20},{6,22},{8,24},{10,26},{12,28},{14,30},{16,0},... | collective-permute-start | bytes 196616 | tf_op jit(solution)/shard_map/ppermute | solution.py:856
  20.0 14.3 %collective-permute-start.8 = (bf16[4,256,128]{2,1,0:T(8,128)(2,1)S(1)}, bf16[4,256,128]{2,1,0:T(8,128)(2,1)S(1)}, u32[]{:S(2)}, u32[]{:S(2)}) collective-permute-start(bf16[4,256,128]{2,1,0:T(8,128)(2,1)S(1)} %pad_maximum_fusion.1.refs_4_.refs_0_), channel_id=1, source_target_pairs={{0,6},{2,4},{4,2},{6,0},{8,14},{10,12},{12,10},{14,8},{16,22},{18,... | collective-permute-start | bytes 786440 | tf_op jit(solution)/shard_map/ppermute | solution.py:856
  22.5 11.8 %collective-permute-start.7 = (bf16[4,256,128]{2,1,0:T(8,128)(2,1)S(1)}, bf16[4,256,128]{2,1,0:T(8,128)(2,1)S(1)}, u32[]{:S(2)}, u32[]{:S(2)}) collective-permute-start(bf16[4,256,128]{2,1,0:T(8,128)(2,1)S(1)} %pad_maximum_fusion.1.refs_4_.refs_0_), channel_id=1, source_target_pairs={{0,4},{2,6},{4,0},{6,2},{8,12},{10,14},{12,8},{14,10},{16,20},{18,... | collective-permute-start | bytes 786440 | tf_op jit(solution)/shard_map/ppermute | solution.py:856
  23.0 11.3 %collective-permute-start.6 = (bf16[4,256,128]{2,1,0:T(8,128)(2,1)S(1)}, bf16[4,256,128]{2,1,0:T(8,128)(2,1)S(1)}, u32[]{:S(2)}, u32[]{:S(2)}) collective-permute-start(bf16[4,256,128]{2,1,0:T(8,128)(2,1)S(1)} %pad_maximum_fusion.1.refs_4_.refs_0_), channel_id=1, source_target_pairs={{0,2},{2,0},{4,6},{6,4},{8,10},{10,8},{12,14},{14,12},{16,18},{18,... | collective-permute-start | bytes 786440 | tf_op jit(solution)/shard_map/ppermute | solution.py:856
  46.6 6.8 %collective-permute-start.10 = (bf16[256,128]{1,0:T(8,128)(2,1)S(1)}, bf16[256,128]{1,0:T(8,128)(2,1)S(1)}, u32[]{:S(2)}, u32[]{:S(2)}) collective-permute-start(bf16[256,128]{1,0:T(8,128)(2,1)S(1)} %get-tuple-element.129), channel_id=1, source_target_pairs={{0,16},{2,18},{4,20},{6,22},{8,24},{10,26},{12,28},{14,30},{16,0},... | collective-permute-start | bytes 196616 | tf_op jit(solution)/shard_map/ppermute | solution.py:856
  56.3 20.6 %collective-permute-start.15 = (bf16[4,256,128]{2,1,0:T(8,128)(2,1)S(1)}, bf16[4,256,128]{2,1,0:T(8,128)(2,1)S(1)}, u32[]{:S(2)}, u32[]{:S(2)}) collective-permute-start(bf16[4,256,128]{2,1,0:T(8,128)(2,1)S(1)} %pad_maximum_fusion.2.refs_1_), channel_id=1, source_target_pairs={{0,6},{2,4},{4,2},{6,0},{8,14},{10,12},{12,10},{14,8},{16,22},{18,... | collective-permute-start | bytes 786440 | tf_op jit(solution)/shard_map/ppermute | solution.py:856
  58.8 18.1 %collective-permute-start.14 = (bf16[4,256,128]{2,1,0:T(8,128)(2,1)S(1)}, bf16[4,256,128]{2,1,0:T(8,128)(2,1)S(1)}, u32[]{:S(2)}, u32[]{:S(2)}) collective-permute-start(bf16[4,256,128]{2,1,0:T(8,128)(2,1)S(1)} %pad_maximum_fusion.2.refs_1_), channel_id=1, source_target_pairs={{0,4},{2,6},{4,0},{6,2},{8,12},{10,14},{12,8},{14,10},{16,20},{18,... | collective-permute-start | bytes 786440 | tf_op jit(solution)/shard_map/ppermute | solution.py:856
  59.5 17.5 %collective-permute-start.13 = (bf16[4,256,128]{2,1,0:T(8,128)(2,1)S(1)}, bf16[4,256,128]{2,1,0:T(8,128)(2,1)S(1)}, u32[]{:S(2)}, u32[]{:S(2)}) collective-permute-start(bf16[4,256,128]{2,1,0:T(8,128)(2,1)S(1)} %pad_maximum_fusion.2.refs_1_), channel_id=1, source_target_pairs={{0,2},{2,0},{4,6},{6,4},{8,10},{10,8},{12,14},{14,12},{16,18},{18,... | collective-permute-start | bytes 786440 | tf_op jit(solution)/shard_map/ppermute | solution.py:856
  80.9 11.8 %collective-permute-start.17 = (bf16[256,1152]{1,0:T(8,128)(2,1)S(1)}, bf16[256,1152]{1,0:T(8,128)(2,1)S(1)}, u32[]{:S(2)}, u32[]{:S(2)}) collective-permute-start(bf16[256,1152]{1,0:T(8,128)(2,1)S(1)} %get-tuple-element.138.refs_1_), channel_id=1, source_target_pairs={{0,1},{1,0},{2,3},{3,2},{4,5},{5,4},{6,7},{7,6},{8,9},{9,8},{10,11... | collective-permute-start | bytes 1769480 | tf_op jit(solution)/shard_map/ppermute | solution.py:852
  81.1 10.4 %collective-permute-start.18 = (bf16[78,16,128]{2,1,0:T(8,128)(2,1)S(1)}, bf16[78,16,128]{2,1,0:T(8,128)(2,1)S(1)}, u32[]{:S(2)}, u32[]{:S(2)}) collective-permute-start(bf16[78,16,128]{2,1,0:T(8,128)(2,1)S(1)} %get-tuple-element.140), channel_id=1, source_target_pairs={{0,2},{2,0},{4,6},{6,4},{8,10},{10,8},{12,14},{14,12},{16,18},{18,... | collective-permute-start | bytes 958472 | tf_op jit(solution)/shard_map/ppermute | solution.py:856
  82.7 16.4 %collective-permute-start.19 = (bf16[78,16,128]{2,1,0:T(8,128)(2,1)S(1)}, bf16[78,16,128]{2,1,0:T(8,128)(2,1)S(1)}, u32[]{:S(2)}, u32[]{:S(2)}) collective-permute-start(bf16[78,16,128]{2,1,0:T(8,128)(2,1)S(1)} %get-tuple-element.141), channel_id=1, source_target_pairs={{0,4},{2,6},{4,0},{6,2},{8,12},{10,14},{12,8},{14,10},{16,20},{18,... | collective-permute-start | bytes 958472 | tf_op jit(solution)/shard_map/ppermute | solution.py:856
  84.2 15.0 %collective-permute-start.20 = (bf16[78,16,128]{2,1,0:T(8,128)(2,1)S(1)}, bf16[78,16,128]{2,1,0:T(8,128)(2,1)S(1)}, u32[]{:S(2)}, u32[]{:S(2)}) collective-permute-start(bf16[78,16,128]{2,1,0:T(8,128)(2,1)S(1)} %get-tuple-element.142), channel_id=1, source_target_pairs={{0,6},{2,4},{4,2},{6,0},{8,14},{10,12},{12,10},{14,8},{16,22},{18,... | collective-permute-start | bytes 958472 | tf_op jit(solution)/shard_map/ppermute | solution.py:856
  84.6 14.5 %collective-permute-start.21 = (bf16[256,128]{1,0:T(8,128)(2,1)S(1)}, bf16[256,128]{1,0:T(8,128)(2,1)S(1)}, u32[]{:S(2)}, u32[]{:S(2)}) collective-permute-start(bf16[256,128]{1,0:T(8,128)(2,1)S(1)} %get-tuple-element.143), channel_id=1, source_target_pairs={{0,8},{2,10},{4,12},{6,14},{8,0},{10,2},{12,4},{14,6},{16,24},{18,... | collective-permute-start | bytes 196616 | tf_op jit(solution)/shard_map/ppermute | solution.py:856
  91.5 7.6 %collective-permute-start.22 = (bf16[256,128]{1,0:T(8,128)(2,1)S(1)}, bf16[256,128]{1,0:T(8,128)(2,1)S(1)}, u32[]{:S(2)}, u32[]{:S(2)}) collective-permute-start(bf16[256,128]{1,0:T(8,128)(2,1)S(1)} %get-tuple-element.144), channel_id=1, source_target_pairs={{0,16},{2,18},{4,20},{6,22},{8,24},{10,26},{12,28},{14,30},{16,0},... | collective-permute-start | bytes 196616 | tf_op jit(solution)/shard_map/ppermute | solution.py:856
  92.8 6.4 %collective-permute-start.23 = (bf16[256,128]{1,0:T(8,128)(2,1)S(1)}, bf16[256,128]{1,0:T(8,128)(2,1)S(1)}, u32[]{:S(2)}, u32[]{:S(2)}) collective-permute-start(bf16[256,128]{1,0:T(8,128)(2,1)S(1)} %get-tuple-element.145), channel_id=1, source_target_pairs={{0,24},{2,26},{4,28},{6,30},{8,16},{10,18},{12,20},{14,22},{16,8},... | collective-permute-start | bytes 196616 | tf_op jit(solution)/shard_map/ppermute | solution.py:856
  100.1 20.9 %collective-permute-start.31 = (bf16[1056,128]{1,0:T(8,128)(2,1)S(1)}, bf16[1056,128]{1,0:T(8,128)(2,1)S(1)}, u32[]{:S(2)}, u32[]{:S(2)}) collective-permute-start(bf16[1056,128]{1,0:T(8,128)(2,1)S(1)} %scale.1.refs_8_.refs_5_), channel_id=1, source_target_pairs={{0,6},{2,4},{4,2},{6,0},{8,14},{10,12},{12,10},{14,8},{16,22},{18,... | collective-permute-start | bytes 811016 | tf_op jit(solution)/shard_map/ppermute | solution.py:856
  101.8 21.0 %collective-permute-start.30 = (bf16[1056,128]{1,0:T(8,128)(2,1)S(1)}, bf16[1056,128]{1,0:T(8,128)(2,1)S(1)}, u32[]{:S(2)}, u32[]{:S(2)}) collective-permute-start(bf16[1056,128]{1,0:T(8,128)(2,1)S(1)} %scale.1.refs_8_.refs_5_), channel_id=1, source_target_pairs={{0,4},{2,6},{4,0},{6,2},{8,12},{10,14},{12,8},{14,10},{16,20},{18,... | collective-permute-start | bytes 811016 | tf_op jit(solution)/shard_map/ppermute | solution.py:856
  103.1 20.4 %collective-permute-start.29 = (bf16[1056,128]{1,0:T(8,128)(2,1)S(1)}, bf16[1056,128]{1,0:T(8,128)(2,1)S(1)}, u32[]{:S(2)}, u32[]{:S(2)}) collective-permute-start(bf16[1056,128]{1,0:T(8,128)(2,1)S(1)} %scale.1.refs_8_.refs_5_), channel_id=1, source_target_pairs={{0,2},{2,0},{4,6},{6,4},{8,10},{10,8},{12,14},{14,12},{16,18},{18,... | collective-permute-start | bytes 811016 | tf_op jit(solution)/shard_map/ppermute | solution.py:856
  103.8 14.3 %collective-permute-start.24 = (bf16[78,16,128]{2,1,0:T(8,128)(2,1)S(1)}, bf16[78,16,128]{2,1,0:T(8,128)(2,1)S(1)}, u32[]{:S(2)}, u32[]{:S(2)}) collective-permute-start(bf16[78,16,128]{2,1,0:T(8,128)(2,1)S(1)} %add_convert_fusion.2), channel_id=1, source_target_pairs={{0,8},{2,10},{4,12},{6,14},{8,0},{10,2},{12,4},{14,6},{16,24},{18,... | collective-permute-start | bytes 958472 | tf_op jit(solution)/shard_map/ppermute | solution.py:856
  118.0 19.4 %collective-permute-start.26 = (bf16[256,128]{1,0:T(8,128)(2,1)S(1)}, bf16[256,128]{1,0:T(8,128)(2,1)S(1)}, u32[]{:S(2)}, u32[]{:S(2)}) collective-permute-start(bf16[256,128]{1,0:T(8,128)(2,1)S(1)} %get-tuple-element.164), channel_id=1, source_target_pairs={{0,8},{2,10},{4,12},{6,14},{8,0},{10,2},{12,4},{14,6},{16,24},{18,... | collective-permute-start | bytes 196616 | tf_op jit(solution)/shard_map/ppermute | solution.py:856
  119.1 18.3 %collective-permute-start.27 = (bf16[256,128]{1,0:T(8,128)(2,1)S(1)}, bf16[256,128]{1,0:T(8,128)(2,1)S(1)}, u32[]{:S(2)}, u32[]{:S(2)}) collective-permute-start(bf16[256,128]{1,0:T(8,128)(2,1)S(1)} %get-tuple-element.165), channel_id=1, source_target_pairs={{0,16},{2,18},{4,20},{6,22},{8,24},{10,26},{12,28},{14,30},{16,0},... | collective-permute-start | bytes 196616 | tf_op jit(solution)/shard_map/ppermute | solution.py:856
  121.0 16.4 %collective-permute-start.28 = (bf16[256,128]{1,0:T(8,128)(2,1)S(1)}, bf16[256,128]{1,0:T(8,128)(2,1)S(1)}, u32[]{:S(2)}, u32[]{:S(2)}) collective-permute-start(bf16[256,128]{1,0:T(8,128)(2,1)S(1)} %get-tuple-element.166), channel_id=1, source_target_pairs={{0,24},{2,26},{4,28},{6,30},{8,16},{10,18},{12,20},{14,22},{16,8},... | collective-permute-start | bytes 196616 | tf_op jit(solution)/shard_map/ppermute | solution.py:856
  122.8 17.6 %collective-permute-start.25 = (bf16[78,16,128]{2,1,0:T(8,128)(2,1)S(1)}, bf16[78,16,128]{2,1,0:T(8,128)(2,1)S(1)}, u32[]{:S(2)}, u32[]{:S(2)}) collective-permute-start(bf16[78,16,128]{2,1,0:T(8,128)(2,1)S(1)} %add_convert_fusion.1), channel_id=1, source_target_pairs={{0,16},{2,18},{4,20},{6,22},{8,24},{10,26},{12,28},{14,30},{16,0},... | collective-permute-start | bytes 958472 | tf_op jit(solution)/shard_map/ppermute | solution.py:856
  140.4 14.2 %collective-permute-start.40 = (bf16[78,16,128]{2,1,0:T(8,128)(2,1)S(1)}, bf16[78,16,128]{2,1,0:T(8,128)(2,1)S(1)}, u32[]{:S(2)}, u32[]{:S(2)}) collective-permute-start(bf16[78,16,128]{2,1,0:T(8,128)(2,1)S(1)} %add_convert_fusion.refs_0_), channel_id=1, source_target_pairs={{0,6},{2,4},{4,2},{6,0},{8,14},{10,12},{12,10},{14,8},{16,22},{18,... | collective-permute-start | bytes 958472 | tf_op jit(solution)/shard_map/ppermute | solution.py:856
  142.3 14.0 %collective-permute-start.39 = (bf16[78,16,128]{2,1,0:T(8,128)(2,1)S(1)}, bf16[78,16,128]{2,1,0:T(8,128)(2,1)S(1)}, u32[]{:S(2)}, u32[]{:S(2)}) collective-permute-start(bf16[78,16,128]{2,1,0:T(8,128)(2,1)S(1)} %add_convert_fusion.refs_0_), channel_id=1, source_target_pairs={{0,4},{2,6},{4,0},{6,2},{8,12},{10,14},{12,8},{14,10},{16,20},{18,... | collective-permute-start | bytes 958472 | tf_op jit(solution)/shard_map/ppermute | solution.py:856
  143.0 7.0 %collective-permute-start.32 = (bf16[256,128]{1,0:T(8,128)(2,1)S(1)}, bf16[256,128]{1,0:T(8,128)(2,1)S(1)}, u32[]{:S(2)}, u32[]{:S(2)}) collective-permute-start(bf16[256,128]{1,0:T(8,128)(2,1)S(1)} %get-tuple-element.176), channel_id=1, source_target_pairs={{0,8},{2,10},{4,12},{6,14},{8,0},{10,2},{12,4},{14,6},{16,24},{18,... | collective-permute-start | bytes 196616 | tf_op jit(solution)/shard_map/ppermute | solution.py:856
  143.0 8.0 %collective-permute-start.33 = (bf16[256,128]{1,0:T(8,128)(2,1)S(1)}, bf16[256,128]{1,0:T(8,128)(2,1)S(1)}, u32[]{:S(2)}, u32[]{:S(2)}) collective-permute-start(bf16[256,128]{1,0:T(8,128)(2,1)S(1)} %get-tuple-element.177), channel_id=1, source_target_pairs={{0,16},{2,18},{4,20},{6,22},{8,24},{10,26},{12,28},{14,30},{16,0},... | collective-permute-start | bytes 196616 | tf_op jit(solution)/shard_map/ppermute | solution.py:856
  150.0 7.1 %collective-permute-start.38 = (bf16[78,16,128]{2,1,0:T(8,128)(2,1)S(1)}, bf16[78,16,128]{2,1,0:T(8,128)(2,1)S(1)}, u32[]{:S(2)}, u32[]{:S(2)}) collective-permute-start(bf16[78,16,128]{2,1,0:T(8,128)(2,1)S(1)} %add_convert_fusion.refs_0_), channel_id=1, source_target_pairs={{0,2},{2,0},{4,6},{6,4},{8,10},{10,8},{12,14},{14,12},{16,18},{18,... | collective-permute-start | bytes 958472 | tf_op jit(solution)/shard_map/ppermute | solution.py:856
  154.6 18.1 %collective-permute-start.35 = (bf16[256,1024]{1,0:T(8,128)(2,1)S(1)}, bf16[256,1024]{1,0:T(8,128)(2,1)S(1)}, u32[]{:S(2)}, u32[]{:S(2)}) collective-permute-start(bf16[256,1024]{1,0:T(8,128)(2,1)S(1)} %get-tuple-element.190.refs_3_), channel_id=1, source_target_pairs={{0,1},{1,0},{2,3},{3,2},{4,5},{5,4},{6,7},{7,6},{8,9},{9,8},{10,11... | collective-permute-start | bytes 1572872 | tf_op jit(solution)/shard_map/ppermute | solution.py:852
  158.7 7.1 %collective-permute-start.42 = (bf16[28,16,128]{2,1,0:T(8,128)(2,1)S(1)}, bf16[28,16,128]{2,1,0:T(8,128)(2,1)S(1)}, u32[]{:S(2)}, u32[]{:S(2)}) collective-permute-start(bf16[28,16,128]{2,1,0:T(8,128)(2,1)S(1)} %get-tuple-element.202), channel_id=1, source_target_pairs={{0,4},{2,6},{4,0},{6,2},{8,12},{10,14},{12,8},{14,10},{16,20},{18,... | collective-permute-start | bytes 344072 | tf_op jit(solution)/shard_map/ppermute | solution.py:856
  165.9 6.7 %collective-permute-start.44 = (bf16[28,16,128]{2,1,0:T(8,128)(2,1)S(1)}, bf16[28,16,128]{2,1,0:T(8,128)(2,1)S(1)}, u32[]{:S(2)}, u32[]{:S(2)}) collective-permute-start(bf16[28,16,128]{2,1,0:T(8,128)(2,1)S(1)} %add_convert_fusion.5), channel_id=1, source_target_pairs={{0,16},{2,18},{4,20},{6,22},{8,24},{10,26},{12,28},{14,30},{16,0},... | collective-permute-start | bytes 344072 | tf_op jit(solution)/shard_map/ppermute | solution.py:856
  166.1 18.6 %collective-permute-start.50 = (bf16[4,24,16,128]{3,2,1,0:T(8,128)(2,1)S(1)}, bf16[4,24,16,128]{3,2,1,0:T(8,128)(2,1)S(1)}, u32[]{:S(2)}, u32[]{:S(2)}) collective-permute-start(bf16[4,24,16,128]{3,2,1,0:T(8,128)(2,1)S(1)} %pad_maximum_fusion), channel_id=1, source_target_pairs={{0,1},{1,0},{2,3},{3,2},{4,5},{5,4},{6,7},{7,6},{8,9},{9,8},{10,11... | collective-permute-start | bytes 1179656 | tf_op jit(solution)/shard_map/ppermute | solution.py:852
  (58 other events, 709.9 us)

commit v3 on v2

--- a/solution.py
+++ b/solution.py
@@ -3,6 +3,7 @@
 
 import jax
 import jax.numpy as jnp
+import numpy as np
 from jax import lax
 from jax.experimental import pallas as pl
 from jax.experimental.pallas import tpu as pltpu
@@ -16,7 +17,8 @@
 BF = jnp.bfloat16
 F32 = jnp.float32
 LOG2E = 1.4426950408889634
-VMEM_SMALL = 20 * 1024 * 1024
+STEP = 3
+VMEM_SMALL = 28 * 1024 * 1024
 VMEM_LARGE = 56 * 1024 * 1024
 
 
@@ -209,11 +211,29 @@
         q_out[k][...] = q_scr[hi ^ k]
 
 
-def load_tiles(cfg, scr, pieces):
-    R = cfg.R
-    for p, piece in enumerate(pieces):
-        for t in range(cfg.NT):
-            scr[t, p * R : (p + 1) * R, :] = piece[t * R : (t + 1) * R, :]
+def tile_of(cfg, pieces, t):
+    rows = pl.ds(pl.multiple_of(t * cfg.R, cfg.R), cfg.R)
+    return jnp.concatenate([piece[rows, :] for piece in pieces], axis=0)
+
+
+def list_items(cfg, starts, items):
+    def per_query(qt, count):
+        def one(s, at):
+            items[0, at] = qt
+            items[1, at] = s
+            return at + 1
+
+        return lax.fori_loop(start_of(starts, qt * cfg.span) // cfg.span, qt + 1, one, count)
+
+    count = lax.fori_loop(0, cfg.NT, per_query, 0)
+    for i in range(STEP - 1):
+        items[0, count + i] = 0
+        items[1, count + i] = cfg.NT - 1
+    return (count + STEP - 1) // STEP
+
+
+def items_scratch(cfg):
+    return pltpu.SMEM((2, cfg.NT * (cfg.NT + 1) // 2 + STEP), jnp.int32)
 
 
 def split_pieces(ref, count):
@@ -243,68 +263,53 @@
     return jnp.concatenate(parts, axis=0).astype(BF)
 
 
-def query_tile_ranges(cfg, starts, qt):
-    first = qt * cfg.span
-    s_lo = start_of(starts, first) // cfg.span
-    s_full = (start_of(starts, first + cfg.span - 1) + cfg.span - 1) // cfg.span
-    return s_lo, jnp.minimum(s_full, qt)
-
-
 def attend_kernel(cfg, meta, *refs):
-    G, T, R, hd = cfg.G, cfg.T, cfg.R, cfg.hd
+    G, R, hd, QH = cfg.G, cfg.R, cfg.hd, cfg.QH
     q_in, own, others = refs[:G], refs[G], refs[G + 1 : G + cfg.lo]
     rest = refs[G + cfg.lo :]
-    o_out, o_all, linv, kv_scr, va_scr, q_scr = rest[:G], *rest[G:]
-    pieces = split_pieces(own, G)
+    o_out, o_all, linv, q_scr, acc_scr, items = rest[:G], *rest[G:]
+    kv_pieces = split_pieces(own, G)
     for ref in others:
-        pieces = pieces + split_pieces(ref, G)
-    load_tiles(cfg, kv_scr, pieces)
-    load_tiles(cfg, q_scr, q_in)
+        kv_pieces = kv_pieces + split_pieces(ref, G)
     starts = doc_starts(cfg, meta)
-    QH = cfg.QH
+    steps = list_items(cfg, starts, items)
     scale = hd ** (-0.5) * LOG2E
     key_off = token_in_span(cfg, meta, iota((1, cfg.KT), 1))
     row_off = token_in_span(cfg, meta, iota((2 * QH, 1), 0) % QH)
-    lane_first = iota((cfg.KT, 2 * hd), 1) < hd
-
-    def fill(t, carry):
-        va_scr[t] = jnp.where(lane_first, 1.0, kv_scr[t].astype(F32)).astype(BF)
+    key_lanes = iota((cfg.KT, 2 * hd), 1) < hd
+    for t in range(cfg.NT):
+        q_scr[t] = pad_queries(cfg, tile_of(cfg, q_in, t), 0)
+        acc_scr[t] = jnp.zeros((2 * QH, 2 * hd), F32)
+
+    def step(i, carry):
+        parts = []
+        for u in range(STEP):
+            qt, s = items[0, i * STEP + u], items[1, i * STEP + u]
+            kv = tile_of(cfg, kv_pieces, s)
+            token = row_off + qt * cfg.span
+            key_token = key_off + s * cfg.span
+            e = jnp.exp2(mm_nt(q_scr[qt], kv) * scale)
+            e = jnp.where((key_token <= token) & (key_token >= start_of(starts, token)), e, 0.0)
+            parts.append((qt, mm(e.astype(BF), jnp.where(key_lanes, jnp.ones_like(kv), kv))))
+        for qt, part in parts:
+            acc_scr[qt] += part
         return carry
 
-    lax.fori_loop(0, cfg.NT, fill, 0)
+    lax.fori_loop(0, steps, step, 0)
     half = iota((QH, 2 * hd), 1) < hd
-
-    def query_tile(qt, carry):
-        queries = pad_queries(cfg, q_scr[qt], 0)
-        token = row_off + qt * cfg.span
-        first_key = start_of(starts, token)
-        s_lo, s_full = query_tile_ranges(cfg, starts, qt)
-
-        def tile(s, acc, masked):
-            e = jnp.exp2(mm_nt(queries, kv_scr[s]) * scale)
-            if masked:
-                key_token = key_off + s * cfg.span
-                e = jnp.where((key_token <= token) & (key_token >= first_key), e, 0.0)
-            return acc + mm(e.astype(BF), va_scr[s])
-
-        acc = jnp.zeros((2 * QH, 2 * hd), F32)
-        acc = lax.fori_loop(s_lo, s_full, lambda s, a: tile(s, a, True), acc)
-        acc = lax.fori_loop(s_full, qt, lambda s, a: tile(s, a, False), acc)
-        acc = tile(qt, acc, True)
+    for t in range(cfg.NT):
+        acc = acc_scr[t]
         inv0 = 1.0 / acc[:QH]
         inv1 = 1.0 / acc[QH:]
         out0 = pltpu.roll(acc[:QH], hd, 1) * inv0
         out1 = acc[QH:] * pltpu.roll(inv1, hd, 1)
         out = jnp.where(half, out0, out1).astype(BF)
         inv = jnp.where(half, inv0, pltpu.roll(inv1, hd, 1))
-        rows = pl.ds(pl.multiple_of(qt * R, R), R)
+        rows = slice(t * R, (t + 1) * R)
         for k in range(G):
             o_out[k][rows, :] = out[k * R : (k + 1) * R]
             o_all[k, rows, :] = out[k * R : (k + 1) * R]
             linv[k, rows, :] = inv[k * R : (k + 1) * R]
-        return carry
-
-    lax.fori_loop(0, cfg.NT, query_tile, 0)
 
 
 def head_sums(cfg, prod):
@@ -336,74 +341,63 @@
 
 
 def grad_query_kernel(cfg, meta, *refs):
-    G, T, R, hd = cfg.G, cfg.T, cfg.R, cfg.hd
+    G, R, hd, QH = cfg.G, cfg.R, cfg.hd, cfg.QH
     q_in, own, others = refs[:G], refs[G], refs[G + 1 : G + cfg.lo]
     go_ref, o_ref = refs[G + cfg.lo : G + cfg.lo + 2]
     rest = refs[G + cfg.lo + 2 :]
-    dq_out, kv_scr, q_scr, go_scr, o_scr = rest[:G], *rest[G:]
-    pieces = split_pieces(own, G)
+    dq_out, q_scr, go_scr, delta_scr, acc_scr, items = rest[:G], *rest[G:]
+    kv_pieces = split_pieces(own, G)
     for ref in others:
-        pieces = pieces + split_pieces(ref, G)
-    load_tiles(cfg, kv_scr, pieces)
-    load_tiles(cfg, q_scr, q_in)
-    load_tiles(cfg, go_scr, message_pieces(cfg, go_ref))
-    load_tiles(cfg, o_scr, split_pieces(o_ref, G))
+        kv_pieces = kv_pieces + split_pieces(ref, G)
     starts = doc_starts(cfg, meta)
-    QH = cfg.QH
+    steps = list_items(cfg, starts, items)
     scale = hd ** (-0.5) * LOG2E
     key_off = token_in_span(cfg, meta, iota((1, cfg.KT), 1))
     row_off = token_in_span(cfg, meta, iota((2 * QH, 1), 0) % QH)
     half = iota((QH, 2 * hd), 1) < hd
-
-    def query_tile(qt, carry):
-        queries = pad_queries(cfg, q_scr[qt], 0)
-        grads = pad_queries(cfg, go_scr[qt], 1)
-        prod = go_scr[qt].astype(F32) * o_scr[qt].astype(F32)
-        delta = jnp.concatenate(
-            [
-                jnp.sum(jnp.where(half, prod, 0.0), axis=1, keepdims=True),
-                jnp.sum(jnp.where(half, 0.0, prod), axis=1, keepdims=True),
-            ],
-            axis=0,
-        )
-        token = row_off + qt * cfg.span
-        first_key = start_of(starts, token)
-        s_lo, s_full = query_tile_ranges(cfg, starts, qt)
-
-        def tile(s, acc, masked):
-            kv = kv_scr[s]
-            e = jnp.exp2(mm_nt(queries, kv) * scale)
-            if masked:
-                key_token = key_off + s * cfg.span
-                e = jnp.where((key_token <= token) & (key_token >= first_key), e, 0.0)
-            ds = e * (mm_nt(grads, kv) - delta)
-            return acc + mm(ds.astype(BF), kv)
-
-        acc = jnp.zeros((2 * QH, 2 * hd), F32)
-        acc = lax.fori_loop(s_lo, s_full, lambda s, a: tile(s, a, True), acc)
-        acc = lax.fori_loop(s_full, qt, lambda s, a: tile(s, a, False), acc)
-        acc = tile(qt, acc, True)
+    for t in range(cfg.NT):
+        go = tile_of(cfg, message_pieces(cfg, go_ref), t)
+        prod = go.astype(F32) * tile_of(cfg, split_pieces(o_ref, G), t).astype(F32)
+        q_scr[t] = pad_queries(cfg, tile_of(cfg, q_in, t), 0)
+        go_scr[t] = pad_queries(cfg, go, 1)
+        delta_scr[t, :QH] = jnp.sum(jnp.where(half, prod, 0.0), axis=1, keepdims=True)
+        delta_scr[t, QH:] = jnp.sum(jnp.where(half, 0.0, prod), axis=1, keepdims=True)
+        acc_scr[t] = jnp.zeros((2 * QH, 2 * hd), F32)
+
+    def step(i, carry):
+        parts = []
+        for u in range(STEP):
+            qt, s = items[0, i * STEP + u], items[1, i * STEP + u]
+            kv = tile_of(cfg, kv_pieces, s)
+            token = row_off + qt * cfg.span
+            key_token = key_off + s * cfg.span
+            e = jnp.exp2(mm_nt(q_scr[qt], kv) * scale)
+            ds = e * (mm_nt(go_scr[qt], kv) - delta_scr[qt])
+            ds = jnp.where((key_token <= token) & (key_token >= start_of(starts, token)), ds, 0.0)
+            parts.append((qt, mm(ds.astype(BF), kv)))
+        for qt, part in parts:
+            acc_scr[qt] += part
+        return carry
+
+    lax.fori_loop(0, steps, step, 0)
+    for t in range(cfg.NT):
+        acc = acc_scr[t]
         out = jnp.where(half, acc[:QH], pltpu.roll(acc[QH:], hd, 1)) * hd ** (-0.5)
         out = out.astype(BF)
-        rows = pl.ds(pl.multiple_of(qt * R, R), R)
         for k in range(G):
-            dq_out[k][rows, :] = out[k * R : (k + 1) * R]
-        return carry
-
-    lax.fori_loop(0, cfg.NT, query_tile, 0)
+            dq_out[k][t * R : (t + 1) * R, :] = out[k * R : (k + 1) * R]
 
 
 def grad_key_kernel(cfg, meta, *refs):
-    G, T, R, hd, lo = cfg.G, cfg.T, cfg.R, cfg.hd, cfg.lo
+    G, T, R, hd, lo, QH, NT = cfg.G, cfg.T, cfg.R, cfg.hd, cfg.lo, cfg.QH, cfg.NT
     own = refs[0]
     q_refs, go_refs = (refs[1 + i * lo : 1 + (i + 1) * lo] for i in range(2))
     rest = refs[1 + 2 * lo :]
-    dkv_out, kv_scr, q_scr, go_scr, delta_scr = rest[:G], *rest[G:]
-    load_tiles(cfg, kv_scr, split_pieces(own, G))
-    load_tiles(cfg, q_scr, [piece for ref in q_refs for piece in split_pieces(ref, G)])
-    load_tiles(cfg, go_scr, [piece for ref in go_refs for piece in message_pieces(cfg, ref)])
+    dkv_out, key_scr, value_scr, delta_scr, gk_scr, gv_scr, items = rest[:G], *rest[G:]
+    q_pieces = [piece for ref in q_refs for piece in split_pieces(ref, G)]
+    go_pieces = [piece for ref in go_refs for piece in message_pieces(cfg, ref)]
     starts = doc_starts(cfg, meta)
-    QH, NT = cfg.QH, cfg.NT
+    steps = list_items(cfg, starts, items)
     scale = hd ** (-0.5) * LOG2E
     rows = cfg.groups * NT
     for j in range(lo):
@@ -416,54 +410,46 @@
     query_off = token_in_span(cfg, meta, iota((1, cfg.KT), 1))
     row_off = token_in_span(cfg, meta, iota((2 * QH, 1), 0) % QH)
     first = iota((QH, 2 * hd), 1) < hd
-
-    def key_tile(kt, carry):
-        kv = kv_scr[kt].astype(F32)
+    for t in range(NT):
+        kv = tile_of(cfg, split_pieces(own, G), t).astype(F32)
         rolled = pltpu.roll(kv, hd, 1)
-        keys = jnp.concatenate(
-            [jnp.where(first, kv, 0.0), jnp.where(first, 0.0, rolled)], axis=0
-        ).astype(BF)
-        values = jnp.concatenate(
-            [jnp.where(first, rolled, 0.0), jnp.where(first, 0.0, kv)], axis=0
-        ).astype(BF)
-        key_token = row_off + kt * cfg.span
-        end_first = end_of(starts, kt * cfg.span)
-        end_last = end_of(starts, (kt + 1) * cfg.span - 1)
-        q_full = jnp.maximum(end_first // cfg.span, kt + 1)
-        q_stop = (end_last - 1) // cfg.span + 1
-
-        def tile(t, acc, masked):
-            grad_keys, grad_values = acc
-            queries, grads = q_scr[t], go_scr[t]
-            e = jnp.exp2(mm_nt(keys, queries) * scale)
-            if masked:
-                token = query_off + t * cfg.span
-                e = jnp.where((key_token <= token) & (key_token >= start_of(starts, token)), e, 0.0)
-            dp = mm_nt(values, grads)
+        keys = [jnp.where(first, kv, 0.0), jnp.where(first, 0.0, rolled)]
+        values = [jnp.where(first, rolled, 0.0), jnp.where(first, 0.0, kv)]
+        key_scr[t] = jnp.concatenate(keys, axis=0).astype(BF)
+        value_scr[t] = jnp.concatenate(values, axis=0).astype(BF)
+        gk_scr[t] = jnp.zeros((2 * QH, 2 * hd), F32)
+        gv_scr[t] = jnp.zeros((2 * QH, 2 * hd), F32)
+
+    def step(i, carry):
+        parts = []
+        for u in range(STEP):
+            t, kt = items[0, i * STEP + u], items[1, i * STEP + u]
+            queries, grads = tile_of(cfg, q_pieces, t), tile_of(cfg, go_pieces, t)
+            key_token = row_off + kt * cfg.span
+            token = query_off + t * cfg.span
+            e = jnp.exp2(mm_nt(key_scr[kt], queries) * scale)
+            e = jnp.where((key_token <= token) & (key_token >= start_of(starts, token)), e, 0.0)
+            dp = mm_nt(value_scr[kt], grads)
             delta = delta_scr[t]
-            ds = jnp.concatenate(
-                [
-                    (e[:QH] * (dp[:QH] - delta[0:1])).astype(BF),
-                    (e[QH:] * (dp[QH:] - delta[1:2])).astype(BF),
-                ],
-                axis=0,
-            )
-            return grad_keys + mm(ds, queries), grad_values + mm(e.astype(BF), grads)
-
-        zero = jnp.zeros((2 * QH, 2 * hd), F32)
-        acc = tile(kt, (zero, zero), True)
-        acc = lax.fori_loop(kt + 1, q_full, lambda t, a: tile(t, a, False), acc)
-        acc = lax.fori_loop(q_full, q_stop, lambda t, a: tile(t, a, True), acc)
-        grad_keys, grad_values = acc
-        gk = (grad_keys[:QH] + pltpu.roll(grad_keys[QH:], hd, 1)) * hd ** (-0.5)
-        gv = pltpu.roll(grad_values[:QH], hd, 1) + grad_values[QH:]
+            ds = [
+                (e[:QH] * (dp[:QH] - delta[0:1])).astype(BF),
+                (e[QH:] * (dp[QH:] - delta[1:2])).astype(BF),
+            ]
+            ds = jnp.concatenate(ds, axis=0)
+            parts.append((kt, mm(ds, queries), mm(e.astype(BF), grads)))
+        for kt, gk, gv in parts:
+            gk_scr[kt] += gk
+            gv_scr[kt] += gv
+        return carry
+
+    lax.fori_loop(0, steps, step, 0)
+    for t in range(NT):
+        gk, gv = gk_scr[t], gv_scr[t]
+        gk = (gk[:QH] + pltpu.roll(gk[QH:], hd, 1)) * hd ** (-0.5)
+        gv = pltpu.roll(gv[:QH], hd, 1) + gv[QH:]
         out = jnp.where(first, gk, gv).astype(BF)
-        rows = pl.ds(pl.multiple_of(kt * R, R), R)
         for k in range(G):
-            dkv_out[k][rows, :] = out[k * R : (k + 1) * R]
-        return carry
-
-    lax.fori_loop(0, cfg.NT, key_tile, 0)
+            dkv_out[k][t * R : (t + 1) * R, :] = out[k * R : (k + 1) * R]
 
 
 def place_pieces(cfg, hi, scr, pieces):
@@ -482,141 +468,82 @@
     part[:, cfg.D :] = mm(rows, ao[...]).astype(BF)
 
 
+def hidden_grad_kernel(cfg, meta, cot_ref, wd, bd, ad, out, turned):
+    cot = cot_ref[...]
+    side = (adapter_mask(cfg, meta) * mm_nt(cot, bd[...])).astype(BF)
+    turned[...] = mm(side, slot_select(cfg, meta)).T.astype(BF)
+    tile = 256
+    for f in range(0, cfg.F, tile):
+        at = slice(f, f + tile)
+        out[:, at] = mm_nt(cot, wd[at, :]) + mm_nt(side, ad[at, :])
+
+
 def ffn_kernel(
-    cfg, units, steps, meta, x_ref, own, other, bo, gain, wg, wu, wd, bg, bu, ag, au, ad, bd, cot_ref,
+    cfg, units, meta, x_ref, own, other, bo, gain, wg, wu, wd, bg, bu, ag, au, ad, cot_ref, gh, gst,
     mixed_ref, dfn_ref, part_ref, oside, *refs,
 ):
-    step = pl.program_id(0)
-    S, D = cfg.S, cfg.D
-    chunks, refs = refs[: units.n], refs[units.n :]
-    fn, sg, su, gsd, sgt, sut, gsdt, down, side_sum, dfn, gsg, gsu, grads = refs
+    D, F = cfg.D, cfg.F
+    chunks, (hidden_scr, gg_scr, gu_scr, grads) = refs[: units.n], refs[units.n :]
     flip = meta[0] % cfg.lo
-
-    @pl.when(step == 0)
-    def _():
-        mask = adapter_mask(cfg, meta)
-        select = slot_select(cfg, meta)
-        total = own[...].astype(F32) + other[...].astype(F32)
-        out_side = (mask * total[:, D:]).astype(BF)
-        oside[...] = mm(out_side, select).astype(BF)
-        mixed = x_ref[...].astype(F32) + total[:, :D] + mm(out_side, bo[...])
-        mixed_ref[...] = mixed
-        rr = lax.rsqrt(jnp.mean(mixed * mixed, axis=-1, keepdims=True) + norm_eps)
-        normed = (mixed * rr * gain[...]).astype(BF)
-        fn[...] = normed
-        side_g = (mask * mm(normed, ag[...])).astype(BF)
-        side_u = (mask * mm(normed, au[...])).astype(BF)
-        grad_side = (mask * mm_nt(cot_ref[...], bd[...])).astype(BF)
-        sg[...] = side_g
-        su[...] = side_u
-        gsd[...] = grad_side
-        sgt[...] = mm(side_g, select).T.astype(BF)
-        sut[...] = mm(side_u, select).T.astype(BF)
-        gsdt[...] = mm(grad_side, select).T.astype(BF)
-        down[...] = jnp.zeros_like(down)
-        side_sum[...] = jnp.zeros_like(side_sum)
-        dfn[...] = jnp.zeros_like(dfn)
-        gsg[...] = jnp.zeros_like(gsg)
-        gsu[...] = jnp.zeros_like(gsu)
-
-    normed = fn[...]
-    gate = mm(normed, wg[...]) + mm(sg[...], bg[...])
-    upper = mm(normed, wu[...]) + mm(su[...], bu[...])
-    grad_hidden = mm_nt(cot_ref[...], wd[...]) + mm_nt(gsd[...], ad[...])
-    sigma = 1.0 / (1.0 + jnp.exp(-gate))
-    silu = gate * sigma
-    hidden = (silu * upper).astype(BF)
-    grad_gate = (grad_hidden * upper * (sigma + silu * (1.0 - sigma))).astype(BF)
-    grad_upper = (grad_hidden * silu).astype(BF)
-    down[...] += mm(hidden, wd[...])
-    side_sum[...] += mm(hidden, ad[...])
-    dfn[...] += mm_nt(grad_gate, wg[...]) + mm_nt(grad_upper, wu[...])
-    gsg[...] += mm_nt(grad_gate, bg[...])
-    gsu[...] += mm_nt(grad_upper, bu[...])
-    for i, (left, right) in enumerate(((sgt, grad_gate), (sut, grad_upper), (gsdt, hidden))):
-        first = step * (right.shape[1] // 128)
-        units.store(grads, flip, 1, i, mm(left[...], right).astype(BF), first)
-
-    @pl.when(step == steps - 1)
-    def _():
-        mask = adapter_mask(cfg, meta)
-        select = slot_select(cfg, meta)
-        side_g = (mask * gsg[...]).astype(BF)
-        side_u = (mask * gsu[...]).astype(BF)
-        dfn_ref[...] = (dfn[...] + mm_nt(side_g, ag[...]) + mm_nt(side_u, au[...])).astype(BF)
-        part_ref[:, :D] = down[...].astype(BF)
-        part_ref[:, D:] = side_sum[...].astype(BF)
-        side_d = (mask * side_sum[...]).astype(BF)
-        for i, (side, right) in enumerate(((side_g, fn), (side_u, fn), (side_d, cot_ref))):
-            left = mm(side, select).T.astype(BF)
-            units.store(grads, flip, 0, i, mm(left, right[...]).astype(BF), 0)
-        units.clear_spare(grads, flip)
-        for j, chunk in enumerate(chunks):
-            chunk[...] = grads[j]
-
-
-def ffn_call(cfg, units, meta, x, own, other, bo, gain, wg, wu, wd, bg, bu, ag, au, ad, bd, cot):
+    mask = adapter_mask(cfg, meta)
+    select = slot_select(cfg, meta)
+    compact = lambda side: mm(side, select).T.astype(BF)
+    total = own[...].astype(F32) + other[...].astype(F32)
+    out_side = (mask * total[:, D:]).astype(BF)
+    oside[...] = mm(out_side, select).astype(BF)
+    mixed = x_ref[...].astype(F32) + total[:, :D] + mm(out_side, bo[...])
+    mixed_ref[...] = mixed
+    rr = lax.rsqrt(jnp.mean(mixed * mixed, axis=-1, keepdims=True) + norm_eps)
+    normed = (mixed * rr * gain[...]).astype(BF)
+    side_g = (mask * mm(normed, ag[...])).astype(BF)
+    side_u = (mask * mm(normed, au[...])).astype(BF)
+    turned = compact(side_g), compact(side_u), gst[...]
+    tile = 256
+    for f in range(0, F, tile):
+        at = slice(f, f + tile)
+        grad_hidden = gh[:, at]
+        gate = mm(normed, wg[:, at]) + mm(side_g, bg[:, at])
+        upper = mm(normed, wu[:, at]) + mm(side_u, bu[:, at])
+        sigma = 1.0 / (1.0 + jnp.exp(-gate))
+        silu = gate * sigma
+        hidden = (silu * upper).astype(BF)
+        grad_gate = (grad_hidden * upper * (sigma + silu * (1.0 - sigma))).astype(BF)
+        grad_upper = (grad_hidden * silu).astype(BF)
+        hidden_scr[:, at] = hidden
+        gg_scr[:, at] = grad_gate
+        gu_scr[:, at] = grad_upper
+    side_g = (mask * mm_nt(gg_scr[...], bg[...])).astype(BF)
+    side_u = (mask * mm_nt(gu_scr[...], bu[...])).astype(BF)
+    side_sum = mm(hidden_scr[...], ad[...])
+    for d in range(0, D, tile):
+        at = slice(d, d + tile)
+        dfn = mm_nt(gg_scr[...], wg[at, :]) + mm_nt(gu_scr[...], wu[at, :])
+        dfn_ref[:, at] = (dfn + mm_nt(side_g, ag[at, :]) + mm_nt(side_u, au[at, :])).astype(BF)
+    for d in range(0, D, tile):
+        at = slice(d, d + tile)
+        part_ref[:, at] = mm(hidden_scr[...], wd[:, at]).astype(BF)
+    part_ref[:, D:] = side_sum.astype(BF)
+    side_d = (mask * side_sum).astype(BF)
+    for i, (side, right) in enumerate(((side_g, normed), (side_u, normed), (side_d, cot_ref[...]))):
+        units.store(grads, 0, i, mm(compact(side), right).astype(BF))
+    for i, right in enumerate((gg_scr, gu_scr, hidden_scr)):
+        units.store(grads, 1, i, mm(turned[i], right[...]).astype(BF))
+    units.clear_spare(grads)
+    for j, chunk in enumerate(chunks):
+        chunk[...] = grads[j ^ flip]
+
+
+def ffn_call(cfg, units, meta, *ins):
     T, D, F, AW, S = cfg.T, cfg.D, cfg.F, cfg.AW, cfg.S
-    tile = 256
-    steps = F // tile
-    whole = lambda shape: pl.BlockSpec(shape, lambda i: (0,) * len(shape))
-    cols = lambda rows: pl.BlockSpec((rows, tile), lambda i: (0, i))
-    rows = lambda width: pl.BlockSpec((tile, width), lambda i: (i, 0))
-    outs = [
-        ((T, D), F32),
-        ((T, D), BF),
-        ((T, D + AW), BF),
-        ((T, S), BF),
-    ] + [((units.u, 16, 128), BF)] * units.n
-    out_specs = [
-        whole((T, D)),
-        whole((T, D)),
-        whole((T, D + AW)),
-        whole((T, S)),
-    ] + [whole((units.u, 16, 128))] * units.n
-    return pl.pallas_call(
-        with_meta(functools.partial(ffn_kernel, cfg, units, steps)),
-        grid=(steps,),
-        out_shape=[jax.ShapeDtypeStruct(s, d) for s, d in outs],
-        in_specs=[
-            SMEM,
-            SMEM,
-            whole((T, D)),
-            whole((T, D + AW)),
-            whole((T, D + AW)),
-            whole((AW, D)),
-            whole((1, D)),
-            cols(D),
-            cols(D),
-            rows(D),
-            cols(AW),
-            cols(AW),
-            whole((D, AW)),
-            whole((D, AW)),
-            rows(AW),
-            whole((AW, D)),
-            whole((T, D)),
-        ],
-        out_specs=out_specs,
-        scratch_shapes=[
-            pltpu.VMEM((T, D), BF),
-            pltpu.VMEM((T, AW), BF),
-            pltpu.VMEM((T, AW), BF),
-            pltpu.VMEM((T, AW), BF),
-            pltpu.VMEM((S, T), BF),
-            pltpu.VMEM((S, T), BF),
-            pltpu.VMEM((S, T), BF),
-            pltpu.VMEM((T, D), F32),
-            pltpu.VMEM((T, AW), F32),
-            pltpu.VMEM((T, D), F32),
-            pltpu.VMEM((T, AW), F32),
-            pltpu.VMEM((T, AW), F32),
-            pltpu.VMEM((units.n, units.u, 16, 128), BF),
-        ],
-        compiler_params=params(dimension_semantics=("arbitrary",)),
-        cost_estimate=cost(19),
+    return call(
+        functools.partial(ffn_kernel, cfg, units),
+        [((T, D), F32), ((T, D), BF), ((T, D + AW), BF), ((T, S), BF)]
+        + [((units.u, 16, 128), BF)] * units.n,
+        [meta, *ins],
+        scratch=[pltpu.VMEM((T, F), BF)] * 3 + [pltpu.VMEM((units.n, units.u, 16, 128), BF)],
+        us=14,
         name="ffn",
-    )(*meta, x, own, other, bo, gain, wg, wu, wd, bg, bu, ag, au, ad, bd, cot)
+    )
 
 
 def mixed_grad_kernel(cfg, meta, *refs):
@@ -758,7 +685,7 @@
             out += [(i // per, base + i % per) for i in range(count, per * self.n)]
         return out
 
-    def store(self, out, flip, which, array, values, first):
+    def store(self, out, which, array, values, first=0):
         widths, per, base = (
             (self.shared, self.us, 0) if which == 0 else (self.private, self.up, self.us)
         )
@@ -766,20 +693,22 @@
         for c in range(values.shape[1] // 128):
             for a in range(self.high):
                 unit = at + c * self.high + a
-                out[(unit // per) ^ flip, base + unit % per] = values[
+                out[unit // per, base + unit % per] = values[
                     a * 16 : a * 16 + 16, c * 128 : c * 128 + 128
                 ]
 
-    def clear_spare(self, out, flip):
+    def clear_spare(self, out):
         for chunk, off in self.spare():
-            out[chunk ^ flip, off] = jnp.zeros((16, 128), BF)
-
-
-def pack(units, out, flip, arrays):
+            out[chunk, off] = jnp.zeros((16, 128), BF)
+
+
+def pack(units, scr, flip, outs, arrays):
     for i, values in enumerate(arrays):
         which = int(i >= len(units.shared))
-        units.store(out, flip, which, i - which * len(units.shared), values, 0)
-    units.clear_spare(out, flip)
+        units.store(scr, which, i - which * len(units.shared), values)
+    units.clear_spare(scr)
+    for j, out in enumerate(outs):
+        out[...] = scr[j ^ flip]
 
 
 def add_halves(keep, got, count):
@@ -793,25 +722,25 @@
     kw = bkv.shape[1] // 2
     shared = add_halves(keep_q, got_q, 1) + add_halves(keep, got, 2) + [ograds[1]]
     private = [ograds[0], bq[...], bkv[:, :kw], bkv[:, kw:]]
-    pack(units, scr, meta[0] % cfg.lo, shared + private)
-    for j, out in enumerate(outs):
-        out[...] = scr[j]
-
-
-def unpack(ref, spots, place):
+    pack(units, scr, meta[0] % cfg.lo, outs, shared + private)
+
+
+def unpack(ref, spots):
     cols = {}
     for chunk, off, a, c in spots:
-        cols.setdefault(c, []).append(ref[place(chunk), off])
+        cols.setdefault(c, []).append(ref[chunk, off])
     return jnp.concatenate([jnp.concatenate(cols[c], axis=0) for c in sorted(cols)], axis=1)
 
 
 def expand_kernel(cfg, units, plan, halves, meta, *refs):
-    own_in, other, outs, own = refs[: cfg.lo], refs[cfg.lo], refs[cfg.lo + 1 : -1], refs[-1]
+    own_in, other_in, outs = refs[: cfg.lo], refs[cfg.lo], refs[cfg.lo + 1 : -2]
+    own, other = refs[-2:]
+    flip = meta[0] % cfg.lo
     for j in range(cfg.lo):
-        own[j] = own_in[j][...]
+        own[j ^ flip] = own_in[j][...]
+        other[j ^ flip] = other_in[j]
     wa = meta[1]
     select = slot_select(cfg, meta)
-    place = lambda chunk: chunk ^ (meta[0] % cfg.lo)
 
     def write(out, values, transposed, at):
         full = mm(select, values)
@@ -822,11 +751,11 @@
 
     for (which, i, transposed), out in zip(plan, outs):
         spots = units.places(which)[i]
-        mine = unpack(own, spots, place)
+        mine = unpack(own, spots)
         if which == 1:
             write(out, mine, transposed, 0)
         else:
-            theirs = unpack(other, spots, place)
+            theirs = unpack(other, spots)
             if not halves:
                 total = mine.astype(F32) + theirs.astype(F32)
                 write(out, total.astype(BF), transposed, 0)
@@ -886,8 +815,8 @@
     qg = query_gain.reshape(1, head_dim)
     kg = key_gain.reshape(1, head_dim)
 
-    lane = jnp.arange(2 * head_dim, dtype=jnp.int32) % (head_dim // 2)
-    inverse = jnp.exp(lane.astype(F32) * (-2.0 * math.log(theta_base) / head_dim))[None, :]
+    lane = np.arange(2 * head_dim) % (head_dim // 2)
+    inverse = np.exp(lane * (-2.0 * math.log(theta_base) / head_dim)).astype(np.float32)[None, :]
 
     piece = ((T, gw), BF)
     pre = call(
@@ -918,12 +847,21 @@
 
     kv = to_plane(jnp.stack(to_heads(kv_send)))
     q = to_heads(q_send)
-    tiles = lambda rows: pltpu.VMEM((cfg.NT, rows, gw), BF)
+    grad_hidden, gst = call(
+        functools.partial(hidden_grad_kernel, cfg),
+        [((T, cfg.F), F32), ((S, T), BF)],
+        [meta, cot, down_weight, down_adapt_out, down_adapt_in],
+        us=3,
+        name="hidden_grad",
+    )
+    grad_hidden, *both = after(grad_hidden, *kv, *q)
+    kv, q = both[:lo], both[lo:]
+    tiles = lambda dtype, width=gw: pltpu.VMEM((cfg.NT, 2 * cfg.QH, width), dtype)
     attn = call(
         functools.partial(attend_kernel, cfg),
         [piece] * G + [((G, T, gw), BF), ((G, T, gw), F32)],
         [meta] + q + kv,
-        scratch=[tiles(cfg.KT), tiles(cfg.KT), tiles(cfg.QH)],
+        scratch=[tiles(BF), tiles(F32), items_scratch(cfg)],
         us=12,
         name="attend",
     )
@@ -943,11 +881,10 @@
     ffn = ffn_call(
         cfg, units_f, meta, x, opart, swap_cores(opart), out_adapt_out, gain_f, gate_weight, up_weight,
         down_weight, gate_adapt_out, up_adapt_out, gate_adapt_in, up_adapt_in, down_adapt_in,
-        down_adapt_out, cot,
+        cot, grad_hidden, gst,
     )
     mixed, dfn, dpart, oside, *parts_f = ffn
     dfn, *q_plane = after(dfn, *q_plane)
-    parts_f = [parts_f[0]] + [permute(cfg, parts_f[j], j) for j in range(1, lo)]
     mg = call(
         functools.partial(mixed_grad_kernel, cfg),
         [((T, D), F32), ((2, S, D // 2), BF)] + [piece] * G,
@@ -955,22 +892,12 @@
         + o
         + [out_weight, out_adapt_in, out_adapt_out, oside],
         scratch=[pltpu.VMEM((T, QW), BF), pltpu.VMEM((G, T, gw), BF), pltpu.VMEM((T, D), BF)],
-        us=4.5,
+        us=0.01,
         name="mixed_grad",
     )
     grad_mixed, ograds, go_send = mg[0], mg[1], mg[2:]
     go_heads = to_heads(go_send)
-    dpart, _ = after(dpart, go_send[0])
-    (out_rows,) = call(
-        functools.partial(output_kernel, cfg),
-        [((T, D), BF)],
-        [meta, mixed, dpart, swap_cores(dpart), down_adapt_out],
-        us=2,
-        name="output",
-    )
-    out_rows, *both = after(out_rows, *parts_f, *go_heads)
-    parts_f, go_heads = both[:lo], both[lo:]
-    sum_f = add(parts_f)
+    parts_f = [parts_f[0]] + [permute(cfg, parts_f[j], j) for j in range(1, lo)]
     message = G * T + -(-2 * cfg.groups * cfg.NT // 16) * 16
     (go_all,) = call(
         functools.partial(scale_kernel, cfg),
@@ -980,15 +907,17 @@
             pltpu.VMEM((cfg.NT, cfg.QH, gw), F32),
             pltpu.VMEM((cfg.groups * cfg.NT, gw), F32),
         ],
-        us=2,
+        us=0.01,
         name="scale",
     )
+    go_all, *parts_f = after(go_all, *parts_f)
+    sum_f = add(parts_f)
     go_plane = to_plane(go_all)
     dq_send = call(
         functools.partial(grad_query_kernel, cfg),
         [piece] * G,
         [meta] + q + kv + [go_all, o_all],
-        scratch=[tiles(cfg.KT), tiles(cfg.QH), tiles(cfg.QH), tiles(cfg.QH)],
+        scratch=[tiles(BF), tiles(BF), tiles(F32, 1), tiles(F32), items_scratch(cfg)],
         us=13.5,
         name="grad_query",
     )
@@ -1000,8 +929,8 @@
         functools.partial(grad_key_kernel, cfg),
         [piece] * G,
         [meta, kv[0]] + q_plane + go_plane,
-        scratch=[tiles(cfg.QH), tiles(cfg.KT), tiles(cfg.KT)]
-        + [pltpu.VMEM((cfg.NT, 16, cfg.KT), F32)],
+        scratch=[tiles(BF), tiles(BF), pltpu.VMEM((cfg.NT, 16, cfg.KT), F32), tiles(F32)]
+        + [tiles(F32), items_scratch(cfg)],
         us=16,
         name="grad_key",
     )
@@ -1009,7 +938,16 @@
     dq, dkv_send = both[:G], both[G:]
     sum_f = add([sum_f, got_f])
     dkv = to_heads(dkv_send)
-    pieces_f = to_plane(sum_f)
+    all_f = [sum_f] + [permute(cfg, sum_f, j) for j in range(1, lo - 1)]
+    dpart, _ = after(dpart, dkv_send[0])
+    (out_rows,) = call(
+        functools.partial(output_kernel, cfg),
+        [((T, D), BF)],
+        [meta, mixed, dpart, swap_cores(dpart), down_adapt_out],
+        us=0.01,
+        name="output",
+    )
+    out_rows, *dkv = after(out_rows, *dkv)
 
     qpart, bgrad_q, akeep_q, asend_q = call(
         functools.partial(query_back_kernel, cfg),
@@ -1020,7 +958,7 @@
             normed, qraw, sides, cos, sin, qg, query_weight, query_adapt_in, query_adapt_out,
         ],
         scratch=[pltpu.VMEM((T, QW), BF), pltpu.VMEM((S, D), F32)],
-        us=3.5,
+        us=0.01,
         name="query_back",
     )
     dnormed, bgrad_kv, akeep_kv, asend_kv = call(
@@ -1033,52 +971,59 @@
             value_adapt_in, key_adapt_out, value_adapt_out, qpart,
         ],
         scratch=[pltpu.VMEM((T, 2 * KW), BF), pltpu.VMEM((2 * S, D), F32)],
-        us=4.5,
+        us=0.01,
         name="key_value_back",
     )
-    (input_rows,) = call(
-        functools.partial(input_grad_kernel, cfg),
-        [((T, D), BF)],
-        [meta, x, gain_a, grad_mixed, dnormed, swap_cores(dnormed)],
-        us=3,
-        name="input_grad",
-    )
-
-    def expand(units, pieces, plan, halves, outs, name):
-        theirs = swap_cores(jnp.stack([value[: units.us] for value in pieces]))
+    def expand(units, chunks, plan, halves, outs, name):
+        theirs = swap_cores(jnp.stack([chunk[: units.us] for chunk in chunks]))
         return call(
             functools.partial(expand_kernel, cfg, units, plan, halves),
             outs,
-            [meta] + pieces + [theirs],
-            scratch=[pltpu.VMEM((units.n, units.u, 16, 128), BF)],
+            [meta, *chunks, theirs],
+            scratch=[
+                pltpu.VMEM((units.n, units.u, 16, 128), BF),
+                pltpu.VMEM((units.n, units.us, 16, 128), BF),
+            ],
             us=4,
             name=name,
         )
 
+    dnormed, *all_f = after(dnormed, *all_f)
     units_q = Units(cfg, lo, [D // 2] * 4, [QW, QW, KW, KW])
-    dnormed, bgrad_kv, *pieces_f = after(dnormed, bgrad_kv, *pieces_f)
+    dn_other = swap_cores(dnormed)
     parts_q = call(
         functools.partial(pack_qkv_kernel, cfg, units_q),
         [((units_q.u, 16, 128), BF)] * lo,
         [meta, akeep_q, swap_cores(asend_q), akeep_kv, swap_cores(asend_kv), ograds, bgrad_q]
         + [bgrad_kv],
         scratch=[pltpu.VMEM((lo, units_q.u, 16, 128), BF)],
-        us=2,
+        us=0.01,
         name="pack_qkv",
     )
     sum_q = add([parts_q[0]] + [permute(cfg, parts_q[j], j) for j in range(1, lo)])
-    for bit in upper_bits(cfg):
-        sum_q = add([sum_q, permute(cfg, sum_q, bit)])
-    pieces_q = to_plane(sum_q)
+    sum_q, dn_other, sum_f = after(sum_q, dn_other, sum_f)
+    all_f = all_f + [permute(cfg, sum_f, lo - 1)]
+    (input_rows,) = call(
+        functools.partial(input_grad_kernel, cfg),
+        [((T, D), BF)],
+        [meta, x, gain_a, grad_mixed, dnormed, dn_other],
+        us=0.01,
+        name="input_grad",
+    )
+    got_q, input_rows = after(permute(cfg, sum_q, near), input_rows)
+    sum_q = add([sum_q, got_q])
+    got_q, all_f[-1] = after(permute(cfg, sum_q, far), all_f[-1])
+    pieces_q = to_plane(add([sum_q, got_q]))
     gate_in, up_in, down_out, gate_out, up_out, down_in = expand(
         units_f,
-        pieces_f,
+        all_f,
         [(0, 0, True), (0, 1, True), (0, 2, False), (1, 0, False), (1, 1, False), (1, 2, True)],
         False,
         [((D, AW), F32), ((D, AW), F32), ((AW, D), F32)]
         + [((AW, cfg.F), F32), ((AW, cfg.F), F32), ((cfg.F, AW), F32)],
         "expand_ffn",
     )
+    down_out, *pieces_q = after(down_out, *pieces_q)
     query_in, key_in, value_in, out_out, out_in, query_out, key_out, value_out = expand(
         units_q,
         pieces_q,

time: 189 us -> 170 us (0.90)
  waiting for transfers between devices: 51.8 us -> 36.3 us
  Pallas kernels: 80.2 us -> 67.7 us
  starting transfers between devices: 54 us -> 62.9 us
    pallas_call x1 -> x0, Pallas kernels: 16.9 us -> none  [ffn_call(): pl.pallas_call(with_meta(functools.partial(ffn_kernel, cfg, units, steps)...]
    ppermute x43, waiting for transfers between devices: 49.9 us -> 33.2 us  [permute(): return lax.ppermute(value, 'ctx', [(i, i ^ bits) for i in range(cfg.n)])]
    ppermute x43, starting transfers between devices: 52.8 us -> 62 us  [permute(): return lax.ppermute(value, 'ctx', [(i, i ^ bits) for i in range(cfg.n)])]
    pallas_call x14 -> x16, Pallas kernels: 63.3 us -> 67.7 us  [call(): pl.pallas_call(with_meta(kernel), out_shape=[jax.ShapeDtypeStruct(s, d) f...]
  transfers between devices with their start and end apart: 51 -> 51, of which waited for: 19 -> 18; matrix products, arithmetic and copies ran while one was open for 0% -> 1% of each run, Pallas kernels for 30% -> 30%
where the time goes in v3:
time: 170 us
  Pallas kernels  67.7 us (40%)
  starting transfers between devices  62.9 us (37%)
  waiting for transfers between devices  36.3 us (21%)
    pallas_call x16, Pallas kernels, call(): pl.pallas_call(with_meta(kernel), out_shape=[jax.ShapeDtypeStruct(s, d) f...  67.7 us
    ppermute x43, starting transfers between devices, permute(): return lax.ppermute(value, 'ctx', [(i, i ^ bits) for i in range(cfg.n)])  62 us
    ppermute x43, waiting for transfers between devices, permute(): return lax.ppermute(value, 'ctx', [(i, i ^ bits) for i in range(cfg.n)])  33.2 us
  transfers between devices with their start and end apart: 51, of which 18 were waited for; matrix products, arithmetic and copies ran while one was open for 1% of the time, Pallas kernels for 30%

profile of v3, /device:TPU:0, one launch (start us, length us, event | category | flops | bytes accessed | tf_op | source)
XLA Modules:
  0.0 170.2 jit_solution(43266492235338115)
XLA Ops:
  0.7 5.9 %pre.1 = (bf16[256,128]{1,0:T(8,128)(2,1)}, bf16[256,128]{1,0:T(8,128)(2,1)}, bf16[256,128]{1,0:T(8,128)(2,1)}, bf16[256,128]{1,0:T(8,128)(2,1)}, bf16[256,128]{...) custom-call(s32[4]{0:T(128)} %extra.31, ...), custom_call_target="tpu_custom_call" | custom-call | flops 6899999744 | tf_op jit(solution)/shard_map/pre/pallas_call | solution.py:155
  6.6 5.1 %collective-permute-start.2 = (bf16[256,128]{1,0:T(8,128)(2,1)}, bf16[256,128]{1,0:T(8,128)(2,1)S(1)}, u32[]{:S(2)}, u32[]{:S(2)}) collective-permute-start(bf16[256,128]{1,0:T(8,128)(2,1)} %get-tuple-element.146), channel_id=1, source_target_pairs={{0,24},{2,26},{4,28},{6,30},{8,16},{10,18},{12,20},{14,22},{16,8},... | collective-permute-start | bytes 196616 | tf_op jit(solution)/shard_map/ppermute | solution.py:785
  13.8 2.9 %collective-permute-start.7 = (bf16[256,128]{1,0:T(8,128)(2,1)}, bf16[256,128]{1,0:T(8,128)(2,1)S(1)}, u32[]{:S(2)}, u32[]{:S(2)}) collective-permute-start(bf16[256,128]{1,0:T(8,128)(2,1)} %get-tuple-element.149), channel_id=1, source_target_pairs={{0,16},{2,18},{4,20},{6,22},{8,24},{10,26},{12,28},{14,30},{16,0},... | collective-permute-start | bytes 196616 | tf_op jit(solution)/shard_map/ppermute | solution.py:785
  16.7 2.0 %collective-permute-start.8 = (bf16[256,128]{1,0:T(8,128)(2,1)}, bf16[256,128]{1,0:T(8,128)(2,1)S(1)}, u32[]{:S(2)}, u32[]{:S(2)}) collective-permute-start(bf16[256,128]{1,0:T(8,128)(2,1)} %get-tuple-element.150), channel_id=1, source_target_pairs={{0,24},{2,26},{4,28},{6,30},{8,16},{10,18},{12,20},{14,22},{16,8},... | collective-permute-start | bytes 196616 | tf_op jit(solution)/shard_map/ppermute | solution.py:785
  23.3 2.8 %hidden_grad.1 = (f32[256,2304]{1,0:T(8,128)S(1)}, bf16[64,256]{1,0:T(8,128)(2,1)S(1)}) custom-call(s32[4]{0:T(128)S(1)} %copy-done.22, s32[4]{0:T(128)S(1)} %copy-done.23, bf16[256,1024]{1,0:T(8,128)(2,1)S(1)} %bitcast.35, bf16[2304,1024]{1,0:T(8,128)(2,1)S(1)} %copy-done.28, bf16[128,1024]{1,0:T(8,128)(2,1)S(1)} %copy-done.16, bf16[2304,128]{1,0:T(8,128)(2,1)S(1)} %copy-done.31), custom_call_target="tpu_custom_call" | custom-call | flops 3449999872 | tf_op jit(solution)/shard_map/hidden_grad/pallas_call | solution.py:155
  26.0 2.9 %collective-permute-done.3.refs_5_ = bf16[4,256,128]{2,1,0:T(8,128)(2,1)S(1)} collective-permute-done((bf16[4,256,128]{2,1,0:T(8,128)(2,1)S(1)}, bf16[4,256,128]{2,1,0:T(8,128)(2,1)S(1)}, u32[]{:S(2)}, u32[]{:S(2)}) %collective-permute-start.3) | collective-permute-done | bytes 262176 | tf_op jit(solution)/shard_map/ppermute | solution.py:785
  28.9 4.5 %collective-permute-done.4.refs_6_ = bf16[4,256,128]{2,1,0:T(8,128)(2,1)S(1)} collective-permute-done((bf16[4,256,128]{2,1,0:T(8,128)(2,1)S(1)}, bf16[4,256,128]{2,1,0:T(8,128)(2,1)S(1)}, u32[]{:S(2)}, u32[]{:S(2)}) %collective-permute-start.4) | collective-permute-done | bytes 262176 | tf_op jit(solution)/shard_map/ppermute | solution.py:785
  33.5 7.8 %attend.1 = (bf16[256,128]{1,0:T(8,128)(2,1)S(1)}, bf16[256,128]{1,0:T(8,128)(2,1)S(1)}, bf16[256,128]{1,0:T(8,128)(2,1)S(1)}, bf16[256,128]{1,0:T(8,128)(2,1)S(...) custom-call(s32[4]{0:T(128)S(1)} %copy-done.22, s32[4]{0:T(128)S(1)} %copy-done.23, ...), custom_call_target="tpu_custom_call" | custom-call | flops 13799999488 | tf_op jit(solution)/shard_map/attend/pallas_call | solution.py:155
  41.4 2.0 %collective-permute-start.10 = (bf16[256,128]{1,0:T(8,128)(2,1)S(1)}, bf16[256,128]{1,0:T(8,128)(2,1)S(1)}, u32[]{:S(2)}, u32[]{:S(2)}) collective-permute-start(bf16[256,128]{1,0:T(8,128)(2,1)S(1)} %get-tuple-element.161), channel_id=1, source_target_pairs={{0,16},{2,18},{4,20},{6,22},{8,24},{10,26},{12,28},{14,30},{16,0},... | collective-permute-start | bytes 196616 | tf_op jit(solution)/shard_map/ppermute | solution.py:785
  43.4 2.4 %collective-permute-start.11 = (bf16[256,128]{1,0:T(8,128)(2,1)S(1)}, bf16[256,128]{1,0:T(8,128)(2,1)S(1)}, u32[]{:S(2)}, u32[]{:S(2)}) collective-permute-start(bf16[256,128]{1,0:T(8,128)(2,1)S(1)} %get-tuple-element.162), channel_id=1, source_target_pairs={{0,24},{2,26},{4,28},{6,30},{8,16},{10,18},{12,20},{14,22},{16,8},... | collective-permute-start | bytes 196616 | tf_op jit(solution)/shard_map/ppermute | solution.py:785
  46.6 2.8 %collective-permute-done.11.refs_3_.refs_8_ = bf16[256,128]{1,0:T(8,128)(2,1)S(1)} collective-permute-done((bf16[256,128]{1,0:T(8,128)(2,1)S(1)}, bf16[256,128]{1,0:T(8,128)(2,1)S(1)}, u32[]{:S(2)}, u32[]{:S(2)}) %collective-permute-start.11) | collective-permute-done | bytes 65568 | tf_op jit(solution)/shard_map/ppermute | solution.py:785
  54.4 11.4 %ffn.1 = (f32[256,1024]{1,0:T(8,128)S(1)}, bf16[256,1024]{1,0:T(8,128)(2,1)S(1)}, bf16[256,1152]{1,0:T(8,128)(2,1)S(1)}, bf16[256,64]{1,0:T(8,128)(2,1)S(1)}, bf...) custom-call(s32[4]{0:T(128)S(1)} %copy-done.22, ...), custom_call_target="tpu_custom_call" | custom-call | flops 16099999744 | tf_op jit(solution)/shard_map/ffn/pallas_call | solution.py:155
  69.6 2.0 %mixed_grad.1 = (f32[256,1024]{1,0:T(8,128)S(1)}, bf16[2,64,512]{2,1,0:T(8,128)(2,1)S(1)}, bf16[256,128]{1,0:T(8,128)(2,1)S(1)}, bf16[256,128]{1,0:T(8,128)(2,1)...) custom-call(s32[4]{0:T(128)S(1)} %copy-done.22, s32[4]{0:T(128)S(1)} %copy-done.23, ...), custom_call_target="tpu_custom_call" | custom-call | flops 11500000 | tf_op jit(solution)/shard_map/mixed_grad/pallas_call | solution.py:155
  71.6 2.9 %collective-permute-start.18 = (bf16[256,128]{1,0:T(8,128)(2,1)S(1)}, bf16[256,128]{1,0:T(8,128)(2,1)S(1)}, u32[]{:S(2)}, u32[]{:S(2)}) collective-permute-start(bf16[256,128]{1,0:T(8,128)(2,1)S(1)} %get-tuple-element.173), channel_id=1, source_target_pairs={{0,16},{2,18},{4,20},{6,22},{8,24},{10,26},{12,28},{14,30},{16,0},... | collective-permute-start | bytes 196616 | tf_op jit(solution)/shard_map/ppermute | solution.py:785
  74.6 1.8 %collective-permute-done.17.refs_1_ = bf16[256,128]{1,0:T(8,128)(2,1)S(1)} collective-permute-done((bf16[256,128]{1,0:T(8,128)(2,1)S(1)}, bf16[256,128]{1,0:T(8,128)(2,1)S(1)}, u32[]{:S(2)}, u32[]{:S(2)}) %collective-permute-start.17) | collective-permute-done | bytes 65568 | tf_op jit(solution)/shard_map/ppermute | solution.py:785
  76.4 2.3 %collective-permute-start.19 = (bf16[256,128]{1,0:T(8,128)(2,1)S(1)}, bf16[256,128]{1,0:T(8,128)(2,1)S(1)}, u32[]{:S(2)}, u32[]{:S(2)}) collective-permute-start(bf16[256,128]{1,0:T(8,128)(2,1)S(1)} %get-tuple-element.174), channel_id=1, source_target_pairs={{0,24},{2,26},{4,28},{6,30},{8,16},{10,18},{12,20},{14,22},{16,8},... | collective-permute-start | bytes 196616 | tf_op jit(solution)/shard_map/ppermute | solution.py:785
  78.7 3.8 %collective-permute-done.19.refs_3_ = bf16[256,128]{1,0:T(8,128)(2,1)S(1)} collective-permute-done((bf16[256,128]{1,0:T(8,128)(2,1)S(1)}, bf16[256,128]{1,0:T(8,128)(2,1)S(1)}, u32[]{:S(2)}, u32[]{:S(2)}) %collective-permute-start.19) | collective-permute-done | bytes 65568 | tf_op jit(solution)/shard_map/ppermute | solution.py:785
  87.4 9.8 %grad_query.1 = (bf16[256,128]{1,0:T(8,128)(2,1)S(1)}, bf16[256,128]{1,0:T(8,128)(2,1)S(1)}, bf16[256,128]{1,0:T(8,128)(2,1)S(1)}, bf16[256,128]{1,0:T(8,128)(2,1)S(1)}) custom-call(s32[4]{0:T(128)S(1)} %copy-done.22, s32[4]{0:T(128)S(1)} %copy-done.23, bf16[256,128]{1,0:T(8,128)(2,1)S(1)} %copy-done.21, ...), custom_call_target="tpu_custom_call" | custom-call | flops 15525000192 | tf_op jit(solution)/shard_map/grad_query/pallas_call | solution.py:155
  97.4 3.0 %collective-permute-start.24 = (bf16[78,16,128]{2,1,0:T(8,128)(2,1)S(1)}, bf16[78,16,128]{2,1,0:T(8,128)(2,1)S(1)}, u32[]{:S(2)}, u32[]{:S(2)}) collective-permute-start(bf16[78,16,128]{2,1,0:T(8,128)(2,1)S(1)} %add_convert_fusion.1), channel_id=1, source_target_pairs={{0,16},{2,18},{4,20},{6,22},{8,24},{10,26},{12,28},{14,30},{16,0},... | collective-permute-start | bytes 958472 | tf_op jit(solution)/shard_map/ppermute | solution.py:785
  100.5 2.0 %collective-permute-start.26 = (bf16[256,128]{1,0:T(8,128)(2,1)S(1)}, bf16[256,128]{1,0:T(8,128)(2,1)S(1)}, u32[]{:S(2)}, u32[]{:S(2)}) collective-permute-start(bf16[256,128]{1,0:T(8,128)(2,1)S(1)} %get-tuple-element.193), channel_id=1, source_target_pairs={{0,16},{2,18},{4,20},{6,22},{8,24},{10,26},{12,28},{14,30},{16,0},... | collective-permute-start | bytes 196616 | tf_op jit(solution)/shard_map/ppermute | solution.py:785
  102.5 2.4 %collective-permute-start.27 = (bf16[256,128]{1,0:T(8,128)(2,1)S(1)}, bf16[256,128]{1,0:T(8,128)(2,1)S(1)}, u32[]{:S(2)}, u32[]{:S(2)}) collective-permute-start(bf16[256,128]{1,0:T(8,128)(2,1)S(1)} %get-tuple-element.194), channel_id=1, source_target_pairs={{0,24},{2,26},{4,28},{6,30},{8,16},{10,18},{12,20},{14,22},{16,8},... | collective-permute-start | bytes 196616 | tf_op jit(solution)/shard_map/ppermute | solution.py:785
  104.8 11.0 %grad_key.1 = (bf16[256,128]{1,0:T(8,128)(2,1)S(1)}, bf16[256,128]{1,0:T(8,128)(2,1)S(1)}, bf16[256,128]{1,0:T(8,128)(2,1)S(1)}, bf16[256,128]{1,0:T(8,128)(2,1)S(1)}) custom-call(s32[4]{0:T(128)S(1)} %copy-done.22, s32[4]{0:T(128)S(1)} %copy-done.23, bf16[4,256,128]{2,1,0:T(8,128)(2,1)S(1)} %pad_maximum_fusion.1.refs_4_.refs_0_, ...), custom_call_target="tpu_custom_call" | custom-call | flops 18400000000 | tf_op jit(solution)/shard_map/grad_key/pallas_call | solution.py:155
  115.8 2.6 %collective-permute-done.26.refs_2_ = bf16[256,128]{1,0:T(8,128)(2,1)S(1)} collective-permute-done((bf16[256,128]{1,0:T(8,128)(2,1)S(1)}, bf16[256,128]{1,0:T(8,128)(2,1)S(1)}, u32[]{:S(2)}, u32[]{:S(2)}) %collective-permute-start.26) | collective-permute-done | bytes 65568 | tf_op jit(solution)/shard_map/ppermute | solution.py:785
  124.9 2.4 %query_back.1 = (f32[256,1024]{1,0:T(8,128)S(1)}, bf16[64,512]{1,0:T(8,128)(2,1)S(1)}, bf16[64,512]{1,0:T(8,128)(2,1)S(1)}, bf16[64,512]{1,0:T(8,128)(2,1)S(1)}) custom-call(s32[4]{0:T(128)S(1)} %copy-done.22, s32[4]{0:T(128)S(1)} %copy-done.23, bf16[256,128]{1,0:T(8,128)(2,1)S(1)} %get-tuple-element.209.refs_0_, ...), custom_call_target="tpu_custom_call" | custom-call | flops 11500000 | tf_op jit(solution)/shard_map/query_back/pallas_call | solution.py:155
  129.8 2.5 %key_value_back.1 = (bf16[256,1024]{1,0:T(8,128)(2,1)S(1)}, bf16[64,512]{1,0:T(8,128)(2,1)S(1)}, bf16[128,512]{1,0:T(8,128)(2,1)S(1)}, bf16[128,512]{1,0:T(8,128)(2,1)S(1)}) custom-call(s32[4]{0:T(128)S(1)} %copy-done.22, s32[4]{0:T(128)S(1)} %copy-done.23, bf16[256,128]{1,0:T(8,128)(2,1)S(1)} %get-tuple-element.220.refs_0_, ...), custom_call_target="tpu_custom_call" | custom-call | flops 11500000 | tf_op jit(solution)/shard_map/key_value_back/pallas_call | solution.py:155
  138.8 3.3 %collective-permute-done.39 = bf16[28,16,128]{2,1,0:T(8,128)(2,1)S(1)} collective-permute-done((bf16[28,16,128]{2,1,0:T(8,128)(2,1)S(1)}, bf16[28,16,128]{2,1,0:T(8,128)(2,1)S(1)}, u32[]{:S(2)}, u32[]{:S(2)}) %collective-permute-start.39) | collective-permute-done | bytes 114720 | tf_op jit(solution)/shard_map/ppermute | solution.py:785
  147.1 1.9 %input_grad.1 = bf16[256,1024]{1,0:T(8,128)(2,1)} custom-call(s32[4]{0:T(128)S(1)} %copy-done.22, s32[4]{0:T(128)S(1)} %copy-done.23, bf16[256,1024]{1,0:T(8,128)(2,1)S(1)} %bitcast.34, f32[1,1024]{1,0:T(1,128)S(1)} %bitcast.43, f32[256,1024]{1,0:T(8,128)S(1)} %get-tuple-element.239.refs_2_, bf16[256,1024]{1,0:T(8,128)(2,1)S(1)} %get-tuple-element.237.refs_3_, ...), custom_call_target="tpu_custom_call" | custom-call | flops 11500000 | tf_op jit(solution)/shard_map/input_grad/pallas_call | solution.py:155
  149.1 2.2 %collective-permute-start.44 = (bf16[28,16,128]{2,1,0:T(8,128)(2,1)S(1)}, bf16[28,16,128]{2,1,0:T(8,128)(2,1)S(1)}, u32[]{:S(2)}, u32[]{:S(2)}) collective-permute-start(bf16[28,16,128]{2,1,0:T(8,128)(2,1)S(1)} %add_convert_fusion.4), channel_id=1, source_target_pairs={{0,16},{2,18},{4,20},{6,22},{8,24},{10,26},{12,28},{14,30},{16,0},... | collective-permute-start | bytes 344072 | tf_op jit(solution)/shard_map/ppermute | solution.py:785
  151.4 5.6 %collective-permute-done.44 = bf16[28,16,128]{2,1,0:T(8,128)(2,1)S(1)} collective-permute-done((bf16[28,16,128]{2,1,0:T(8,128)(2,1)S(1)}, bf16[28,16,128]{2,1,0:T(8,128)(2,1)S(1)}, u32[]{:S(2)}, u32[]{:S(2)}) %collective-permute-start.44) | collective-permute-done | bytes 114720 | tf_op jit(solution)/shard_map/ppermute | solution.py:785
  160.7 3.3 %expand_ffn.1 = (f32[1024,128]{1,0:T(8,128)}, f32[1024,128]{1,0:T(8,128)}, f32[128,1024]{1,0:T(8,128)}, f32[128,2304]{1,0:T(8,128)}, f32[128,2304]{1,0:T(8,128)}, /*index=5*/f32[2304,128]{1,0:T(8,128)}) custom-call(s32[4]{0:T(128)S(1)} %copy-done.22, s32[4]{0:T(128)S(1)} %copy-done.23, bf16[78,16,128]{2,1,0:T(8,128)(2,1)S(1)} %add_convert_fusion.refs_0_, ...), custom_call_target="tpu_custom_call" | custom-call | flops 4600000000 | tf_op jit(solution)/shard_map/expand_ffn/pallas_call | solution.py:155
  164.1 1.9 %collective-permute-done.48.refs_2_ = bf16[28,16,128]{2,1,0:T(8,128)(2,1)S(1)} collective-permute-done((bf16[28,16,128]{2,1,0:T(8,128)(2,1)S(1)}, bf16[28,16,128]{2,1,0:T(8,128)(2,1)S(1)}, u32[]{:S(2)}, u32[]{:S(2)}) %collective-permute-start.48) | collective-permute-done | bytes 114720 | tf_op jit(solution)/shard_map/ppermute | solution.py:785
  167.6 2.5 %expand_qkv.1 = (f32[1024,128]{1,0:T(8,128)}, f32[1024,128]{1,0:T(8,128)}, f32[1024,128]{1,0:T(8,128)}, f32[128,1024]{1,0:T(8,128)}, f32[512,128]{1,0:T(8,128)},...) custom-call(s32[4]{0:T(128)S(1)} %copy-done.22, s32[4]{0:T(128)S(1)} %copy-done.23, ...), custom_call_target="tpu_custom_call" | custom-call | flops 4600000000 | tf_op jit(solution)/shard_map/expand_qkv/pallas_call | solution.py:155
  (181 shorter events, 46.9 us)
Async XLA Ops:
  6.6 10.1 %collective-permute-start.2 = (bf16[256,128]{1,0:T(8,128)(2,1)}, bf16[256,128]{1,0:T(8,128)(2,1)S(1)}, u32[]{:S(2)}, u32[]{:S(2)}) collective-permute-start(bf16[256,128]{1,0:T(8,128)(2,1)} %get-tuple-element.146), channel_id=1, source_target_pairs={{0,24},{2,26},{4,28},{6,30},{8,16},{10,18},{12,20},{14,22},{16,8},... | collective-permute-start | bytes 196616 | tf_op jit(solution)/shard_map/ppermute | solution.py:785
  11.8 7.0 %collective-permute-start.1 = (bf16[256,128]{1,0:T(8,128)(2,1)}, bf16[256,128]{1,0:T(8,128)(2,1)S(1)}, u32[]{:S(2)}, u32[]{:S(2)}) collective-permute-start(bf16[256,128]{1,0:T(8,128)(2,1)} %get-tuple-element.145), channel_id=1, source_target_pairs={{0,16},{2,18},{4,20},{6,22},{8,24},{10,26},{12,28},{14,30},{16,0},... | collective-permute-start | bytes 196616 | tf_op jit(solution)/shard_map/ppermute | solution.py:785
  11.8 7.0 %collective-permute-start = (bf16[256,128]{1,0:T(8,128)(2,1)}, bf16[256,128]{1,0:T(8,128)(2,1)S(1)}, u32[]{:S(2)}, u32[]{:S(2)}) collective-permute-start(bf16[256,128]{1,0:T(8,128)(2,1)} %get-tuple-element.144), channel_id=1, source_target_pairs={{0,8},{2,10},{4,12},{6,14},{8,0},{10,2},{12,4},{14,6},{16,24},{18,... | collective-permute-start | bytes 196616 | tf_op jit(solution)/shard_map/ppermute | solution.py:785
  12.4 10.3 %collective-permute-start.6 = (bf16[256,128]{1,0:T(8,128)(2,1)}, bf16[256,128]{1,0:T(8,128)(2,1)S(1)}, u32[]{:S(2)}, u32[]{:S(2)}) collective-permute-start(bf16[256,128]{1,0:T(8,128)(2,1)} %get-tuple-element.148), channel_id=1, source_target_pairs={{0,8},{2,10},{4,12},{6,14},{8,0},{10,2},{12,4},{14,6},{16,24},{18,... | collective-permute-start | bytes 196616 | tf_op jit(solution)/shard_map/ppermute | solution.py:785
  13.8 12.2 %collective-permute-start.7 = (bf16[256,128]{1,0:T(8,128)(2,1)}, bf16[256,128]{1,0:T(8,128)(2,1)S(1)}, u32[]{:S(2)}, u32[]{:S(2)}) collective-permute-start(bf16[256,128]{1,0:T(8,128)(2,1)} %get-tuple-element.149), channel_id=1, source_target_pairs={{0,16},{2,18},{4,20},{6,22},{8,24},{10,26},{12,28},{14,30},{16,0},... | collective-permute-start | bytes 196616 | tf_op jit(solution)/shard_map/ppermute | solution.py:785
  16.7 9.3 %collective-permute-start.8 = (bf16[256,128]{1,0:T(8,128)(2,1)}, bf16[256,128]{1,0:T(8,128)(2,1)S(1)}, u32[]{:S(2)}, u32[]{:S(2)}) collective-permute-start(bf16[256,128]{1,0:T(8,128)(2,1)} %get-tuple-element.150), channel_id=1, source_target_pairs={{0,24},{2,26},{4,28},{6,30},{8,16},{10,18},{12,20},{14,22},{16,8},... | collective-permute-start | bytes 196616 | tf_op jit(solution)/shard_map/ppermute | solution.py:785
  19.6 9.3 %collective-permute-start.3 = (bf16[4,256,128]{2,1,0:T(8,128)(2,1)S(1)}, bf16[4,256,128]{2,1,0:T(8,128)(2,1)S(1)}, u32[]{:S(2)}, u32[]{:S(2)}) collective-permute-start(bf16[4,256,128]{2,1,0:T(8,128)(2,1)S(1)} %pad_maximum_fusion.1.refs_4_.refs_0_), channel_id=1, source_target_pairs={{0,2},{2,0},{4,6},{6,4},{8,10},{10,8},{12,14},{14,12},{16,18},{18,... | collective-permute-start | bytes 786440 | tf_op jit(solution)/shard_map/ppermute | solution.py:785
  21.2 12.2 %collective-permute-start.4 = (bf16[4,256,128]{2,1,0:T(8,128)(2,1)S(1)}, bf16[4,256,128]{2,1,0:T(8,128)(2,1)S(1)}, u32[]{:S(2)}, u32[]{:S(2)}) collective-permute-start(bf16[4,256,128]{2,1,0:T(8,128)(2,1)S(1)} %pad_maximum_fusion.1.refs_4_.refs_0_), channel_id=1, source_target_pairs={{0,4},{2,6},{4,0},{6,2},{8,12},{10,14},{12,8},{14,10},{16,20},{18,... | collective-permute-start | bytes 786440 | tf_op jit(solution)/shard_map/ppermute | solution.py:785
  22.7 10.7 %collective-permute-start.5 = (bf16[4,256,128]{2,1,0:T(8,128)(2,1)S(1)}, bf16[4,256,128]{2,1,0:T(8,128)(2,1)S(1)}, u32[]{:S(2)}, u32[]{:S(2)}) collective-permute-start(bf16[4,256,128]{2,1,0:T(8,128)(2,1)S(1)} %pad_maximum_fusion.1.refs_4_.refs_0_), channel_id=1, source_target_pairs={{0,6},{2,4},{4,2},{6,0},{8,14},{10,12},{12,10},{14,8},{16,22},{18,... | collective-permute-start | bytes 786440 | tf_op jit(solution)/shard_map/ppermute | solution.py:785
  50.7 15.1 %collective-permute-start.13 = (bf16[4,256,128]{2,1,0:T(8,128)(2,1)S(1)}, bf16[4,256,128]{2,1,0:T(8,128)(2,1)S(1)}, u32[]{:S(2)}, u32[]{:S(2)}) collective-permute-start(bf16[4,256,128]{2,1,0:T(8,128)(2,1)S(1)} %pad_maximum_fusion.2.refs_1_), channel_id=1, source_target_pairs={{0,2},{2,0},{4,6},{6,4},{8,10},{10,8},{12,14},{14,12},{16,18},{18,... | collective-permute-start | bytes 786440 | tf_op jit(solution)/shard_map/ppermute | solution.py:785
  52.0 13.8 %collective-permute-start.14 = (bf16[4,256,128]{2,1,0:T(8,128)(2,1)S(1)}, bf16[4,256,128]{2,1,0:T(8,128)(2,1)S(1)}, u32[]{:S(2)}, u32[]{:S(2)}) collective-permute-start(bf16[4,256,128]{2,1,0:T(8,128)(2,1)S(1)} %pad_maximum_fusion.2.refs_1_), channel_id=1, source_target_pairs={{0,4},{2,6},{4,0},{6,2},{8,12},{10,14},{12,8},{14,10},{16,20},{18,... | collective-permute-start | bytes 786440 | tf_op jit(solution)/shard_map/ppermute | solution.py:785
  52.9 13.2 %collective-permute-start.15 = (bf16[4,256,128]{2,1,0:T(8,128)(2,1)S(1)}, bf16[4,256,128]{2,1,0:T(8,128)(2,1)S(1)}, u32[]{:S(2)}, u32[]{:S(2)}) collective-permute-start(bf16[4,256,128]{2,1,0:T(8,128)(2,1)S(1)} %pad_maximum_fusion.2.refs_1_), channel_id=1, source_target_pairs={{0,6},{2,4},{4,2},{6,0},{8,14},{10,12},{12,10},{14,8},{16,22},{18,... | collective-permute-start | bytes 786440 | tf_op jit(solution)/shard_map/ppermute | solution.py:785
  66.1 17.3 %collective-permute-start.20 = (bf16[78,16,128]{2,1,0:T(8,128)(2,1)S(1)}, bf16[78,16,128]{2,1,0:T(8,128)(2,1)S(1)}, u32[]{:S(2)}, u32[]{:S(2)}) collective-permute-start(bf16[78,16,128]{2,1,0:T(8,128)(2,1)S(1)} %get-tuple-element.178), channel_id=1, source_target_pairs={{0,2},{2,0},{4,6},{6,4},{8,10},{10,8},{12,14},{14,12},{16,18},{18,... | collective-permute-start | bytes 958472 | tf_op jit(solution)/shard_map/ppermute | solution.py:785
  67.2 16.2 %collective-permute-start.21 = (bf16[78,16,128]{2,1,0:T(8,128)(2,1)S(1)}, bf16[78,16,128]{2,1,0:T(8,128)(2,1)S(1)}, u32[]{:S(2)}, u32[]{:S(2)}) collective-permute-start(bf16[78,16,128]{2,1,0:T(8,128)(2,1)S(1)} %get-tuple-element.179), channel_id=1, source_target_pairs={{0,4},{2,6},{4,0},{6,2},{8,12},{10,14},{12,8},{14,10},{16,20},{18,... | collective-permute-start | bytes 958472 | tf_op jit(solution)/shard_map/ppermute | solution.py:785
  68.4 15.3 %collective-permute-start.22 = (bf16[78,16,128]{2,1,0:T(8,128)(2,1)S(1)}, bf16[78,16,128]{2,1,0:T(8,128)(2,1)S(1)}, u32[]{:S(2)}, u32[]{:S(2)}) collective-permute-start(bf16[78,16,128]{2,1,0:T(8,128)(2,1)S(1)} %get-tuple-element.180), channel_id=1, source_target_pairs={{0,6},{2,4},{4,2},{6,0},{8,14},{10,12},{12,10},{14,8},{16,22},{18,... | collective-permute-start | bytes 958472 | tf_op jit(solution)/shard_map/ppermute | solution.py:785
  71.6 7.0 %collective-permute-start.18 = (bf16[256,128]{1,0:T(8,128)(2,1)S(1)}, bf16[256,128]{1,0:T(8,128)(2,1)S(1)}, u32[]{:S(2)}, u32[]{:S(2)}) collective-permute-start(bf16[256,128]{1,0:T(8,128)(2,1)S(1)} %get-tuple-element.173), channel_id=1, source_target_pairs={{0,16},{2,18},{4,20},{6,22},{8,24},{10,26},{12,28},{14,30},{16,0},... | collective-permute-start | bytes 196616 | tf_op jit(solution)/shard_map/ppermute | solution.py:785
  83.7 16.8 %collective-permute-start.28 = (bf16[1056,128]{1,0:T(8,128)(2,1)S(1)}, bf16[1056,128]{1,0:T(8,128)(2,1)S(1)}, u32[]{:S(2)}, u32[]{:S(2)}) collective-permute-start(bf16[1056,128]{1,0:T(8,128)(2,1)S(1)} %scale.1.refs_8_.refs_5_), channel_id=1, source_target_pairs={{0,2},{2,0},{4,6},{6,4},{8,10},{10,8},{12,14},{14,12},{16,18},{18,... | collective-permute-start | bytes 811016 | tf_op jit(solution)/shard_map/ppermute | solution.py:785
  84.6 17.8 %collective-permute-start.29 = (bf16[1056,128]{1,0:T(8,128)(2,1)S(1)}, bf16[1056,128]{1,0:T(8,128)(2,1)S(1)}, u32[]{:S(2)}, u32[]{:S(2)}) collective-permute-start(bf16[1056,128]{1,0:T(8,128)(2,1)S(1)} %scale.1.refs_8_.refs_5_), channel_id=1, source_target_pairs={{0,4},{2,6},{4,0},{6,2},{8,12},{10,14},{12,8},{14,10},{16,20},{18,... | collective-permute-start | bytes 811016 | tf_op jit(solution)/shard_map/ppermute | solution.py:785
  86.0 18.8 %collective-permute-start.30 = (bf16[1056,128]{1,0:T(8,128)(2,1)S(1)}, bf16[1056,128]{1,0:T(8,128)(2,1)S(1)}, u32[]{:S(2)}, u32[]{:S(2)}) collective-permute-start(bf16[1056,128]{1,0:T(8,128)(2,1)S(1)} %scale.1.refs_8_.refs_5_), channel_id=1, source_target_pairs={{0,6},{2,4},{4,2},{6,0},{8,14},{10,12},{12,10},{14,8},{16,22},{18,... | collective-permute-start | bytes 811016 | tf_op jit(solution)/shard_map/ppermute | solution.py:785
  87.3 9.9 %collective-permute-start.23 = (bf16[78,16,128]{2,1,0:T(8,128)(2,1)S(1)}, bf16[78,16,128]{2,1,0:T(8,128)(2,1)S(1)}, u32[]{:S(2)}, u32[]{:S(2)}) collective-permute-start(bf16[78,16,128]{2,1,0:T(8,128)(2,1)S(1)} %add_convert_fusion.2), channel_id=1, source_target_pairs={{0,8},{2,10},{4,12},{6,14},{8,0},{10,2},{12,4},{14,6},{16,24},{18,... | collective-permute-start | bytes 958472 | tf_op jit(solution)/shard_map/ppermute | solution.py:785
  97.4 21.0 %collective-permute-start.24 = (bf16[78,16,128]{2,1,0:T(8,128)(2,1)S(1)}, bf16[78,16,128]{2,1,0:T(8,128)(2,1)S(1)}, u32[]{:S(2)}, u32[]{:S(2)}) collective-permute-start(bf16[78,16,128]{2,1,0:T(8,128)(2,1)S(1)} %add_convert_fusion.1), channel_id=1, source_target_pairs={{0,16},{2,18},{4,20},{6,22},{8,24},{10,26},{12,28},{14,30},{16,0},... | collective-permute-start | bytes 958472 | tf_op jit(solution)/shard_map/ppermute | solution.py:785
  100.4 15.4 %collective-permute-start.25 = (bf16[256,128]{1,0:T(8,128)(2,1)S(1)}, bf16[256,128]{1,0:T(8,128)(2,1)S(1)}, u32[]{:S(2)}, u32[]{:S(2)}) collective-permute-start(bf16[256,128]{1,0:T(8,128)(2,1)S(1)} %get-tuple-element.192), channel_id=1, source_target_pairs={{0,8},{2,10},{4,12},{6,14},{8,0},{10,2},{12,4},{14,6},{16,24},{18,... | collective-permute-start | bytes 196616 | tf_op jit(solution)/shard_map/ppermute | solution.py:785
  100.5 18.0 %collective-permute-start.26 = (bf16[256,128]{1,0:T(8,128)(2,1)S(1)}, bf16[256,128]{1,0:T(8,128)(2,1)S(1)}, u32[]{:S(2)}, u32[]{:S(2)}) collective-permute-start(bf16[256,128]{1,0:T(8,128)(2,1)S(1)} %get-tuple-element.193), channel_id=1, source_target_pairs={{0,16},{2,18},{4,20},{6,22},{8,24},{10,26},{12,28},{14,30},{16,0},... | collective-permute-start | bytes 196616 | tf_op jit(solution)/shard_map/ppermute | solution.py:785
  102.5 16.0 %collective-permute-start.27 = (bf16[256,128]{1,0:T(8,128)(2,1)S(1)}, bf16[256,128]{1,0:T(8,128)(2,1)S(1)}, u32[]{:S(2)}, u32[]{:S(2)}) collective-permute-start(bf16[256,128]{1,0:T(8,128)(2,1)S(1)} %get-tuple-element.194), channel_id=1, source_target_pairs={{0,24},{2,26},{4,28},{6,30},{8,16},{10,18},{12,20},{14,22},{16,8},... | collective-permute-start | bytes 196616 | tf_op jit(solution)/shard_map/ppermute | solution.py:785
  118.6 13.8 %collective-permute-start.40 = (bf16[78,16,128]{2,1,0:T(8,128)(2,1)S(1)}, bf16[78,16,128]{2,1,0:T(8,128)(2,1)S(1)}, u32[]{:S(2)}, u32[]{:S(2)}) collective-permute-start(bf16[78,16,128]{2,1,0:T(8,128)(2,1)S(1)} %add_convert_fusion.refs_0_), channel_id=1, source_target_pairs={{0,2},{2,0},{4,6},{6,4},{8,10},{10,8},{12,14},{14,12},{16,18},{18,... | collective-permute-start | bytes 958472 | tf_op jit(solution)/shard_map/ppermute | solution.py:785
  119.6 12.7 %collective-permute-start.41 = (bf16[78,16,128]{2,1,0:T(8,128)(2,1)S(1)}, bf16[78,16,128]{2,1,0:T(8,128)(2,1)S(1)}, u32[]{:S(2)}, u32[]{:S(2)}) collective-permute-start(bf16[78,16,128]{2,1,0:T(8,128)(2,1)S(1)} %add_convert_fusion.refs_0_), channel_id=1, source_target_pairs={{0,4},{2,6},{4,0},{6,2},{8,12},{10,14},{12,8},{14,10},{16,20},{18,... | collective-permute-start | bytes 958472 | tf_op jit(solution)/shard_map/ppermute | solution.py:785
  120.4 8.6 %collective-permute-start.32 = (bf16[256,128]{1,0:T(8,128)(2,1)S(1)}, bf16[256,128]{1,0:T(8,128)(2,1)S(1)}, u32[]{:S(2)}, u32[]{:S(2)}) collective-permute-start(bf16[256,128]{1,0:T(8,128)(2,1)S(1)} %get-tuple-element.205), channel_id=1, source_target_pairs={{0,8},{2,10},{4,12},{6,14},{8,0},{10,2},{12,4},{14,6},{16,24},{18,... | collective-permute-start | bytes 196616 | tf_op jit(solution)/shard_map/ppermute | solution.py:785
  121.6 8.1 %collective-permute-start.33 = (bf16[256,128]{1,0:T(8,128)(2,1)S(1)}, bf16[256,128]{1,0:T(8,128)(2,1)S(1)}, u32[]{:S(2)}, u32[]{:S(2)}) collective-permute-start(bf16[256,128]{1,0:T(8,128)(2,1)S(1)} %get-tuple-element.206), channel_id=1, source_target_pairs={{0,16},{2,18},{4,20},{6,22},{8,24},{10,26},{12,28},{14,30},{16,0},... | collective-permute-start | bytes 196616 | tf_op jit(solution)/shard_map/ppermute | solution.py:785
  132.3 11.6 %collective-permute-start.42 = (bf16[256,1024]{1,0:T(8,128)(2,1)S(1)}, bf16[256,1024]{1,0:T(8,128)(2,1)S(1)}, u32[]{:S(2)}, u32[]{:S(2)}) collective-permute-start(bf16[256,1024]{1,0:T(8,128)(2,1)S(1)} %get-tuple-element.237.refs_3_), channel_id=1, source_target_pairs={{0,1},{1,0},{2,3},{3,2},{4,5},{5,4},{6,7},{7,6},{8,9},{9,8},{10,11... | collective-permute-start | bytes 1572872 | tf_op jit(solution)/shard_map/ppermute | solution.py:781
  145.3 11.6 %collective-permute-start.45 = (bf16[78,16,128]{2,1,0:T(8,128)(2,1)S(1)}, bf16[78,16,128]{2,1,0:T(8,128)(2,1)S(1)}, u32[]{:S(2)}, u32[]{:S(2)}) collective-permute-start(bf16[78,16,128]{2,1,0:T(8,128)(2,1)S(1)} %add_convert_fusion.refs_0_), channel_id=1, source_target_pairs={{0,6},{2,4},{4,2},{6,0},{8,14},{10,12},{12,10},{14,8},{16,22},{18,... | collective-permute-start | bytes 958472 | tf_op jit(solution)/shard_map/ppermute | solution.py:785
  149.1 7.8 %collective-permute-start.44 = (bf16[28,16,128]{2,1,0:T(8,128)(2,1)S(1)}, bf16[28,16,128]{2,1,0:T(8,128)(2,1)S(1)}, u32[]{:S(2)}, u32[]{:S(2)}) collective-permute-start(bf16[28,16,128]{2,1,0:T(8,128)(2,1)S(1)} %add_convert_fusion.4), channel_id=1, source_target_pairs={{0,16},{2,18},{4,20},{6,22},{8,24},{10,26},{12,28},{14,30},{16,0},... | collective-permute-start | bytes 344072 | tf_op jit(solution)/shard_map/ppermute | solution.py:785
  158.2 7.7 %collective-permute-start.48 = (bf16[28,16,128]{2,1,0:T(8,128)(2,1)S(1)}, bf16[28,16,128]{2,1,0:T(8,128)(2,1)S(1)}, u32[]{:S(2)}, u32[]{:S(2)}) collective-permute-start(bf16[28,16,128]{2,1,0:T(8,128)(2,1)S(1)} %add_convert_fusion.3.refs_0_), channel_id=1, source_target_pairs={{0,4},{2,6},{4,0},{6,2},{8,12},{10,14},{12,8},{14,10},{16,20},{18,... | collective-permute-start | bytes 344072 | tf_op jit(solution)/shard_map/ppermute | solution.py:785
  (57 other events, 711.1 us)
